TPU v7x, 32 devices: a whole 2x2x4 slice. The times are simulated.
32 devices in a mesh: groups: 2 (over y), blk: 4 (over z), side: 2 (over x), tp: 2 (over core).
Axes of the slice: x: 2, y: 2, z: 4, core: 2. Of those that a mesh axis runs over, the one named last changes fastest.
Arguments:
- queries: bfloat16 [4, 512, 4096], P(('groups', 'side'), 'blk', 'tp'), parts along dimension 0, may hold values from -8 to 8
- key_rows: bfloat16 [4, 512, 256], P(('groups', 'side'), 'blk', 'tp'), parts along dimension 0, may hold values from -8 to 8
- value_rows: bfloat16 [4, 512, 256], P(('groups', 'side'), 'blk', 'tp'), parts along dimension 0, may hold values from -6 to 6
- segments: int32 [4, 512], P(('groups', 'side'), 'blk'), parts along dimension 0, may hold values from 0 to 1, never falling along the last dimension, each value on 1 to 384 neighbouring positions
- hidden_entry_rows: bfloat16 [4, 512, 4096], P(('groups', 'side'), 'blk', 'tp'), parts along dimension 0, may hold values from -6 to 6
- expert_ids: int32 [4, 512, 8], P(('groups', 'side'), 'blk'), parts along dimension 0, may hold values from 0 to 127, all different within a row; in each aligned block of 128 rows (0 to 127, 128 to 255, ..., all dimensions but the last counted through in order) at most 10 rows name the same one
- route_weight: float32 [4, 512, 8], P(('groups', 'side'), 'blk'), parts along dimension 0, may hold values from 0.2 to 1
- w_gate: bfloat16 [4, 2048, 1536], P('blk', 'tp', 'side'), may hold values from -0.09375 to 0.09375
- w_up: bfloat16 [4, 2048, 1536], P('blk', 'tp', 'side'), may hold values from -0.09375 to 0.09375
- w_down: bfloat16 [4, 1536, 2048], P('blk', 'side', 'tp'), may hold values from -0.15625 to 0.15625
Outputs:
- attended: bfloat16 [4, 512, 4096], P(('groups', 'side'), 'blk', 'tp'), parts along dimension 0
- moe_out: bfloat16 [4, 512, 4096], P(('groups', 'side'), 'blk', 'tp'), parts along dimension 0
There are 2 independent parts, one for each index of `groups`. A program takes and returns all parts, laid end to end along the dimension named above; an argument that names none is the same for every part. Nothing has to cross between parts.
Inputs may be any that keep to these rules, and one draw needn't show every extreme that they name: `expert_ids`: in the 128 rows of one device (aligned blocks of rows of a sequence) no expert is named by more than 10 rows, and in some such block one is named by exactly 10; a row names 8 different experts. `segments`: document numbers never fall along a sequence; a document spans at most 384 positions, and one spans exactly that many.
All inputs are finite; a program needn't handle non-finite values.
Results may differ from a plain program's by a relative error of at most 0.02.
Values may be sent and summed in bfloat16 or wider, within the bound.
No kernel may reach another device: no remote copies, remote signals or barrier semaphores. Data moves between devices by JAX's collectives and lax.ppermute only.
A program may use at most 64 MiB of HBM per device.

v0:
```python
import math

import jax
import jax.numpy as jnp
from jax import lax
from jax.sharding import PartitionSpec as P

HEAD_DIM = 128
CAP = 10


def passed_along(value, axis, steps):
    count = lax.axis_size(axis)
    pairs = [(source, (source + steps) % count) for source in range(count)]
    return lax.ppermute(value, axis, pairs)


def slot_choice(id_rows, experts, capacity):
    named = id_rows[:, :, None] == jnp.arange(experts, dtype=jnp.int32)[None, None, :]
    hits = jnp.sum(named.astype(jnp.int32), axis=1)
    ranks = jnp.cumsum(hits, axis=0) - hits
    levels = jnp.arange(capacity, dtype=jnp.int32)[None, :, None]
    return (hits.T[:, None, :] > 0) & (ranks.T[:, None, :] == levels)


def routing_slot_index(id_rows, experts, capacity):
    chosen = slot_choice(id_rows, experts, capacity)
    row_iota = jnp.arange(id_rows.shape[0], dtype=jnp.int32)
    index = jnp.sum(jnp.where(chosen, row_iota[None, None, :], 0), axis=2)
    valid = jnp.any(chosen, axis=2)
    return (index, valid)


def pick_rows(rows, index, valid):
    taken = jnp.take(rows, index, axis=0)
    return jnp.where(valid[..., None], taken, jnp.zeros((), rows.dtype))


def slot_weights(id_rows, weight_rows, experts, capacity):
    named = id_rows[:, :, None] == jnp.arange(experts, dtype=jnp.int32)[None, None, :]
    shares = jnp.sum(jnp.where(named, weight_rows[:, :, None], 0.0), axis=1)
    chosen = slot_choice(id_rows, experts, capacity)
    return chosen.astype(jnp.float32) * shares.T[:, None, :]


def body(
    queries,
    key_rows,
    value_rows,
    segments,
    hidden_entry_rows,
    expert_ids,
    route_weight,
    w_gate,
    w_up,
    w_down,
):
    length = queries.shape[1]
    head_size = HEAD_DIM
    kv_here = key_rows.shape[2] // head_size
    group = queries.shape[2] // (head_size * kv_here)
    query_portion = queries[0].reshape(length, kv_here, group, head_size)
    local_segment_labels = segments[0]
    query_pos = lax.axis_index("blk") * length + jnp.arange(length, dtype=jnp.int32)
    factor = 1.0 / math.sqrt(head_size)
    start_state = (
        jnp.full((length, kv_here, group), -1e30, jnp.float32),
        jnp.zeros((length, kv_here, group), jnp.float32),
        jnp.zeros((length, kv_here, group, head_size), jnp.float32),
    )
    key_piece = lax.all_gather(key_rows[0], "blk", axis=0, tiled=True)
    value_fragment = lax.all_gather(value_rows[0], "blk", axis=0, tiled=True)
    segment_piece = lax.all_gather(local_segment_labels, "blk", axis=0, tiled=True)
    rows_in = key_piece.shape[0]
    width = math.gcd(rows_in, 512)

    def one_block(block_index, state):
        row_max, totals, accumulated = state
        begin = block_index * width
        key_tile_block = lax.dynamic_slice_in_dim(key_piece, begin, width, 0).reshape(
            width, kv_here, head_size
        )
        value_block = lax.dynamic_slice_in_dim(value_fragment, begin, width, 0).reshape(
            width, kv_here, head_size
        )
        segment_block = lax.dynamic_slice_in_dim(segment_piece, begin, width, 0)
        key_pos = begin + jnp.arange(width, dtype=jnp.int32)
        allowed = (key_pos[None, :] <= query_pos[:, None]) & (
            segment_block[None, :] == local_segment_labels[:, None]
        )
        masking = allowed[:, None, None, :]
        scores = (
            jnp.einsum(
                "wsmz,usz->wsmu", query_portion, key_tile_block, preferred_element_type=jnp.float32
            )
            * factor
        )
        scores = jnp.where(masking, scores, -1e30)
        new_max = jnp.maximum(row_max, jnp.max(scores, axis=3))
        rescale = jnp.exp(row_max - new_max)
        weights = jnp.where(masking, jnp.exp(scores - new_max[..., None]), 0.0)
        totals = totals * rescale + jnp.sum(weights, axis=3)
        update = jnp.einsum(
            "jzre,ezm->jzrm",
            weights.astype(jnp.bfloat16),
            value_block,
            preferred_element_type=jnp.float32,
        )
        accumulated = accumulated * rescale[..., None] + update
        return (new_max, totals, accumulated)

    row_max, totals, accumulated = lax.fori_loop(0, rows_in // width, one_block, start_state)
    attended = (
        (accumulated / totals[..., None])
        .astype(jnp.bfloat16)
        .reshape(1, length, group * kv_here * head_size)
    )
    experts = lax.axis_size("blk") // 2
    capacity = CAP
    ff_here = w_gate.shape[2]
    quarter = hidden_entry_rows.shape[2] // 2
    index, valid = routing_slot_index(expert_ids[0], experts, capacity)
    taken = pick_rows(hidden_entry_rows[0], index, valid)
    outgoing = (
        taken.reshape(experts, capacity, 2, quarter)
        .transpose(2, 0, 1, 3)
        .reshape(2 * experts, capacity, quarter)[:, None]
    )
    arrived = lax.all_to_all(outgoing, "blk", split_axis=0, concat_axis=0, tiled=True)
    shards = lax.all_gather(arrived, "side", axis=1, tiled=True)
    gate_piece = jnp.einsum("bscd,df->bscf", shards, w_gate[0], preferred_element_type=jnp.float32)
    up_piece = jnp.einsum("bscd,df->bscf", shards, w_up[0], preferred_element_type=jnp.float32)
    projected = jnp.concatenate([gate_piece, up_piece], axis=3)
    gate_part = projected[..., :ff_here]
    up_part = projected[..., ff_here:]
    gate_sum, up_sum = (
        lax.psum(gate_part.astype(jnp.bfloat16), "tp").astype(jnp.float32),
        lax.psum(up_part.astype(jnp.bfloat16), "tp").astype(jnp.float32),
    )
    both_sums = jnp.stack([gate_sum, up_sum])
    partner_sums = passed_along(
        both_sums.astype(jnp.bfloat16), "blk", lax.axis_size("blk") // 2
    ).astype(both_sums.dtype)
    full_sums = both_sums + partner_sums
    hidden = (jax.nn.silu(full_sums[0]) * full_sums[1]).astype(jnp.bfloat16)
    part_out = jnp.einsum(
        "bscf,fd->bscd", hidden, w_down[0], preferred_element_type=jnp.float32
    ).astype(jnp.bfloat16)
    parts = lax.all_to_all(part_out, "side", split_axis=1, concat_axis=1, tiled=True)
    slot_out = jnp.sum(parts, axis=1, dtype=jnp.float32).astype(jnp.bfloat16)
    returned = lax.all_to_all(slot_out, "blk", split_axis=0, concat_axis=0, tiled=True)
    returned_split = returned.astype(jnp.float32).reshape(2, experts, capacity, quarter)
    own_weighted = slot_weights(expert_ids[0], route_weight[0], experts, capacity)
    mixed = jnp.einsum(
        "ecr,kecq->rkq", own_weighted, returned_split, precision=lax.Precision.HIGHEST
    )
    moe_out = mixed.reshape(mixed.shape[0], 2 * quarter).astype(jnp.bfloat16)[None]
    return (attended, moe_out)


def solution(mesh):
    placed = (
        P(("groups", "side"), "blk", "tp"),
        P(("groups", "side"), "blk", "tp"),
        P(("groups", "side"), "blk", "tp"),
        P(("groups", "side"), "blk"),
        P(("groups", "side"), "blk", "tp"),
        P(("groups", "side"), "blk", None),
        P(("groups", "side"), "blk", None),
        P("blk", "tp", "side"),
        P("blk", "tp", "side"),
        P("blk", "side", "tp"),
    )
    return jax.shard_map(
        body,
        mesh=mesh,
        in_specs=placed,
        out_specs=(P(("groups", "side"), "blk", "tp"), P(("groups", "side"), "blk", "tp")),
        check_vma=False,
    )
```

profile of v0, /device:TPU:0, one launch (start us, length us, event | category | flops | bytes accessed | tf_op | source)
XLA Modules:
  0.0 130.9 jit_solution(2119913399250369770)
XLA Ops:
  7.2 0.8 convert_reduce_fusion
  8.0 0.1 copy.47
  8.1 0.2 reduce_window_sum.12
  8.4 0.1 select_reduce_fusion
  8.5 0.1 fusion.50
  8.7 1.8 %gather_fusion = bf16[20,2048]{1,0:T(8,128)(2,1)S(1)} fusion(bf16[128,2048]{1,0:T(8,128)(2,1)} %bitcast.124, s32[1024]{0:T(1024)S(1)} %pad_clamp_fusion), kind=kCustom, calls=%fused_computation | custom fusion | bytes 163920 | tf_op jit(solution)/shard_map/jit(_take)/gather | solution.py:35
  10.6 0.7 fusion.47
  11.3 6.3 %all-to-all-start = ((bf16[4,1,10,1024]{3,2,1,0:T(8,128)(2,1)}), bf16[4,1,10,1024]{3,2,1,0:T(8,128)(2,1)S(1)}, u32[]{:S(2)}, u32[]{:S(2)}) async-start(bf16[4,1,10,1024]{3,2,1,0:T(8,128)(2,1)} %bitcast.21), calls=%async_computation | async-start | bytes 262144 | tf_op jit(solution)/shard_map/all_to_all | solution.py:129
  17.7 11.5 %all-gather = s32[1,512]{1,0:T(1,128)S(1)} all-gather(s32[1,128]{1,0:T(1,128)} %param.13), channel_id=2, replica_groups=mesh['groups'=2,'blk'=4,'side'=2,'tp'=2] {'blk'}, dimensions={1}, use_global_device_ids=true | all-gather | bytes 2560 | tf_op jit(solution)/shard_map/all_gather | solution.py:73
  29.1 0.8 fusion.41
  29.9 1.1 copy.62
  31.1 13.6 %all-gather.1 = bf16[1,512,128]{2,1,0:T(8,128)(2,1)S(1)} all-gather(bf16[1,128,128]{2,1,0:T(8,128)(2,1)} %param.11), channel_id=3, replica_groups=mesh['groups'=2,'blk'=4,'side'=2,'tp'=2] {'blk'}, dimensions={1}, use_global_device_ids=true | all-gather | bytes 163840 | tf_op jit(solution)/shard_map/all_gather | solution.py:71
  44.7 5.6 %all_gather.15 = bf16[4,2,10,1024]{3,2,1,0:T(8,128)(2,1)S(1)} all-gather(bf16[4,1,10,1024]{3,2,1,0:T(8,128)(2,1)S(1)} %all-to-all-done), channel_id=1, replica_groups=mesh['groups'=2,'blk'=4,'side'=2,'tp'=2] {'side'}, dimensions={1}, use_global_device_ids=true | all-gather | bytes 245760 | tf_op jit(solution)/shard_map/all_gather | solution.py:130
  50.3 2.5 %fusion.33 = bf16[1,4,2,10,768]{4,3,2,1,0:T(8,128)(2,1)} fusion(bf16[4,2,10,1024]{3,2,1,0:T(8,128)(2,1)S(1)} %all_gather.15, bf16[1,1024,768]{2,1,0:T(8,128)(2,1)} %param.17), kind=kOutput, calls=%fused_computation.24 | convolution fusion | flops 125890560 | bytes 1859584 | tf_op jit(solution)/shard_map/bscd,df->bscf/dot_general | solution.py:131
  52.8 2.5 %fusion.30 = bf16[1,4,2,10,768]{4,3,2,1,0:T(8,128)(2,1)} fusion(bf16[4,2,10,1024]{3,2,1,0:T(8,128)(2,1)S(1)} %all_gather.15, bf16[1,1024,768]{2,1,0:T(8,128)(2,1)} %param.18), kind=kOutput, calls=%fused_computation.23 | convolution fusion | flops 125890560 | bytes 1859584 | tf_op jit(solution)/shard_map/bscd,df->bscf/dot_general | solution.py:132
  55.3 2.7 %fusion = (f32[128,16]{0,1:T(8,128)S(1)}, f32[512,128,16]{1,0,2:T(8,128)}) fusion(pred[128,512]{0,1:T(8,128)(4,1)S(1)} %fusion.41, bf16[128,16,128]{2,1,0:T(8,128)(2,1)S(1)} %bitcast.123, bf16[1,512,128]{2,1,0:T(8,128)(2,1)S(1)} %all-gather.1), kind=kOutput, calls=%fused_computation.3 | convolution fusion | flops 271579136 | bytes 4923392 | tf_op jit(solution)/shard_map/while/body/eval_jaxpr/wsmz,usz->wsmu/dot_general | solution.py:93
  57.9 14.3 %all-reduce.3.cloned.1.call-done = (bf16[1,4,2,10,768]{4,3,2,1,0:T(8,128)(2,1)}, bf16[1,4,2,10,768]{4,3,2,1,0:T(8,128)(2,1)}) async-done(((bf16[1,4,2,10,768]{4,3,2,1,0:T(8,128)(2,1)}, bf16[1,4,2,10,768]{4,3,2,1,0:T(8,128)(2,1)}), (bf16[1,4,2,10,768]{4,3,2,1,0:T(8,128)(2,1)}, bf16[1,4,2,10,768]{4,3,2,1,0:T(8,128)(2,1)})) %all-reduce.3.cloned.1.call-update) | async-done | bytes 245776 | tf_op jit(solution)/shard_map/psum | solution.py:137
  72.2 0.9 constant_dynamic-update-slice_fusion.1
  73.1 0.9 constant_dynamic-update-slice_fusion
  74.1 2.7 %collective-permute-start = (bf16[2,4,2,10,768]{4,3,2,1,0:T(8,128)(2,1)S(1)}, bf16[2,4,2,10,768]{4,3,2,1,0:T(8,128)(2,1)S(1)}, u32[]{:S(2)}, u32[]{:S(2)}) collective-permute-start(bf16[2,4,2,10,768]{4,3,2,1,0:T(8,128)(2,1)S(1)} %constant_dynamic-update-slice_fusion), channel_id=1, source_target_pairs={{0,8},{4,12},{8,0},{12,4},{1,9},{5,13},{9,1},{13,5},{2,10},{6,14},... | collective-permute-start | bytes 737288 | tf_op jit(solution)/shard_map/ppermute | solution.py:15
  76.8 3.2 %fusion.1 = f32[128,16]{0,1:T(8,128)S(1)} fusion(f32[512,128,16]{1,0,2:T(8,128)} %get-tuple-element.48, f32[128,16]{0,1:T(8,128)S(1)} %broadcast_maximum_fusion, pred[128,512]{0,1:T(8,128)(4,1)S(1)} %fusion.41), kind=kLoop, calls=%fused_computation.4 | loop fusion | flops 5240832 | bytes 4276224 | tf_op jit(solution)/shard_map/while/body/eval_jaxpr/reduce_sum | solution.py:102
  80.1 14.8 %collective-permute-done = bf16[2,4,2,10,768]{4,3,2,1,0:T(8,128)(2,1)S(1)} collective-permute-done((bf16[2,4,2,10,768]{4,3,2,1,0:T(8,128)(2,1)S(1)}, bf16[2,4,2,10,768]{4,3,2,1,0:T(8,128)(2,1)S(1)}, u32[]{:S(2)}, u32[]{:S(2)}) %collective-permute-start) | collective-permute-done | bytes 245792 | tf_op jit(solution)/shard_map/ppermute | solution.py:15
  94.9 0.4 fusion.21
  95.4 0.8 copy.51
  96.2 3.4 %all-to-all-start.1 = ((bf16[4,2,10,1024]{3,0,2,1:T(4,128)(2,1)}), bf16[4,2,10,1024]{3,0,2,1:T(4,128)(2,1)S(1)}, u32[]{:S(2)}, u32[]{:S(2)}) async-start(bf16[4,2,10,1024]{3,0,2,1:T(4,128)(2,1)} %copy.51), calls=%async_computation.1 | async-start | bytes 327680 | tf_op jit(solution)/shard_map/all_to_all | solution.py:149
  99.7 12.3 %all-gather.2 = bf16[1,512,128]{1,2,0:T(8,128)(2,1)S(1)} all-gather(bf16[1,128,128]{1,2,0:T(8,128)(2,1)S(1)} %copy.45), channel_id=4, replica_groups=mesh['groups'=2,'blk'=4,'side'=2,'tp'=2] {'blk'}, dimensions={1}, use_global_device_ids=true | all-gather | bytes 163840 | tf_op jit(solution)/shard_map/all_gather | solution.py:72
  112.1 0.7 copy.61
  112.8 3.9 %all-to-all-start.2 = ((bf16[4,10,1024]{2,1,0:T(8,128)(2,1)}), bf16[4,10,1024]{2,1,0:T(8,128)(2,1)S(1)}, u32[]{:S(2)}, u32[]{:S(2)}) async-start(bf16[4,10,1024]{2,1,0:T(8,128)(2,1)} %copy.61), calls=%async_computation.2 | async-start | bytes 262144 | tf_op jit(solution)/shard_map/all_to_all | solution.py:151
  116.7 3.4 %divide_convert_fusion = bf16[1,128,128,16]{2,1,3,0:T(8,128)(2,1)S(1)} fusion(f32[512,128,16]{1,0,2:T(8,128)} %get-tuple-element.48, f32[128,16]{0,1:T(8,128)S(1)} %broadcast_maximum_fusion, pred[128,512]{0,1:T(8,128)(4,1)S(1)} %fusion.41, f32[128,16]{0,1:T(8,128)S(1)} %get-tuple-element.46, f32[128,16]{0,1:T(8,128)S(1)} %get-tuple-element.45, ...), kind=kOutput, calls=%fused_computation.25 | convolution fusion | flops 274464768 | bytes 4939776 | tf_op jit(solution)/shard_map/while/body/eval_jaxpr/jzre,ezm->jzrm/dot_general | solution.py:103
  120.1 1.0 copy.55
  121.1 1.4 %all-to-all-done.2 = bf16[4,10,1024]{2,1,0:T(8,128)(2,1)S(1)} async-done(((bf16[4,10,1024]{2,1,0:T(8,128)(2,1)}), bf16[4,10,1024]{2,1,0:T(8,128)(2,1)S(1)}, u32[]{:S(2)}, u32[]{:S(2)}) %all-to-all-start.2) | async-done | bytes 81952 | tf_op jit(solution)/shard_map/all_to_all | solution.py:151
  122.7 1.4 %fusion.4 = bf16[1,128,2048]{2,1,0:T(8,128)(2,1)} fusion(bf16[2048,10,2]{0,2,1:T(2,128)(2,1)S(1)} %bitcast.125, f32[2,128]{1,0:T(2,128)S(1)} %bitcast.132, s32[2,128]{1,0:T(2,128)S(1)} %copy.49, pred[2,128]{1,0:T(4,128)(4,1)S(1)} %compare_bitcast_fusion), kind=kOutput, calls=%fused_computation.8 | convolution fusion | flops 63184384 | bytes 608512 | tf_op jit(solution)/shard_map/ecr,kecq->rkq/dot_general | solution.py:154
  (28 shorter events, 0.7 us)
Async XLA Ops:
  7.2 87.8 %copy-start = (bf16[1,768,1024]{2,1,0:T(8,128)(2,1)S(1)}, bf16[1,768,1024]{2,1,0:T(8,128)(2,1)}, u32[]{:S(2)}) copy-start(bf16[1,768,1024]{2,1,0:T(8,128)(2,1)} %param.19) | copy-start | bytes 4718596
  11.3 33.3 %all-to-all-start = ((bf16[4,1,10,1024]{3,2,1,0:T(8,128)(2,1)}), bf16[4,1,10,1024]{3,2,1,0:T(8,128)(2,1)S(1)}, u32[]{:S(2)}, u32[]{:S(2)}) async-start(bf16[4,1,10,1024]{3,2,1,0:T(8,128)(2,1)} %bitcast.21), calls=%async_computation | async-start | bytes 262144 | tf_op jit(solution)/shard_map/all_to_all | solution.py:129
  17.6 54.6 %all-reduce.3.cloned.1.call-start = ((), (), s32[]{:S(2)}) async-start(), calls=%async_computation.3 | async-start | bytes 786432 | tf_op jit(solution)/shard_map/psum | solution.py:137
  74.1 20.7 %collective-permute-start = (bf16[2,4,2,10,768]{4,3,2,1,0:T(8,128)(2,1)S(1)}, bf16[2,4,2,10,768]{4,3,2,1,0:T(8,128)(2,1)S(1)}, u32[]{:S(2)}, u32[]{:S(2)}) collective-permute-start(bf16[2,4,2,10,768]{4,3,2,1,0:T(8,128)(2,1)S(1)} %constant_dynamic-update-slice_fusion), channel_id=1, source_target_pairs={{0,8},{4,12},{8,0},{12,4},{1,9},{5,13},{9,1},{13,5},{2,10},{6,14},... | collective-permute-start | bytes 737288 | tf_op jit(solution)/shard_map/ppermute | solution.py:15
  76.8 22.8 %copy-start.1 = (bf16[1,128,128]{2,1,0:T(8,128)(2,1)S(1)}, bf16[1,128,128]{2,1,0:T(8,128)(2,1)}, u32[]{:S(2)}) copy-start(bf16[1,128,128]{2,1,0:T(8,128)(2,1)} %param.12) | copy-start | bytes 98308
  96.2 15.8 %all-to-all-start.1 = ((bf16[4,2,10,1024]{3,0,2,1:T(4,128)(2,1)}), bf16[4,2,10,1024]{3,0,2,1:T(4,128)(2,1)S(1)}, u32[]{:S(2)}, u32[]{:S(2)}) async-start(bf16[4,2,10,1024]{3,0,2,1:T(4,128)(2,1)} %copy.51), calls=%async_computation.1 | async-start | bytes 327680 | tf_op jit(solution)/shard_map/all_to_all | solution.py:149
  112.8 9.8 %all-to-all-start.2 = ((bf16[4,10,1024]{2,1,0:T(8,128)(2,1)}), bf16[4,10,1024]{2,1,0:T(8,128)(2,1)S(1)}, u32[]{:S(2)}, u32[]{:S(2)}) async-start(bf16[4,10,1024]{2,1,0:T(8,128)(2,1)} %copy.61), calls=%async_computation.2 | async-start | bytes 262144 | tf_op jit(solution)/shard_map/all_to_all | solution.py:151
  116.7 4.5 %copy-start.2 = (s32[1,128,8]{1,2,0:T(8,128)S(1)}, s32[1,128,8]{1,2,0:T(8,128)}, u32[]{:S(2)}) copy-start(s32[1,128,8]{1,2,0:T(8,128)} %param.15) | copy-start | bytes 12292
  116.7 4.5 %copy-start.3 = (f32[1,128,8]{1,2,0:T(8,128)S(1)}, f32[1,128,8]{1,2,0:T(8,128)}, u32[]{:S(2)}) copy-start(f32[1,128,8]{1,2,0:T(8,128)} %param.16) | copy-start | bytes 12292
Sparse Core Ops, SparseCore 0:
  55.4 16.7 all-reduce.2
where the time goes:
time: 132 us; the launch traced here: 131 us
  blocking collectives  43 us (33%)
  waiting for transfers between devices  30.5 us (23%)
  starting transfers between devices  16.3 us (12%)
  between operations  14.2 us (11%)
  matrix products  12.9 us (10%)
  local copies, waits for them, and re-layouts  7.85 us (6%)
  other arithmetic  6.27 us (5%)
    ppermute x1, waiting for transfers between devices, passed_along(): return lax.ppermute(value, axis, pairs)  14.8 us
    psum x1, waiting for transfers between devices, body(): lax.psum(gate_part.astype(jnp.bfloat16), 'tp').astype(jnp.float32)  14.3 us
    all_gather x1, blocking collectives, body(): key_piece = lax.all_gather(key_rows[0], 'blk', axis=0, tiled=True)  13.6 us
    all_gather x1, blocking collectives, body(): value_fragment = lax.all_gather(value_rows[0], 'blk', axis=0, tiled=True)  12.3 us
    all_gather x1, blocking collectives, body(): lax.all_gather(local_segment_labels, 'blk', axis=0, tiled=True)  11.5 us
    all_to_all x1, starting transfers between devices, body(): lax.all_to_all(outgoing, 'blk', split_axis=0, concat_axis=0, tiled=True)  6.32 us
    all_gather x1, blocking collectives, body(): shards = lax.all_gather(arrived, 'side', axis=1, tiled=True)  5.63 us
    unnamed x13, local copies, waits for them, and re-layouts  3.93 us
  transfers between devices with their start and end apart: 5, of which 3 were waited for; matrix products, arithmetic and copies ran while one was open for 10% of the time, Pallas kernels for 0%

commit v1 on v0

v1 whole, which is shorter than its diff:
```python
import math

import jax
import jax.numpy as jnp
from jax import lax
from jax.experimental import pallas as pl
from jax.experimental.pallas import tpu as pltpu
from jax.sharding import PartitionSpec as P

HEAD_DIM = 128
CAP = 10
BF = jnp.bfloat16
F32 = jnp.float32
VMEM = pl.BlockSpec(memory_space=pltpu.VMEM)


def swapped(value, axis, bit):
    count = lax.axis_size(axis)
    return lax.ppermute(value, axis, [(i, i ^ bit) for i in range(count)])


def up_to(value, step):
    return -(-value // step) * step


def call(kernel, outs, *ins, scratch=(), flops=0, exps=0):
    moved = sum(math.prod(a.shape) * a.dtype.itemsize for a in (*ins, *outs))
    held = sum(math.prod(s.shape) * s.dtype.itemsize for s in scratch)
    return pl.pallas_call(
        kernel,
        out_shape=list(outs),
        in_specs=[VMEM] * len(ins),
        out_specs=[VMEM] * len(outs),
        scratch_shapes=list(scratch),
        compiler_params=pltpu.CompilerParams(vmem_limit_bytes=2 * moved + held + (2 << 20)),
        cost_estimate=pl.CostEstimate(flops=flops, bytes_accessed=moved, transcendentals=exps),
    )(*ins)


def shaped(rows, columns, dtype=BF):
    return jax.ShapeDtypeStruct((rows, columns), dtype)


def dot(a, b):
    return jnp.dot(a, b, preferred_element_type=F32)


def dot_rows(a, b):
    return lax.dot_general(a, b, (((0,), (0,)), ((), ())), preferred_element_type=F32)


def mover(rows_out, rows_in, pieces):
    i = lax.broadcasted_iota(jnp.int32, (rows_out, rows_in), 0)
    j = lax.broadcasted_iota(jnp.int32, (rows_out, rows_in), 1)
    hit = jnp.zeros((rows_out, rows_in), jnp.bool_)
    for to, start in pieces:
        hit = hit | ((j - i == start - to) & (i >= to) & (i < to + CAP))
    return jnp.where(hit, 1.0, 0.0).astype(BF)


class Plan:
    def __init__(self, count):
        self.count, self.experts = count, count // 2
        self.bits = [1 << i for i in range(count.bit_length() - 1)]
        keep = [(0, d) for d in range(count) if not d & self.bits[0]]
        send = [(0, d) for d in range(count) if d & self.bits[0]]
        self.first_keep, self.first_send = keep, send
        self.there = []
        for bit, later in zip(self.bits, self.bits[1:] + [None]):
            received = [(s ^ bit, d ^ bit) for s, d in send]
            pool = [(0, i, g) for i, g in enumerate(keep)] + [(1, i, g) for i, g in enumerate(received)]
            keep, send = [], []
            stage = ([], [])
            for which, place, group in pool:
                goes = later is not None and bool(group[1] & later)
                target = send if goes else keep
                stage[goes].append((which, len(target) * CAP, place * CAP))
                target.append(group)
            self.there.append(stage)
        self.sources = [s for s, _ in keep]
        self.back = []
        groups = [(s, 0) for s in self.sources]
        pool = [(0, i, g) for i, g in enumerate(groups)]
        for bit in reversed(self.bits):
            keep, send = [], []
            stage = ([], [])
            for which, place, group in pool:
                goes = bool(group[0] & bit)
                target = send if goes else keep
                stage[goes].append((which, len(target) * CAP, place * CAP))
                target.append(group)
            self.back.append(stage)
            received = [(s ^ bit, d ^ bit) for s, d in send]
            pool = [(0, i, g) for i, g in enumerate(keep)] + [(1, i, g) for i, g in enumerate(received)]
        self.last_keep, self.last_received = keep, received


def picked(ids, weight, groups, columns, here, experts):
    length = ids.shape[0]
    column = lax.broadcasted_iota(jnp.int32, (1, columns), 1)
    wanted = jnp.full((1, columns), -1, jnp.int32)
    level = jnp.zeros((1, columns), jnp.int32)
    for place, (_, target) in enumerate(groups):
        inside = (column >= place * CAP) & (column < (place + 1) * CAP)
        wanted = jnp.where(inside, (here ^ target) & (experts - 1), wanted)
        level = jnp.where(inside, column - place * CAP, level)
    hits = jnp.zeros((length, columns), F32)
    share = jnp.zeros((length, columns), F32)
    for pick in range(ids.shape[1]):
        named = ids[:, pick : pick + 1] == wanted
        hits = hits + jnp.where(named, 1.0, 0.0)
        if weight is not None:
            share = share + jnp.where(named, weight[:, pick : pick + 1], 0.0)
    i = lax.broadcasted_iota(jnp.int32, (length, length), 0)
    j = lax.broadcasted_iota(jnp.int32, (length, length), 1)
    ranks = dot(jnp.where(j < i, 1.0, 0.0).astype(BF), hits.astype(BF))
    chosen = (hits > 0.5) & (jnp.abs(ranks - level.astype(F32)) < 0.5)
    return jnp.where(chosen, 1.0 if weight is None else share, 0.0)


def run_mask(groups, columns, experts, run):
    column = lax.broadcasted_iota(jnp.int32, (1, columns), 1)
    inside = jnp.zeros((1, columns), jnp.bool_)
    for place, (_, target) in enumerate(groups):
        if (target >= experts) == bool(run):
            inside = inside | ((column >= place * CAP) & (column < (place + 1) * CAP))
    return inside


def body(queries, key_rows, value_rows, segments, hidden_entry_rows, expert_ids, route_weight, w_gate, w_up, w_down):
    length = queries.shape[1]
    blocks, sides, cores = lax.axis_size("blk"), lax.axis_size("side"), lax.axis_size("tp")
    plan = Plan(blocks)
    experts = plan.experts
    quarter, ff = w_gate.shape[1], w_gate.shape[2]
    ids, shares = expert_ids[0], route_weight[0]

    def columns_of(run):
        half = (lax.axis_index("blk") // experts) ^ run
        return pl.ds(pl.multiple_of(half * quarter, quarter), quarter)

    first_rows = up_to(max(len(plan.first_keep), len(plan.first_send)) * CAP, 8)

    def choose(ids_ref, x_ref, send_ref, keep_ref):
        here = lax.axis_index("blk")
        for groups, out in ((plan.first_send, send_ref), (plan.first_keep, keep_ref)):
            sel = picked(ids_ref[...], None, groups, first_rows, here, experts)
            total = 0.0
            for run in range(2):
                part = jnp.where(run_mask(groups, first_rows, experts, run), sel, 0.0).astype(BF)
                total = total + dot_rows(part, x_ref[:, columns_of(run)])
            out[...] = total.astype(BF)

    send, keep = call(
        choose,
        [shaped(first_rows, quarter)] * 2,
        ids,
        hidden_entry_rows[0],
        flops=8 * length * first_rows * quarter,
    )

    def sorter(stage, rows, outs):
        def kernel(keep_ref, received_ref, *out_refs):
            for pieces, out in zip(stage, out_refs):
                total = 0.0
                for which, ref in ((0, keep_ref), (1, received_ref)):
                    part = [(to, start) for w, to, start in pieces if w == which]
                    if part:
                        total = total + dot(mover(out.shape[0], ref.shape[0], part), ref[...])
                out[...] = total.astype(BF)

        return kernel

    def sort(stage, keep, received):
        sizes = [up_to(len(pieces) * CAP, 8) for pieces in stage if pieces]
        outs = call(
            sorter(stage, None, None),
            [shaped(size, keep.shape[1]) for size in sizes],
            keep,
            received,
            flops=4 * keep.shape[0] * keep.shape[1] * sum(sizes),
        )
        return outs if len(outs) == 2 else (outs[0], None)

    for bit, stage in zip(plan.bits, plan.there):
        received = swapped(send, "blk", bit)
        keep, send = sort(stage, keep, received)
    rows = keep
    side_rows = rows.shape[0]

    gathered = [rows]
    whole = rows
    bit = 1
    while bit < sides:
        received = swapped(whole, "side", bit)
        gathered.append(received)
        bit *= 2
        if bit < sides:
            whole = jnp.concatenate([whole, received], axis=0)
    if len(gathered) > 2:
        lower, upper = whole, gathered[-1]
    else:
        lower, upper = gathered[0], gathered[1]
    half = lower.shape[0]

    def project(lower_ref, upper_ref, gate_ref, up_ref, send_ref, keep_ref):
        mine = lax.axis_index("tp") == 0
        low, high = lower_ref[...], upper_ref[...]
        away, stay = jnp.where(mine, high, low), jnp.where(mine, low, high)
        both = jnp.concatenate([away, stay], axis=0)
        for at, weight in ((0, gate_ref), (ff, up_ref)):
            terms = dot(both, weight[...])
            send_ref[:, at : at + ff] = terms[:half].astype(BF)
            keep_ref[:, at : at + ff] = terms[half:]

    term_send, term_keep = call(
        project,
        [shaped(half, 2 * ff), shaped(half, 2 * ff, F32)],
        lower,
        upper,
        w_gate[0],
        w_up[0],
        flops=8 * half * quarter * ff,
    )
    term_received = swapped(term_send, "tp", 1)

    moves = []
    for block in range(half // side_rows):
        for place, source in enumerate(plan.sources):
            moves.append((block * side_rows + place * CAP, block * side_rows + plan.sources.index(source ^ experts) * CAP))

    def add_terms(keep_ref, received_ref, sum_ref, send_ref):
        total = keep_ref[...] + received_ref[...].astype(F32)
        sum_ref[...] = total
        send_ref[...] = dot(mover(half, half, moves), total.astype(BF)).astype(BF)

    sums, sums_send = call(
        add_terms,
        [shaped(half, 2 * ff, F32), shaped(half, 2 * ff)],
        term_keep,
        term_received,
        flops=4 * half * half * ff,
    )
    sums_received = swapped(sums_send, "blk", experts)

    def activate(sum_ref, received_ref, hidden_ref):
        gate = sum_ref[:, :ff] + received_ref[:, :ff].astype(F32)
        up = sum_ref[:, ff:] + received_ref[:, ff:].astype(F32)
        hidden_ref[...] = (gate / (1.0 + jnp.exp(-gate)) * up).astype(BF)

    (hidden,) = call(activate, [shaped(half, ff)], sums, sums_received, exps=half * ff)
    hidden_received = swapped(hidden, "tp", 1)

    def project_back(hidden_ref, received_ref, down_ref, low_ref, high_ref):
        mine = lax.axis_index("tp") == 0
        here, there = hidden_ref[...], received_ref[...]
        low, high = jnp.where(mine, here, there), jnp.where(mine, there, here)
        out = dot(jnp.concatenate([low, high], axis=0), down_ref[...])
        low_ref[...] = out[:half]
        high_ref[...] = out[half:].astype(BF)

    low, high = call(
        project_back,
        [shaped(half, quarter, F32), shaped(half, quarter)],
        hidden,
        hidden_received,
        w_down[0],
        flops=4 * half * ff * quarter,
    )

    bit = sides // 2
    received = swapped(high, "side", bit)
    while bit > 1:
        low = low + received.astype(F32)
        bit //= 2
        size = low.shape[0] // 2
        low, high = low[:size], low[size:].astype(BF)
        received = swapped(high, "side", bit)

    def summed_sorter(stage):
        def kernel(keep_ref, received_ref, *out_refs):
            total = (keep_ref[...] + received_ref[...].astype(F32)).astype(BF)
            for pieces, out in zip(stage, out_refs):
                part = [(to, start) for _, to, start in pieces]
                out[...] = dot(mover(out.shape[0], total.shape[0], part), total).astype(BF)

        return kernel

    stage = plan.back[0]
    sizes = [up_to(len(pieces) * CAP, 8) for pieces in stage]
    keep, send = call(
        summed_sorter(stage),
        [shaped(size, quarter) for size in sizes],
        low,
        received,
        flops=2 * side_rows * quarter * sum(sizes),
    )
    for bit, stage in zip(plan.bits[::-1], plan.back[1:]):
        received = swapped(send, "blk", bit)
        keep, send = sort(stage, keep, received)
    received = swapped(send, "blk", plan.bits[0])

    def share_out(ids_ref, weight_ref, keep_ref, received_ref):
        here = lax.axis_index("blk")
        for groups, out in ((plan.last_keep, keep_ref), (plan.last_received, received_ref)):
            out[...] = picked(ids_ref[...], weight_ref[...], groups, first_rows, here, experts)

    keep_share, received_share = call(share_out, [shaped(length, first_rows, F32)] * 2, ids, shares, flops=1000)

    def mix(keep_ref, received_ref, keep_share_ref, received_share_ref, out_ref):
        for run in range(2):
            total = 0.0
            for groups, rows_ref, share_ref in (
                (plan.last_keep, keep_ref, keep_share_ref),
                (plan.last_received, received_ref, received_share_ref),
            ):
                share = jnp.where(run_mask(groups, first_rows, experts, run), share_ref[...], 0.0)
                coarse = share.astype(BF)
                rest = (share - coarse.astype(F32)).astype(BF)
                total = total + dot(coarse, rows_ref[...]) + dot(rest, rows_ref[...])
            out_ref[:, columns_of(run)] = total.astype(BF)

    (moe_out,) = call(
        mix,
        [shaped(length, 2 * quarter)],
        keep,
        received,
        keep_share,
        received_share,
        flops=16 * length * first_rows * quarter,
    )

    labels = jnp.pad(segments.astype(BF), ((0, 15), (0, 0)))
    held = jnp.concatenate([key_rows[0], value_rows[0], labels], axis=0)[None]
    order = [0]
    for bit in plan.bits[::-1]:
        held = jnp.concatenate([held, swapped(held, "blk", bit)], axis=0)
        order = order + [place ^ bit for place in order]
    heads = queries.shape[2] // HEAD_DIM
    factor = 1.0 / math.sqrt(HEAD_DIM)
    span = blocks * length

    def attend(query_ref, held_ref, segment_ref, out_ref, keys, values, bias):
        here = lax.axis_index("blk")
        i = lax.broadcasted_iota(jnp.int32, (length, length), 0)
        j = lax.broadcasted_iota(jnp.int32, (length, length), 1)
        own = jnp.sum(jnp.where(i == j, segment_ref[...].astype(F32), 0.0), axis=1, keepdims=True)
        for place, other in enumerate(order):
            at = place * length
            keys[at : at + length, :] = held_ref[place, :length, :]
            values[at : at + length, :] = held_ref[place, length : 2 * length, :]
            label = held_ref[place, 2 * length : 2 * length + 16, :].astype(F32)[:1]
            same = own == label
            if other == 0:
                seen = same & (j <= i)
            else:
                seen = same & ((here ^ other) < here)
            bias[:, at : at + length] = jnp.where(seen, 0.0, -1e30)

        def one_head(head):
            columns = pl.ds(pl.multiple_of(head * HEAD_DIM, HEAD_DIM), HEAD_DIM)
            scores = lax.dot_general(
                query_ref[:, columns], keys[...], (((1,), (1,)), ((), ())), preferred_element_type=F32
            )
            scores = scores + bias[...]
            top = jnp.max(scores, axis=1, keepdims=True)
            weights = jnp.exp((scores - top) * factor)
            totals = jnp.sum(weights, axis=1, keepdims=True)
            out = dot(weights.astype(BF), values[...])
            out_ref[:, columns] = (out / totals).astype(BF)

        if span <= 1024:
            for head in range(heads):
                one_head(head)
        else:
            lax.fori_loop(0, heads, lambda head, _: (one_head(head), 0)[1], 0)

    (attended,) = call(
        attend,
        [shaped(length, heads * HEAD_DIM)],
        queries[0],
        held,
        segments,
        scratch=[pltpu.VMEM((span, HEAD_DIM), BF)] * 2 + [pltpu.VMEM((length, span), F32)],
        flops=4 * heads * length * span * HEAD_DIM,
        exps=heads * length * span,
    )
    return attended[None], moe_out[None]


def solution(mesh):
    rows = P(("groups", "side"), "blk", "tp")
    placed = (
        rows,
        rows,
        rows,
        P(("groups", "side"), "blk"),
        rows,
        P(("groups", "side"), "blk", None),
        P(("groups", "side"), "blk", None),
        P("blk", "tp", "side"),
        P("blk", "tp", "side"),
        P("blk", "side", "tp"),
    )
    return jax.shard_map(body, mesh=mesh, in_specs=placed, out_specs=(rows, rows), check_vma=False)
```

time: 132 us -> 55.6 us (0.42)
  blocking collectives: 43 us -> 0 us
  between operations: 14.2 us -> 0.76 us
  matrix products: 12.9 us -> 0 us
  Pallas kernels: 0 us -> 10.5 us
  waiting for transfers between devices: 30.5 us -> 21.7 us
  other arithmetic: 6.27 us -> 0.05 us
  local copies, waits for them, and re-layouts: 7.85 us -> 4.77 us
    all_gather x4 -> x0, blocking collectives: 43 us -> none  [the longest x1 13.6 us: body(): key_piece = lax.all_gather(key_rows[0], 'blk', axis=0, tiled=True)]
    ppermute x1 -> x11, starting transfers between devices: 2.74 us -> 17.6 us  [swapped(): return lax.ppermute(value, axis, [(i, i ^ bit) for i in range(count)])]
    psum x1 -> x0, waiting for transfers between devices: 14.3 us -> none  [body(): lax.psum(gate_part.astype(jnp.bfloat16), 'tp').astype(jnp.float32)]
    all_to_all x3 -> x0, starting transfers between devices: 13.6 us -> none  [the longest x1 6.32 us: body(): lax.all_to_all(outgoing, 'blk', split_axis=0, concat_axis=0, tiled=True)]
    dot_general x6 -> x0, matrix products: 12.9 us -> none  [the longest x1 3.42 us: one_block(): jnp.einsum('jzre,ezm->jzrm', weights.astype(jnp.bfloat16), value_block, p...]
    pallas_call x0 -> x12, Pallas kernels: none -> 10.5 us  [call(): pl.pallas_call(kernel, out_shape=list(outs), in_specs=[VMEM] * len(ins),...]
    ppermute x1 -> x11, waiting for transfers between devices: 14.8 us -> 21.7 us  [swapped(): return lax.ppermute(value, axis, [(i, i ^ bit) for i in range(count)])]
    reduce_sum x5 -> x0, other arithmetic: 4.3 us -> none  [the longest x1 3.23 us: one_block(): totals = totals * rescale + jnp.sum(weights, axis=3)]
  transfers between devices with their start and end apart: 5 -> 11, of which waited for: 3 -> 8; matrix products, arithmetic and copies ran while one was open for 10% -> 0% of each run, Pallas kernels for 0% -> 12%
where the time goes in v1:
time: 55.6 us; the launch traced here: 55.3 us
  waiting for transfers between devices  21.7 us (39%)
  starting transfers between devices  17.6 us (32%)
  Pallas kernels  10.5 us (19%)
  local copies, waits for them, and re-layouts  4.77 us (9%)
  between operations  0.76 us (1%)
    ppermute x11, waiting for transfers between devices, swapped(): return lax.ppermute(value, axis, [(i, i ^ bit) for i in range(count)])  21.7 us
    ppermute x11, starting transfers between devices, swapped(): return lax.ppermute(value, axis, [(i, i ^ bit) for i in range(count)])  17.6 us
    pallas_call x12, Pallas kernels, call(): pl.pallas_call(kernel, out_shape=list(outs), in_specs=[VMEM] * len(ins),...  10.5 us
    unnamed x20, local copies, waits for them, and re-layouts  4.77 us
  transfers between devices with their start and end apart: 11, of which 8 were waited for; matrix products, arithmetic and copies ran while one was open for 0% of the time, Pallas kernels for 12%

profile of v1, /device:TPU:0, one launch (start us, length us, event | category | flops | bytes accessed | tf_op | source)
XLA Modules:
  0.0 55.3 jit_solution(13177912958998016991)
XLA Ops:
  0.6 0.8 %copy.12 = s32[1,128,8]{2,1,0:T(8,128)S(1)} copy(s32[1,128,8]{1,2,0:T(8,128)} %param.15) | data formatting | bytes 8192 | tf_op args[5]
  1.4 1.0 %copy-done.3 = bf16[1,128,2048]{2,1,0:T(8,128)(2,1)S(1)} copy-done((bf16[1,128,2048]{2,1,0:T(8,128)(2,1)S(1)}, bf16[1,128,2048]{2,1,0:T(8,128)(2,1)}, u32[]{:S(2)}) %copy-start.3) | copy-done | bytes 524312
  2.5 1.0 %shard_map.114 = (bf16[24,1024]{1,0:T(8,128)(2,1)S(1)}, bf16[24,1024]{1,0:T(8,128)(2,1)S(1)}) custom-call(s32[128,8]{1,0:T(8,128)S(1)} %bitcast.16, bf16[128,2048]{1,0:T(8,128)(2,1)S(1)} %bitcast.18), custom_call_target="tpu_custom_call" | custom-call | flops 25165824 | bytes 626688 | tf_op jit(solution)/shard_map/pallas_call | solution.py:29
  3.5 3.1 %collective-permute-start.2 = (bf16[24,1024]{1,0:T(8,128)(2,1)S(1)}, bf16[24,1024]{1,0:T(8,128)(2,1)S(1)}, u32[]{:S(2)}, u32[]{:S(2)}) collective-permute-start(bf16[24,1024]{1,0:T(8,128)(2,1)S(1)} %get-tuple-element.19), channel_id=1, source_target_pairs={{0,4},{4,0},{8,12},{12,8},{1,5},{5,1},{9,13},{13,9},{2,6},{6,2},{1... | collective-permute-start | bytes 147464 | tf_op jit(solution)/shard_map/ppermute | solution.py:19
  6.6 2.1 %collective-permute-done.2.received_ref = bf16[24,1024]{1,0:T(8,128)(2,1)S(1)} collective-permute-done((bf16[24,1024]{1,0:T(8,128)(2,1)S(1)}, bf16[24,1024]{1,0:T(8,128)(2,1)S(1)}, u32[]{:S(2)}, u32[]{:S(2)}) %collective-permute-start.2) | collective-permute-done | bytes 49184 | tf_op jit(solution)/shard_map/ppermute | solution.py:19
  8.7 0.2 shard_map.115
  8.9 3.1 %collective-permute-start.3 = (bf16[24,1024]{1,0:T(8,128)(2,1)S(1)}, bf16[24,1024]{1,0:T(8,128)(2,1)S(1)}, u32[]{:S(2)}, u32[]{:S(2)}) collective-permute-start(bf16[24,1024]{1,0:T(8,128)(2,1)S(1)} %get-tuple-element.21), channel_id=1, source_target_pairs={{0,8},{4,12},{8,0},{12,4},{1,9},{5,13},{9,1},{13,5},{2,10},{6,14},... | collective-permute-start | bytes 147464 | tf_op jit(solution)/shard_map/ppermute | solution.py:19
  12.0 2.1 %collective-permute-done.3.received_ref = bf16[24,1024]{1,0:T(8,128)(2,1)S(1)} collective-permute-done((bf16[24,1024]{1,0:T(8,128)(2,1)S(1)}, bf16[24,1024]{1,0:T(8,128)(2,1)S(1)}, u32[]{:S(2)}, u32[]{:S(2)}) %collective-permute-start.3) | collective-permute-done | bytes 49184 | tf_op jit(solution)/shard_map/ppermute | solution.py:19
  14.0 0.2 shard_map.116.lower_ref
  14.2 1.9 %collective-permute-start.4 = (bf16[40,1024]{1,0:T(8,128)(2,1)S(1)}, bf16[40,1024]{1,0:T(8,128)(2,1)S(1)}, u32[]{:S(2)}, u32[]{:S(2)}) collective-permute-start(bf16[40,1024]{1,0:T(8,128)(2,1)S(1)} %shard_map.116.lower_ref), channel_id=1, source_target_pairs={{0,2},{2,0},{1,3},{3,1},{4,6},{6,4},{5,7},{7,5},{8,10},{10,8},{9,1... | collective-permute-start | bytes 245768 | tf_op jit(solution)/shard_map/ppermute | solution.py:19
  16.1 2.6 %collective-permute-done.4.upper_ref = bf16[40,1024]{1,0:T(8,128)(2,1)S(1)} collective-permute-done((bf16[40,1024]{1,0:T(8,128)(2,1)S(1)}, bf16[40,1024]{1,0:T(8,128)(2,1)S(1)}, u32[]{:S(2)}, u32[]{:S(2)}) %collective-permute-start.4) | collective-permute-done | bytes 81952 | tf_op jit(solution)/shard_map/ppermute | solution.py:19
  18.7 1.4 %copy-done = bf16[1,1024,768]{2,1,0:T(8,128)(2,1)S(1)} copy-done((bf16[1,1024,768]{2,1,0:T(8,128)(2,1)S(1)}, bf16[1,1024,768]{2,1,0:T(8,128)(2,1)}, u32[]{:S(2)}) %copy-start) | copy-done | bytes 1572888
  20.1 1.4 %copy-done.1 = bf16[1,1024,768]{2,1,0:T(8,128)(2,1)S(1)} copy-done((bf16[1,1024,768]{2,1,0:T(8,128)(2,1)S(1)}, bf16[1,1024,768]{2,1,0:T(8,128)(2,1)}, u32[]{:S(2)}) %copy-start.1) | copy-done | bytes 1572888
  21.5 0.7 %shard_map.117 = (bf16[40,1536]{1,0:T(8,128)(2,1)S(1)}, f32[40,1536]{1,0:T(8,128)S(1)}) custom-call(bf16[40,1024]{1,0:T(8,128)(2,1)S(1)} %shard_map.116.lower_ref, bf16[40,1024]{1,0:T(8,128)(2,1)S(1)} %collective-permute-done.4.upper_ref, bf16[1024,768]{1,0:T(8,128)(2,1)S(1)} %bitcast.13, bf16[1024,768]{1,0:T(8,128)(2,1)S(1)} %bitcast.14), custom_call_target="tpu_custom_call" | custom-call | flops 251658240 | bytes 3678208 | tf_op jit(solution)/shard_map/pallas_call | solution.py:29
  22.3 1.3 %collective-permute-done.5.received_ref = bf16[40,1536]{1,0:T(8,128)(2,1)S(1)} collective-permute-done((bf16[40,1536]{1,0:T(8,128)(2,1)S(1)}, bf16[40,1536]{1,0:T(8,128)(2,1)S(1)}, u32[]{:S(2)}, u32[]{:S(2)}) %collective-permute-start.5) | collective-permute-done | bytes 122912 | tf_op jit(solution)/shard_map/ppermute | solution.py:19
  23.6 0.2 shard_map.118
  23.8 3.0 %collective-permute-start.6 = (bf16[40,1536]{1,0:T(8,128)(2,1)S(1)}, bf16[40,1536]{1,0:T(8,128)(2,1)S(1)}, u32[]{:S(2)}, u32[]{:S(2)}) collective-permute-start(bf16[40,1536]{1,0:T(8,128)(2,1)S(1)} %get-tuple-element.25), channel_id=1, source_target_pairs={{0,8},{4,12},{8,0},{12,4},{1,9},{5,13},{9,1},{13,5},{2,10},{6,14},... | collective-permute-start | bytes 368648 | tf_op jit(solution)/shard_map/ppermute | solution.py:19
  27.0 8.1 %collective-permute-done.6.received_ref = bf16[40,1536]{1,0:T(8,128)(2,1)S(1)} collective-permute-done((bf16[40,1536]{1,0:T(8,128)(2,1)S(1)}, bf16[40,1536]{1,0:T(8,128)(2,1)S(1)}, u32[]{:S(2)}, u32[]{:S(2)}) %collective-permute-start.6) | collective-permute-done | bytes 122912 | tf_op jit(solution)/shard_map/ppermute | solution.py:19
  35.2 0.9 %collective-permute-done = bf16[1,272,128]{2,1,0:T(8,128)(2,1)S(1)} collective-permute-done((bf16[1,272,128]{2,1,0:T(8,128)(2,1)S(1)}, bf16[1,272,128]{2,1,0:T(8,128)(2,1)S(1)}, u32[]{:S(2)}, u32[]{:S(2)}) %collective-permute-start) | collective-permute-done | bytes 69664 | tf_op jit(solution)/shard_map/ppermute | solution.py:19
  36.1 0.8 %collective-permute-start.1 = (bf16[2,272,128]{2,1,0:T(8,128)(2,1)S(1)}, bf16[2,272,128]{2,1,0:T(8,128)(2,1)S(1)}, u32[]{:S(2)}, u32[]{:S(2)}) collective-permute-start(bf16[2,272,128]{2,1,0:T(8,128)(2,1)S(1)} %pad_maximum_fusion.1), channel_id=1, source_target_pairs={{0,4},{4,0},{8,12},{12,8},{1,5},{5,1},{9,13},{13,9},{2,6},{6,2},{1... | collective-permute-start | bytes 417800 | tf_op jit(solution)/shard_map/ppermute | solution.py:19
  36.9 0.4 shard_map.120
  37.3 1.6 %collective-permute-start.8 = (bf16[40,1024]{1,0:T(8,128)(2,1)S(1)}, bf16[40,1024]{1,0:T(8,128)(2,1)S(1)}, u32[]{:S(2)}, u32[]{:S(2)}) collective-permute-start(bf16[40,1024]{1,0:T(8,128)(2,1)S(1)} %get-tuple-element.27), channel_id=1, source_target_pairs={{0,2},{2,0},{1,3},{3,1},{4,6},{6,4},{5,7},{7,5},{8,10},{10,8},{9,1... | collective-permute-start | bytes 245768 | tf_op jit(solution)/shard_map/ppermute | solution.py:19
  38.9 0.1 copy.13
  39.0 0.7 %shard_map.123 = (f32[128,24]{1,0:T(8,128)S(1)}, f32[128,24]{1,0:T(8,128)S(1)}) custom-call(s32[128,8]{1,0:T(8,128)S(1)} %bitcast.17, f32[128,8]{1,0:T(8,128)S(1)} %bitcast.19), custom_call_target="tpu_custom_call" | custom-call | flops 1000 | bytes 32768 | tf_op jit(solution)/shard_map/pallas_call | solution.py:29
  39.7 2.1 %collective-permute-done.8.received_ref = bf16[40,1024]{1,0:T(8,128)(2,1)S(1)} collective-permute-done((bf16[40,1024]{1,0:T(8,128)(2,1)S(1)}, bf16[40,1024]{1,0:T(8,128)(2,1)S(1)}, u32[]{:S(2)}, u32[]{:S(2)}) %collective-permute-start.8) | collective-permute-done | bytes 81952 | tf_op jit(solution)/shard_map/ppermute | solution.py:19
  41.8 0.2 shard_map.121
  42.0 3.4 %collective-permute-start.9 = (bf16[24,1024]{1,0:T(8,128)(2,1)S(1)}, bf16[24,1024]{1,0:T(8,128)(2,1)S(1)}, u32[]{:S(2)}, u32[]{:S(2)}) collective-permute-start(bf16[24,1024]{1,0:T(8,128)(2,1)S(1)} %get-tuple-element.29), channel_id=1, source_target_pairs={{0,8},{4,12},{8,0},{12,4},{1,9},{5,13},{9,1},{13,5},{2,10},{6,14},... | collective-permute-start | bytes 147464 | tf_op jit(solution)/shard_map/ppermute | solution.py:19
  45.5 2.6 %collective-permute-done.9.received_ref = bf16[24,1024]{1,0:T(8,128)(2,1)S(1)} collective-permute-done((bf16[24,1024]{1,0:T(8,128)(2,1)S(1)}, bf16[24,1024]{1,0:T(8,128)(2,1)S(1)}, u32[]{:S(2)}, u32[]{:S(2)}) %collective-permute-start.9) | collective-permute-done | bytes 49184 | tf_op jit(solution)/shard_map/ppermute | solution.py:19
  48.0 0.2 shard_map.122
  48.2 0.5 collective-permute-start.10
  48.7 5.2 %shard_map.113 = bf16[128,2048]{1,0:T(8,128)(2,1)} custom-call(bf16[128,2048]{1,0:T(8,128)(2,1)S(1)} %bitcast.20, bf16[4,272,128]{2,1,0:T(8,128)(2,1)S(1)} %pad_maximum_fusion.held_ref, s32[1,128]{1,0:T(1,128)S(1)} %copy-done.5), custom_call_target="tpu_custom_call" | custom-call | flops 536870912 | bytes 1327616 | tf_op jit(solution)/shard_map/pallas_call | solution.py:29
  53.9 1.5 %shard_map.124 = bf16[128,2048]{1,0:T(8,128)(2,1)} custom-call(bf16[24,1024]{1,0:T(8,128)(2,1)S(1)} %get-tuple-element.30.keep_ref, bf16[24,1024]{1,0:T(8,128)(2,1)S(1)} %collective-permute-done.10.received_ref, f32[128,24]{1,0:T(8,128)S(1)} %get-tuple-element.32.keep_share_ref, f32[128,24]{1,0:T(8,128)S(1)} %get-tuple-element.33.received_share_ref), custom_call_target="tpu_custom_call" | custom-call | flops 50331648 | bytes 647168 | tf_op jit(solution)/shard_map/pallas_call | solution.py:29
  (26 shorter events, 0.4 us)
Async XLA Ops:
  1.4 1.0 %copy-start.3 = (bf16[1,128,2048]{2,1,0:T(8,128)(2,1)S(1)}, bf16[1,128,2048]{2,1,0:T(8,128)(2,1)}, u32[]{:S(2)}) copy-start(bf16[1,128,2048]{2,1,0:T(8,128)(2,1)} %param.14) | copy-start | bytes 1572868
  3.5 5.2 %collective-permute-start.2 = (bf16[24,1024]{1,0:T(8,128)(2,1)S(1)}, bf16[24,1024]{1,0:T(8,128)(2,1)S(1)}, u32[]{:S(2)}, u32[]{:S(2)}) collective-permute-start(bf16[24,1024]{1,0:T(8,128)(2,1)S(1)} %get-tuple-element.19), channel_id=1, source_target_pairs={{0,4},{4,0},{8,12},{12,8},{1,5},{5,1},{9,13},{13,9},{2,6},{6,2},{1... | collective-permute-start | bytes 147464 | tf_op jit(solution)/shard_map/ppermute | solution.py:19
  8.9 5.2 %collective-permute-start.3 = (bf16[24,1024]{1,0:T(8,128)(2,1)S(1)}, bf16[24,1024]{1,0:T(8,128)(2,1)S(1)}, u32[]{:S(2)}, u32[]{:S(2)}) collective-permute-start(bf16[24,1024]{1,0:T(8,128)(2,1)S(1)} %get-tuple-element.21), channel_id=1, source_target_pairs={{0,8},{4,12},{8,0},{12,4},{1,9},{5,13},{9,1},{13,5},{2,10},{6,14},... | collective-permute-start | bytes 147464 | tf_op jit(solution)/shard_map/ppermute | solution.py:19
  14.2 4.5 %collective-permute-start.4 = (bf16[40,1024]{1,0:T(8,128)(2,1)S(1)}, bf16[40,1024]{1,0:T(8,128)(2,1)S(1)}, u32[]{:S(2)}, u32[]{:S(2)}) collective-permute-start(bf16[40,1024]{1,0:T(8,128)(2,1)S(1)} %shard_map.116.lower_ref), channel_id=1, source_target_pairs={{0,2},{2,0},{1,3},{3,1},{4,6},{6,4},{5,7},{7,5},{8,10},{10,8},{9,1... | collective-permute-start | bytes 245768 | tf_op jit(solution)/shard_map/ppermute | solution.py:19
  18.7 1.4 %copy-start = (bf16[1,1024,768]{2,1,0:T(8,128)(2,1)S(1)}, bf16[1,1024,768]{2,1,0:T(8,128)(2,1)}, u32[]{:S(2)}) copy-start(bf16[1,1024,768]{2,1,0:T(8,128)(2,1)} %param.17) | copy-start | bytes 4718596
  20.1 1.4 %copy-start.1 = (bf16[1,1024,768]{2,1,0:T(8,128)(2,1)S(1)}, bf16[1,1024,768]{2,1,0:T(8,128)(2,1)}, u32[]{:S(2)}) copy-start(bf16[1,1024,768]{2,1,0:T(8,128)(2,1)} %param.18) | copy-start | bytes 4718596
  21.5 0.8 %copy-start.5 = (s32[1,128]{1,0:T(1,128)S(1)}, s32[1,128]{1,0:T(1,128)}, u32[]{:S(2)}) copy-start(s32[1,128]{1,0:T(1,128)} %segment_ref.1) | copy-start | bytes 1540
  21.5 5.3 %copy-start.6 = (bf16[1,128,128]{2,1,0:T(8,128)(2,1)S(1)}, bf16[1,128,128]{2,1,0:T(8,128)(2,1)}, u32[]{:S(2)}) copy-start(bf16[1,128,128]{2,1,0:T(8,128)(2,1)} %param.12) | copy-start | bytes 98308
  21.5 5.3 %copy-start.7 = (bf16[1,128,128]{2,1,0:T(8,128)(2,1)S(1)}, bf16[1,128,128]{2,1,0:T(8,128)(2,1)}, u32[]{:S(2)}) copy-start(bf16[1,128,128]{2,1,0:T(8,128)(2,1)} %param.11) | copy-start | bytes 98308
  21.5 15.4 %copy-start.2 = (bf16[1,768,1024]{2,1,0:T(8,128)(2,1)S(1)}, bf16[1,768,1024]{2,1,0:T(8,128)(2,1)}, u32[]{:S(2)}) copy-start(bf16[1,768,1024]{2,1,0:T(8,128)(2,1)} %param.19) | copy-start | bytes 4718596
  22.2 16.7 %copy-start.8 = (f32[1,128,8]{1,2,0:T(8,128)S(1)}, f32[1,128,8]{1,2,0:T(8,128)}, u32[]{:S(2)}) copy-start(f32[1,128,8]{1,2,0:T(8,128)} %param.16) | copy-start | bytes 12292
  22.2 1.4 %collective-permute-start.5 = (bf16[40,1536]{1,0:T(8,128)(2,1)S(1)}, bf16[40,1536]{1,0:T(8,128)(2,1)S(1)}, u32[]{:S(2)}, u32[]{:S(2)}) collective-permute-start(bf16[40,1536]{1,0:T(8,128)(2,1)S(1)} %get-tuple-element.23), channel_id=1, source_target_pairs={{0,1},{1,0},{2,3},{3,2},{4,5},{5,4},{6,7},{7,6},{8,9},{9,8},{10,11... | collective-permute-start | bytes 368648 | tf_op jit(solution)/shard_map/ppermute | solution.py:19
  23.8 11.3 %collective-permute-start.6 = (bf16[40,1536]{1,0:T(8,128)(2,1)S(1)}, bf16[40,1536]{1,0:T(8,128)(2,1)S(1)}, u32[]{:S(2)}, u32[]{:S(2)}) collective-permute-start(bf16[40,1536]{1,0:T(8,128)(2,1)S(1)} %get-tuple-element.25), channel_id=1, source_target_pairs={{0,8},{4,12},{8,0},{12,4},{1,9},{5,13},{9,1},{13,5},{2,10},{6,14},... | collective-permute-start | bytes 368648 | tf_op jit(solution)/shard_map/ppermute | solution.py:19
  26.9 9.2 %collective-permute-start = (bf16[1,272,128]{2,1,0:T(8,128)(2,1)S(1)}, bf16[1,272,128]{2,1,0:T(8,128)(2,1)S(1)}, u32[]{:S(2)}, u32[]{:S(2)}) collective-permute-start(bf16[1,272,128]{2,1,0:T(8,128)(2,1)S(1)} %fusion.2), channel_id=1, source_target_pairs={{0,8},{4,12},{8,0},{12,4},{1,9},{5,13},{9,1},{13,5},{2,10},{6,14},... | collective-permute-start | bytes 208904 | tf_op jit(solution)/shard_map/ppermute | solution.py:19
  35.1 13.6 %copy-start.4 = (bf16[1,128,2048]{2,1,0:T(8,128)(2,1)S(1)}, bf16[1,128,2048]{2,1,0:T(8,128)(2,1)}, u32[]{:S(2)}) copy-start(bf16[1,128,2048]{2,1,0:T(8,128)(2,1)} %param.10) | copy-start | bytes 1572868
  35.1 1.8 %collective-permute-start.7 = (bf16[40,768]{1,0:T(8,128)(2,1)S(1)}, bf16[40,768]{1,0:T(8,128)(2,1)S(1)}, u32[]{:S(2)}, u32[]{:S(2)}) collective-permute-start(bf16[40,768]{1,0:T(8,128)(2,1)S(1)} %shard_map.119.hidden_ref), channel_id=1, source_target_pairs={{0,1},{1,0},{2,3},{3,2},{4,5},{5,4},{6,7},{7,6},{8,9},{9,8},{10,11... | collective-permute-start | bytes 184328 | tf_op jit(solution)/shard_map/ppermute | solution.py:19
  36.1 9.3 %collective-permute-start.1 = (bf16[2,272,128]{2,1,0:T(8,128)(2,1)S(1)}, bf16[2,272,128]{2,1,0:T(8,128)(2,1)S(1)}, u32[]{:S(2)}, u32[]{:S(2)}) collective-permute-start(bf16[2,272,128]{2,1,0:T(8,128)(2,1)S(1)} %pad_maximum_fusion.1), channel_id=1, source_target_pairs={{0,4},{4,0},{8,12},{12,8},{1,5},{5,1},{9,13},{13,9},{2,6},{6,2},{1... | collective-permute-start | bytes 417800 | tf_op jit(solution)/shard_map/ppermute | solution.py:19
  37.3 4.5 %collective-permute-start.8 = (bf16[40,1024]{1,0:T(8,128)(2,1)S(1)}, bf16[40,1024]{1,0:T(8,128)(2,1)S(1)}, u32[]{:S(2)}, u32[]{:S(2)}) collective-permute-start(bf16[40,1024]{1,0:T(8,128)(2,1)S(1)} %get-tuple-element.27), channel_id=1, source_target_pairs={{0,2},{2,0},{1,3},{3,1},{4,6},{6,4},{5,7},{7,5},{8,10},{10,8},{9,1... | collective-permute-start | bytes 245768 | tf_op jit(solution)/shard_map/ppermute | solution.py:19
  42.0 6.0 %collective-permute-start.9 = (bf16[24,1024]{1,0:T(8,128)(2,1)S(1)}, bf16[24,1024]{1,0:T(8,128)(2,1)S(1)}, u32[]{:S(2)}, u32[]{:S(2)}) collective-permute-start(bf16[24,1024]{1,0:T(8,128)(2,1)S(1)} %get-tuple-element.29), channel_id=1, source_target_pairs={{0,8},{4,12},{8,0},{12,4},{1,9},{5,13},{9,1},{13,5},{2,10},{6,14},... | collective-permute-start | bytes 147464 | tf_op jit(solution)/shard_map/ppermute | solution.py:19
  48.2 5.7 %collective-permute-start.10 = (bf16[24,1024]{1,0:T(8,128)(2,1)S(1)}, bf16[24,1024]{1,0:T(8,128)(2,1)S(1)}, u32[]{:S(2)}, u32[]{:S(2)}) collective-permute-start(bf16[24,1024]{1,0:T(8,128)(2,1)S(1)} %get-tuple-element.31), channel_id=1, source_target_pairs={{0,4},{4,0},{8,12},{12,8},{1,5},{5,1},{9,13},{13,9},{2,6},{6,2},{1... | collective-permute-start | bytes 147464 | tf_op jit(solution)/shard_map/ppermute | solution.py:19

commit v2 on v1

v2 whole, which is shorter than its diff:
```python
import math

import jax
import jax.numpy as jnp
from jax import lax
from jax.experimental import pallas as pl
from jax.experimental.pallas import tpu as pltpu
from jax.sharding import PartitionSpec as P

HEAD_DIM = 128
CAP = 10
COST = 3_000_000_000
BF = jnp.bfloat16
F32 = jnp.float32
VMEM = pl.BlockSpec(memory_space=pltpu.VMEM)
HBM = pl.BlockSpec(memory_space=pltpu.HBM)


def swapped(value, axis, bit):
    count = lax.axis_size(axis)
    return lax.ppermute(value, axis, [(i, i ^ bit) for i in range(count)])


def up_to(value, step):
    return -(-value // step) * step


def call(kernel, outs, *ins, scratch=(), semaphores=0, far_in=(), far_out=(), aliases=None, flops=0, exps=0, grant=0):
    moved = sum(math.prod(a.shape) * a.dtype.itemsize for a in (*ins, *outs))
    held = sum(math.prod(s.shape) * s.dtype.itemsize for s in scratch)
    scratch = list(scratch) + ([pltpu.SemaphoreType.DMA((semaphores,))] if semaphores else [])
    return pl.pallas_call(
        kernel,
        out_shape=list(outs),
        in_specs=[HBM if i in far_in else VMEM for i in range(len(ins))],
        out_specs=[HBM if i in far_out else VMEM for i in range(len(outs))],
        scratch_shapes=scratch,
        input_output_aliases=aliases or {},
        compiler_params=pltpu.CompilerParams(vmem_limit_bytes=grant or 2 * moved + held + (2 << 20)),
        cost_estimate=pl.CostEstimate(flops=flops, bytes_accessed=moved, transcendentals=exps),
    )(*ins)


def shaped(rows, columns, dtype=BF):
    return jax.ShapeDtypeStruct((rows, columns), dtype)


def dot(a, b):
    return jnp.dot(a, b, preferred_element_type=F32)


def dot_rows(a, b):
    return lax.dot_general(a, b, (((0,), (0,)), ((), ())), preferred_element_type=F32)


def mover(rows_out, rows_in, pieces):
    i = lax.broadcasted_iota(jnp.int32, (rows_out, rows_in), 0)
    j = lax.broadcasted_iota(jnp.int32, (rows_out, rows_in), 1)
    hit = jnp.zeros((rows_out, rows_in), jnp.bool_)
    for to, start in pieces:
        hit = hit | ((j - i == start - to) & (i >= to) & (i < to + CAP))
    return jnp.where(hit, 1.0, 0.0).astype(BF)


class Plan:
    def __init__(self, count):
        self.count, self.experts = count, count // 2
        self.bits = [1 << i for i in reversed(range(1, count.bit_length() - 1))]
        keep = [(0, d) for d in range(self.experts)]
        send = [(0, d) for d in range(self.experts, count)]
        self.there = []
        for bit, later in zip(self.bits, self.bits[1:] + [1]):
            pool = self.pool(keep, send, bit)
            stage, keep, send = self.split(pool, lambda group: group[1] & later)
            self.there.append(stage)
        near = [s for s, _ in keep]
        self.sources = near + [s ^ 1 for s in near]
        self.back = []
        pool = [(i, j, (s, i)) for i in range(2) for j, s in enumerate(near)]
        for bit in reversed(self.bits):
            stage, keep, send = self.split(pool, lambda group: group[0] & bit)
            self.back.append(stage)
            pool = self.pool(keep, send, bit)
        self.ranked = [d for _, d in keep]

    def pool(self, keep, send, bit):
        received = [(s ^ bit, d ^ bit) for s, d in send]
        return [(0, i, g) for i, g in enumerate(keep)] + [(1, i, g) for i, g in enumerate(received)]

    def split(self, pool, goes):
        stage, groups = ([], []), ([], [])
        for which, place, group in pool:
            side = 1 if goes(group) else 0
            stage[side].append((which, len(groups[side]) * CAP, place * CAP))
            groups[side].append(group)
        return stage, groups[0], groups[1]


def sorted_rows(pieces, size, parts):
    total = 0.0
    for which, part in enumerate(parts):
        moves = [(to, start) for w, to, start in pieces if w == which]
        if moves:
            total = total + dot(mover(size, part.shape[0], moves), part)
    return total.astype(BF)


def ranked(ids, weight, earlier, rows, here, wanted):
    length = ids.shape[1]
    row = lax.broadcasted_iota(jnp.int32, (rows, 1), 0)
    expert = jnp.full((rows, 1), -1, jnp.int32)
    level = jnp.zeros((rows, 1), jnp.int32)
    for place, target in enumerate(wanted):
        inside = (row >= place * CAP) & (row < (place + 1) * CAP)
        expert = jnp.where(inside, here ^ target, expert)
        level = jnp.where(inside, row - place * CAP, level)
    hits = jnp.zeros((rows, length), F32)
    share = jnp.zeros((rows, length), F32)
    for pick in range(ids.shape[0]):
        named = ids[pick : pick + 1, :] == expert
        hits = hits + jnp.where(named, 1.0, 0.0)
        if weight is not None:
            share = share + jnp.where(named, weight[pick : pick + 1, :], 0.0)
    ranks = dot(hits.astype(BF), earlier)
    chosen = (hits > 0.5) & (jnp.abs(ranks - level.astype(F32)) < 0.5)
    return jnp.where(chosen, 1.0 if weight is None else share, 0.0)


def body(queries, key_rows, value_rows, segments, hidden_entry_rows, expert_ids, route_weight, w_gate, w_up, w_down):
    length = queries.shape[1]
    blocks, sides, cores = lax.axis_size("blk"), lax.axis_size("side"), lax.axis_size("tp")
    plan = Plan(blocks)
    experts = plan.experts
    quarter, ff = w_gate.shape[1], w_gate.shape[2]
    ids, shares = expert_ids[0].T, route_weight[0].T
    picks = ids.shape[0]

    def columns_of(run):
        half = (lax.axis_index("blk") // experts) ^ run
        return pl.ds(pl.multiple_of(half * quarter, quarter), quarter)

    def own_expert():
        return lax.axis_index("blk") % experts

    def over_side(value, offset, low):
        return swapped(value, ("blk", "side"), low * sides + offset)

    first_rows = up_to(experts * CAP, 8)
    wide = hidden_entry_rows.shape[2]

    def before(before_ref):
        i = lax.broadcasted_iota(jnp.int32, (length, length), 0)
        j = lax.broadcasted_iota(jnp.int32, (length, length), 1)
        before_ref[...] = jnp.where(i < j, 1.0, 0.0).astype(BF)

    (earlier,) = call(before, [shaped(length, length)], flops=COST)

    def choose(earlier_ref, ids_ref, x_ref, send_ref, keep_ref):
        chosen = ranked(ids_ref[...], None, earlier_ref[...], first_rows, own_expert(), range(experts)).astype(BF)
        send_ref[...] = dot(chosen, x_ref[:, columns_of(1)]).astype(BF)
        keep_ref[...] = dot(chosen, x_ref[:, columns_of(0)]).astype(BF)

    send, keep = call(
        choose, [shaped(first_rows, quarter)] * 2, earlier, ids, hidden_entry_rows[0], flops=COST
    )

    def share_out(earlier_ref, ids_ref, weight_ref, share_ref):
        share = ranked(ids_ref[...], weight_ref[...], earlier_ref[...], first_rows, own_expert(), plan.ranked)
        share_ref[...] = share.astype(BF)

    (share,) = call(share_out, [shaped(first_rows, length)], earlier, ids, shares)

    def pack(after_ref, key_ref, value_ref, segment_ref, held_ref, segment_here, sems):
        copies = [
            pltpu.make_async_copy(key_ref, held_ref.at[0, pl.ds(0, length)], sems.at[0]),
            pltpu.make_async_copy(value_ref, held_ref.at[0, pl.ds(length, length)], sems.at[1]),
            pltpu.make_async_copy(segment_ref, segment_here, sems.at[2]),
        ]
        for copy in copies:
            copy.start()
        copies[2].wait()
        labels = jnp.broadcast_to(segment_here[...].astype(F32), (16, length))
        held_ref[0, 2 * length : 2 * length + 16, :] = labels.astype(BF)
        copies[0].wait()
        copies[1].wait()

    (held,) = call(
        pack,
        [jax.ShapeDtypeStruct((1, 2 * length + 16, HEAD_DIM), BF)],
        send,
        key_rows[0],
        value_rows[0],
        segments,
        scratch=[pltpu.VMEM((1, length), jnp.int32)],
        semaphores=3,
        far_in=(1, 2, 3),
    )

    def sort(stage, *parts):
        sizes = [up_to(len(pieces) * CAP, 8) for pieces in stage]

        def kernel(*refs):
            values = [ref[...] for ref in refs[: len(parts)]]
            for pieces, size, out in zip(stage, sizes, refs[len(parts) :]):
                out[...] = sorted_rows(pieces, size, values)

        return call(
            kernel,
            [shaped(size, quarter) for size in sizes],
            *parts,
            flops=COST,
        )

    for bit, stage in zip(plan.bits, plan.there):
        received = swapped(send, "blk", bit)
        keep, send = sort(stage, keep, received)
    part_rows = len(plan.sources) // 2 * CAP
    padded = keep.shape[0]
    own = [keep] + [over_side(keep, offset, 0) for offset in range(1, sides)]
    other = [over_side(send, offset, 1) for offset in range(sides)]

    held, _ = lax.optimization_barrier((held, keep))
    order = [0]
    for bit in [1 << i for i in reversed(range(blocks.bit_length() - 1))]:
        held = jnp.concatenate([held, swapped(held, "blk", bit)], axis=0)
        order = order + [place ^ bit for place in order]
    side_rows = 2 * part_rows
    half = sides // 2 * side_rows

    def project(*refs):
        own_refs, other_refs, (gate_ref, up_ref, send_ref, keep_ref) = refs[:sides], refs[sides : 2 * sides], refs[2 * sides :]
        groups = range(part_rows // CAP)
        halves = []
        for first in (0, sides // 2):
            total = 0.0
            for at in range(sides // 2):
                for refs_of, shift in ((own_refs, 0), (other_refs, part_rows)):
                    moves = [(at * side_rows + shift + g * CAP, g * CAP) for g in groups]
                    total = total + dot(mover(half, padded, moves), refs_of[first + at][...])
            halves.append(total.astype(BF))
        low, high = halves
        mine = lax.axis_index("tp") == 0
        away, stay = jnp.where(mine, high, low), jnp.where(mine, low, high)
        both = jnp.concatenate([away, stay], axis=0)
        for at, weight in ((0, gate_ref), (ff, up_ref)):
            terms = dot(both, weight[...])
            send_ref[:, at : at + ff] = terms[:half].astype(BF)
            keep_ref[:, at : at + ff] = terms[half:]

    term_send, term_keep = call(
        project,
        [shaped(half, 2 * ff), shaped(half, 2 * ff, F32)],
        *own,
        *other,
        w_gate[0],
        w_up[0],
        flops=8 * half * quarter * ff,
    )
    term_received = swapped(term_send, "tp", 1)

    moves = []
    for block in range(half // side_rows):
        for place, source in enumerate(plan.sources):
            moves.append((block * side_rows + place * CAP, block * side_rows + plan.sources.index(source ^ experts) * CAP))

    def add_terms(keep_ref, received_ref, sum_ref, send_ref):
        total = keep_ref[...] + received_ref[...].astype(F32)
        sum_ref[...] = total
        send_ref[...] = dot(mover(half, half, moves), total.astype(BF)).astype(BF)

    sums, sums_send = call(
        add_terms,
        [shaped(half, 2 * ff, F32), shaped(half, 2 * ff)],
        term_keep,
        term_received,
        flops=4 * half * half * ff,
    )
    sums_received = swapped(sums_send, "blk", experts)

    heads = queries.shape[2] // HEAD_DIM
    factor = 1.0 / math.sqrt(HEAD_DIM)
    span = blocks * length

    def attend(query_ref, held_ref, segment_ref, out_ref, keys, values, bias):
        here = lax.axis_index("blk")
        i = lax.broadcasted_iota(jnp.int32, (length, length), 0)
        j = lax.broadcasted_iota(jnp.int32, (length, length), 1)
        label_here = jnp.sum(jnp.where(i == j, segment_ref[...].astype(F32), 0.0), axis=1, keepdims=True)
        for place, other_block in enumerate(order):
            at = place * length
            keys[at : at + length, :] = held_ref[place, :length, :]
            values[at : at + length, :] = held_ref[place, length : 2 * length, :]
            label = held_ref[place, 2 * length : 2 * length + 16, :].astype(F32)[:1]
            same = label_here == label
            if other_block == 0:
                seen = same & (j <= i)
            else:
                seen = same & ((here ^ other_block) < here)
            bias[:, at : at + length] = jnp.where(seen, 0.0, -1e30)

        def one_head(head):
            columns = pl.ds(pl.multiple_of(head * HEAD_DIM, HEAD_DIM), HEAD_DIM)
            scores = lax.dot_general(
                query_ref[:, columns], keys[...], (((1,), (1,)), ((), ())), preferred_element_type=F32
            )
            scores = scores + bias[...]
            top = jnp.max(scores, axis=1, keepdims=True)
            weights = jnp.exp((scores - top) * factor)
            totals = jnp.sum(weights, axis=1, keepdims=True)
            out = dot(weights.astype(BF), values[...])
            out_ref[:, columns] = (out / totals).astype(BF)

        if span <= 1024:
            for head in range(heads):
                one_head(head)
        else:
            lax.fori_loop(0, heads, lambda head, _: (one_head(head), 0)[1], 0)

    segments_then, _ = lax.optimization_barrier((segments, sums_send))
    (attended,) = call(
        attend,
        [shaped(length, heads * HEAD_DIM)],
        queries[0],
        held,
        segments_then,
        scratch=[pltpu.VMEM((span, HEAD_DIM), BF)] * 2 + [pltpu.VMEM((length, span), F32)],
        flops=4 * heads * length * span * HEAD_DIM,
        exps=heads * length * span,
    )
    sums_received, attended = lax.optimization_barrier((sums_received, attended))

    def activate(sum_ref, received_ref, hidden_ref):
        gate = sum_ref[:, :ff] + received_ref[:, :ff].astype(F32)
        up = sum_ref[:, ff:] + received_ref[:, ff:].astype(F32)
        hidden_ref[...] = (gate / (1.0 + jnp.exp(-gate)) * up).astype(BF)

    (hidden,) = call(activate, [shaped(half, ff)], sums, sums_received, exps=half * ff)
    hidden_received = swapped(hidden, "tp", 1)

    def project_back(hidden_ref, received_ref, down_ref, *out_refs):
        mine = lax.axis_index("tp") == 0
        here, there = hidden_ref[...], received_ref[...]
        low, high = jnp.where(mine, here, there), jnp.where(mine, there, here)
        groups = range(part_rows // CAP)
        total = 0.0
        for first, rows in ((0, low), (sides // 2, high)):
            moves = []
            for at in range(sides // 2):
                for part in range(2):
                    for g in groups:
                        to = (2 * (first + at) + part) * padded + g * CAP
                        moves.append((to, at * side_rows + part * part_rows + g * CAP))
            total = total + dot(mover(2 * sides * padded, half, moves), rows)
        out = dot(total.astype(BF), down_ref[...])
        for place, out_ref in enumerate(out_refs):
            out_ref[...] = out[place * padded : (place + 1) * padded].astype(out_ref.dtype)

    outs = call(
        project_back,
        [shaped(padded, quarter, BF if place else F32) for place in range(2 * sides)],
        hidden,
        hidden_received,
        w_down[0],
        flops=4 * half * ff * quarter,
    )
    own = [outs[0]] + [over_side(outs[2 * offset], offset, 0) for offset in range(1, sides)]
    other = [over_side(outs[2 * offset + 1], offset, 1) for offset in range(sides)]

    def add_parts(*refs):
        sums = []
        for part in (refs[:sides], refs[sides : 2 * sides]):
            total = part[0][...].astype(F32)
            for ref in part[1:]:
                total = total + ref[...].astype(F32)
            sums.append(total.astype(BF))
        for pieces, out in zip(plan.back[0], refs[2 * sides :]):
            out[...] = sorted_rows(pieces, out.shape[0], sums)

    keep, send = call(
        add_parts,
        [shaped(up_to(len(pieces) * CAP, 8), quarter) for pieces in plan.back[0]],
        *own,
        *other,
        flops=8 * padded * padded * quarter,
    )
    for bit, stage in zip(plan.bits[::-1], plan.back[1:]):
        keep, send = sort(stage, keep, swapped(send, "blk", bit))
    received = swapped(send, "blk", plan.bits[0])

    def mix(run):
        def kernel(share_ref, rows_ref, *refs):
            out_ref, here, sems = refs[-3:]
            piece = quarter // 4
            copies = []
            for at in range(4):
                columns = pl.ds(at * piece, piece)
                here[at] = dot_rows(share_ref[...], rows_ref[:, columns]).astype(BF)
                half_at = ((lax.axis_index("blk") // experts) ^ run) * 4 + at
                target = pl.ds(pl.multiple_of(half_at * piece, piece), piece)
                copies.append(pltpu.make_async_copy(here.at[at], out_ref.at[:, target], sems.at[at]))
                copies[-1].start()
            for copy in copies:
                copy.wait()

        return kernel

    moe_out = None
    for run, rows in ((0, keep), (1, received)):
        ins = [share, rows] + ([] if moe_out is None else [moe_out])
        (moe_out,) = call(
            mix(run),
            [shaped(length, wide)],
            *ins,
            scratch=[pltpu.VMEM((4, length, quarter // 4), BF)],
            semaphores=4,
            far_in=(2,),
            far_out=(0,),
            aliases={2: 0} if run else None,
            flops=4 * length * first_rows * quarter,
        )
    return attended[None], moe_out[None]


def solution(mesh):
    rows = P(("groups", "side"), "blk", "tp")
    placed = (
        rows,
        rows,
        rows,
        P(("groups", "side"), "blk"),
        rows,
        P(("groups", "side"), "blk", None),
        P(("groups", "side"), "blk", None),
        P("blk", "tp", "side"),
        P("blk", "tp", "side"),
        P("blk", "side", "tp"),
    )
    return jax.shard_map(body, mesh=mesh, in_specs=placed, out_specs=(rows, rows), check_vma=False)
```

time: 55.6 us -> 44.4 us (0.80)
  waiting for transfers between devices: 21.7 us -> 14.3 us
  local copies, waits for them, and re-layouts: 4.77 us -> 1.06 us
  Pallas kernels: 10.5 us -> 9.7 us
  starting transfers between devices: 17.6 us -> 18.3 us
    ppermute x11 -> x13, waiting for transfers between devices: 21.7 us -> 14.3 us  [swapped(): return lax.ppermute(value, axis, [(i, i ^ bit) for i in range(count)])]
    unnamed x20, local copies, waits for them, and re-layouts: 4.77 us -> 1.06 us
    pallas_call x12 -> x13, Pallas kernels: 10.5 us -> 9.7 us  [call(): pl.pallas_call(kernel, out_shape=list(outs), in_specs=[HBM if i in far_in...]
    ppermute x11 -> x13, starting transfers between devices: 17.6 us -> 18.3 us  [swapped(): return lax.ppermute(value, axis, [(i, i ^ bit) for i in range(count)])]
  transfers between devices with their start and end apart: 11 -> 13, of which waited for: 8 -> 10; matrix products, arithmetic and copies ran while one was open for 0% -> 0% of each run, Pallas kernels for 12% -> 17%
where the time goes in v2:
time: 44.4 us; the launch traced here: 44.2 us
  starting transfers between devices  18.3 us (41%)
  waiting for transfers between devices  14.3 us (32%)
  Pallas kernels  9.7 us (22%)
  local copies, waits for them, and re-layouts  1.06 us (2%)
  between operations  0.76 us (2%)
    ppermute x13, starting transfers between devices, swapped(): return lax.ppermute(value, axis, [(i, i ^ bit) for i in range(count)])  18.3 us
    ppermute x13, waiting for transfers between devices, swapped(): return lax.ppermute(value, axis, [(i, i ^ bit) for i in range(count)])  14.3 us
    pallas_call x13, Pallas kernels, call(): pl.pallas_call(kernel, out_shape=list(outs), in_specs=[HBM if i in far_in...  9.7 us
    unnamed x20, local copies, waits for them, and re-layouts  1.06 us
  transfers between devices with their start and end apart: 13, of which 10 were waited for; matrix products, arithmetic and copies ran while one was open for 0% of the time, Pallas kernels for 17%

profile of v2, /device:TPU:0, one launch (start us, length us, event | category | flops | bytes accessed | tf_op | source)
XLA Modules:
  0.0 44.2 jit_solution(1484203607240549132)
XLA Ops:
  0.7 0.6 %copy-done.5 = s32[1,128,8]{1,2,0:T(8,128)S(1)} copy-done((s32[1,128,8]{1,2,0:T(8,128)S(1)}, s32[1,128,8]{1,2,0:T(8,128)}, u32[]{:S(2)}) %copy-start.5) | copy-done | bytes 4120
  1.3 0.4 copy-done.8
  1.7 0.3 shard_map.114
  2.0 4.1 %collective-permute-start = (bf16[24,1024]{1,0:T(8,128)(2,1)S(1)}, bf16[24,1024]{1,0:T(8,128)(2,1)S(1)}, u32[]{:S(2)}, u32[]{:S(2)}) collective-permute-start(bf16[24,1024]{1,0:T(8,128)(2,1)S(1)} %get-tuple-element.21.after_ref), channel_id=1, source_target_pairs={{0,8},{4,12},{8,0},{12,4},{1,9},{5,13},{9,1},{13,5},{2,10},{6,14},... | collective-permute-start | bytes 147464 | tf_op jit(solution)/shard_map/ppermute | solution.py:21
  6.1 0.1 shard_map.118
  6.3 2.5 %collective-permute-done.refs_1_ = bf16[24,1024]{1,0:T(8,128)(2,1)S(1)} collective-permute-done((bf16[24,1024]{1,0:T(8,128)(2,1)S(1)}, bf16[24,1024]{1,0:T(8,128)(2,1)S(1)}, u32[]{:S(2)}, u32[]{:S(2)}) %collective-permute-start) | collective-permute-done | bytes 49184 | tf_op jit(solution)/shard_map/ppermute | solution.py:21
  8.7 0.2 shard_map.115
  8.9 2.5 %collective-permute-start.6 = (bf16[1,272,128]{2,1,0:T(8,128)(2,1)S(1)}, bf16[1,272,128]{2,1,0:T(8,128)(2,1)S(1)}, u32[]{:S(2)}, u32[]{:S(2)}) collective-permute-start(bf16[1,272,128]{2,1,0:T(8,128)(2,1)S(1)} %shard_map.118), channel_id=1, source_target_pairs={{0,8},{4,12},{8,0},{12,4},{1,9},{5,13},{9,1},{13,5},{2,10},{6,14},... | collective-permute-start | bytes 208904 | tf_op jit(solution)/shard_map/ppermute | solution.py:21
  11.4 2.9 %collective-permute-start.3 = (bf16[24,1024]{1,0:T(8,128)(2,1)S(1)}, bf16[24,1024]{1,0:T(8,128)(2,1)S(1)}, u32[]{:S(2)}, u32[]{:S(2)}) collective-permute-start(bf16[24,1024]{1,0:T(8,128)(2,1)S(1)} %get-tuple-element.23), channel_id=1, source_target_pairs={{0,6},{2,4},{4,2},{6,0},{8,14},{10,12},{12,10},{14,8},{1,7},{3,5},... | collective-permute-start | bytes 147464 | tf_op jit(solution)/shard_map/ppermute | solution.py:21
  14.4 0.5 %collective-permute-start.1 = (bf16[24,1024]{1,0:T(8,128)(2,1)S(1)}, bf16[24,1024]{1,0:T(8,128)(2,1)S(1)}, u32[]{:S(2)}, u32[]{:S(2)}) collective-permute-start(bf16[24,1024]{1,0:T(8,128)(2,1)S(1)} %get-tuple-element.22.refs_0_), channel_id=1, source_target_pairs={{0,2},{2,0},{4,6},{6,4},{8,10},{10,8},{12,14},{14,12},{1,3},{3,1},... | collective-permute-start | bytes 147464 | tf_op jit(solution)/shard_map/ppermute | solution.py:21
  14.9 2.0 %collective-permute-start.7 = (bf16[2,272,128]{2,1,0:T(8,128)(2,1)S(1)}, bf16[2,272,128]{2,1,0:T(8,128)(2,1)S(1)}, u32[]{:S(2)}, u32[]{:S(2)}) collective-permute-start(bf16[2,272,128]{2,1,0:T(8,128)(2,1)S(1)} %pad_maximum_fusion.1), channel_id=1, source_target_pairs={{0,4},{4,0},{8,12},{12,8},{1,5},{5,1},{9,13},{13,9},{2,6},{6,2},{1... | collective-permute-start | bytes 417800 | tf_op jit(solution)/shard_map/ppermute | solution.py:21
  17.0 1.4 %collective-permute-done.2.refs_2_ = bf16[24,1024]{1,0:T(8,128)(2,1)S(1)} collective-permute-done((bf16[24,1024]{1,0:T(8,128)(2,1)S(1)}, bf16[24,1024]{1,0:T(8,128)(2,1)S(1)}, u32[]{:S(2)}, u32[]{:S(2)}) %collective-permute-start.2) | collective-permute-done | bytes 49184 | tf_op jit(solution)/shard_map/ppermute | solution.py:21
  18.4 0.1 collective-permute-done.1.refs_1_
  18.5 0.9 %shard_map.116 = (bf16[40,1536]{1,0:T(8,128)(2,1)S(1)}, f32[40,1536]{1,0:T(8,128)S(1)}) custom-call(bf16[24,1024]{1,0:T(8,128)(2,1)S(1)} %get-tuple-element.22.refs_0_, bf16[24,1024]{1,0:T(8,128)(2,1)S(1)} %collective-permute-done.1.refs_1_, bf16[24,1024]{1,0:T(8,128)(2,1)S(1)} %collective-permute-done.2.refs_2_, ...), custom_call_target="tpu_custom_call" | custom-call | flops 251658240 | bytes 3710976 | tf_op jit(solution)/shard_map/pallas_call | solution.py:32
  19.4 1.3 %collective-permute-done.4.received_ref = bf16[40,1536]{1,0:T(8,128)(2,1)S(1)} collective-permute-done((bf16[40,1536]{1,0:T(8,128)(2,1)S(1)}, bf16[40,1536]{1,0:T(8,128)(2,1)S(1)}, u32[]{:S(2)}, u32[]{:S(2)}) %collective-permute-start.4) | collective-permute-done | bytes 122912 | tf_op jit(solution)/shard_map/ppermute | solution.py:21
  20.7 0.2 shard_map.117
  20.9 0.8 %collective-permute-start.5 = (bf16[40,1536]{1,0:T(8,128)(2,1)S(1)}, bf16[40,1536]{1,0:T(8,128)(2,1)S(1)}, u32[]{:S(2)}, u32[]{:S(2)}) collective-permute-start(bf16[40,1536]{1,0:T(8,128)(2,1)S(1)} %get-tuple-element.26), channel_id=1, source_target_pairs={{0,8},{4,12},{8,0},{12,4},{1,9},{5,13},{9,1},{13,5},{2,10},{6,14},... | collective-permute-start | bytes 368648 | tf_op jit(solution)/shard_map/ppermute | solution.py:21
  21.7 5.2 %shard_map.119 = bf16[128,2048]{1,0:T(8,128)(2,1)} custom-call(bf16[128,2048]{1,0:T(8,128)(2,1)S(1)} %bitcast.24, bf16[4,272,128]{2,1,0:T(8,128)(2,1)S(1)} %pad_maximum_fusion.held_ref, s32[1,128]{1,0:T(1,128)S(1)} %copy-done.7), custom_call_target="tpu_custom_call" | custom-call | flops 536870912 | bytes 1327616 | tf_op jit(solution)/shard_map/pallas_call | solution.py:32
  26.9 3.0 %collective-permute-done.5.received_ref = bf16[40,1536]{1,0:T(8,128)(2,1)S(1)} collective-permute-done((bf16[40,1536]{1,0:T(8,128)(2,1)S(1)}, bf16[40,1536]{1,0:T(8,128)(2,1)S(1)}, u32[]{:S(2)}, u32[]{:S(2)}) %collective-permute-start.5) | collective-permute-done | bytes 122912 | tf_op jit(solution)/shard_map/ppermute | solution.py:21
  30.1 1.2 %collective-permute-done.8.received_ref = bf16[40,768]{1,0:T(8,128)(2,1)S(1)} collective-permute-done((bf16[40,768]{1,0:T(8,128)(2,1)S(1)}, bf16[40,768]{1,0:T(8,128)(2,1)S(1)}, u32[]{:S(2)}, u32[]{:S(2)}) %collective-permute-start.8) | collective-permute-done | bytes 61472 | tf_op jit(solution)/shard_map/ppermute | solution.py:21
  31.3 0.5 %shard_map.122 = (f32[24,1024]{1,0:T(8,128)S(1)}, bf16[24,1024]{1,0:T(8,128)(2,1)S(1)}, bf16[24,1024]{1,0:T(8,128)(2,1)S(1)}, bf16[24,1024]{1,0:T(8,128)(2,1)S(1)}) custom-call(bf16[40,768]{1,0:T(8,128)(2,1)S(1)} %shard_map.121.hidden_ref, bf16[40,768]{1,0:T(8,128)(2,1)S(1)} %collective-permute-done.8.received_ref, bf16[768,1024]{1,0:T(8,128)(2,1)S(1)} %bitcast.17), custom_call_target="tpu_custom_call" | custom-call | flops 125829120 | bytes 1941504 | tf_op jit(solution)/shard_map/pallas_call | solution.py:32
  31.8 0.6 %collective-permute-start.9 = (bf16[24,1024]{1,0:T(8,128)(2,1)S(1)}, bf16[24,1024]{1,0:T(8,128)(2,1)S(1)}, u32[]{:S(2)}, u32[]{:S(2)}) collective-permute-start(bf16[24,1024]{1,0:T(8,128)(2,1)S(1)} %get-tuple-element.33), channel_id=1, source_target_pairs={{0,2},{2,0},{4,6},{6,4},{8,10},{10,8},{12,14},{14,12},{1,3},{3,1},... | collective-permute-start | bytes 147464 | tf_op jit(solution)/shard_map/ppermute | solution.py:21
  32.4 2.9 %collective-permute-start.11 = (bf16[24,1024]{1,0:T(8,128)(2,1)S(1)}, bf16[24,1024]{1,0:T(8,128)(2,1)S(1)}, u32[]{:S(2)}, u32[]{:S(2)}) collective-permute-start(bf16[24,1024]{1,0:T(8,128)(2,1)S(1)} %get-tuple-element.35), channel_id=1, source_target_pairs={{0,6},{2,4},{4,2},{6,0},{8,14},{10,12},{12,10},{14,8},{1,7},{3,5},... | collective-permute-start | bytes 147464 | tf_op jit(solution)/shard_map/ppermute | solution.py:21
  35.4 0.6 %collective-permute-done.9.refs_1_ = bf16[24,1024]{1,0:T(8,128)(2,1)S(1)} collective-permute-done((bf16[24,1024]{1,0:T(8,128)(2,1)S(1)}, bf16[24,1024]{1,0:T(8,128)(2,1)S(1)}, u32[]{:S(2)}, u32[]{:S(2)}) %collective-permute-start.9) | collective-permute-done | bytes 49184 | tf_op jit(solution)/shard_map/ppermute | solution.py:21
  36.0 0.9 %collective-permute-done.10.refs_2_ = bf16[24,1024]{1,0:T(8,128)(2,1)S(1)} collective-permute-done((bf16[24,1024]{1,0:T(8,128)(2,1)S(1)}, bf16[24,1024]{1,0:T(8,128)(2,1)S(1)}, u32[]{:S(2)}, u32[]{:S(2)}) %collective-permute-start.10) | collective-permute-done | bytes 49184 | tf_op jit(solution)/shard_map/ppermute | solution.py:21
  36.9 1.1 %collective-permute-done.11.refs_3_ = bf16[24,1024]{1,0:T(8,128)(2,1)S(1)} collective-permute-done((bf16[24,1024]{1,0:T(8,128)(2,1)S(1)}, bf16[24,1024]{1,0:T(8,128)(2,1)S(1)}, u32[]{:S(2)}, u32[]{:S(2)}) %collective-permute-start.11) | collective-permute-done | bytes 49184 | tf_op jit(solution)/shard_map/ppermute | solution.py:21
  38.0 0.2 shard_map.123
  38.2 1.7 %collective-permute-start.12 = (bf16[24,1024]{1,0:T(8,128)(2,1)S(1)}, bf16[24,1024]{1,0:T(8,128)(2,1)S(1)}, u32[]{:S(2)}, u32[]{:S(2)}) collective-permute-start(bf16[24,1024]{1,0:T(8,128)(2,1)S(1)} %get-tuple-element.36), channel_id=1, source_target_pairs={{0,8},{4,12},{8,0},{12,4},{1,9},{5,13},{9,1},{13,5},{2,10},{6,14},... | collective-permute-start | bytes 147464 | tf_op jit(solution)/shard_map/ppermute | solution.py:21
  39.9 0.1 shard_map.120.share_ref
  40.1 0.9 %shard_map.124.refs_0_ = bf16[128,2048]{1,0:T(8,128)(2,1)} custom-call(bf16[24,128]{1,0:T(8,128)(2,1)S(1)} %shard_map.120.share_ref, bf16[24,1024]{1,0:T(8,128)(2,1)S(1)} %get-tuple-element.37.rows_ref), custom_call_target="tpu_custom_call" | custom-call | flops 12582912 | bytes 579584 | tf_op jit(solution)/shard_map/pallas_call | solution.py:32
  41.0 2.2 %collective-permute-done.12.rows_ref = bf16[24,1024]{1,0:T(8,128)(2,1)S(1)} collective-permute-done((bf16[24,1024]{1,0:T(8,128)(2,1)S(1)}, bf16[24,1024]{1,0:T(8,128)(2,1)S(1)}, u32[]{:S(2)}, u32[]{:S(2)}) %collective-permute-start.12) | collective-permute-done | bytes 49184 | tf_op jit(solution)/shard_map/ppermute | solution.py:21
  43.2 0.9 %shard_map.125 = bf16[128,2048]{1,0:T(8,128)(2,1)} custom-call(bf16[24,128]{1,0:T(8,128)(2,1)S(1)} %shard_map.120.share_ref, bf16[24,1024]{1,0:T(8,128)(2,1)S(1)} %collective-permute-done.12.rows_ref, bf16[128,2048]{1,0:T(8,128)(2,1)} %shard_map.124.refs_0_), custom_call_target="tpu_custom_call", output_to_operand_aliasing={{}: (2, {})} | custom-call | flops 12582912 | bytes 1103872 | tf_op jit(solution)/shard_map/pallas_call | solution.py:32
  (29 shorter events, 0.4 us)
Async XLA Ops:
  0.6 0.7 %copy-start.5 = (s32[1,128,8]{1,2,0:T(8,128)S(1)}, s32[1,128,8]{1,2,0:T(8,128)}, u32[]{:S(2)}) copy-start(s32[1,128,8]{1,2,0:T(8,128)} %param.15) | copy-start | bytes 12292
  0.6 1.0 %copy-start.8 = (bf16[1,128,2048]{2,1,0:T(8,128)(2,1)S(1)}, bf16[1,128,2048]{2,1,0:T(8,128)(2,1)}, u32[]{:S(2)}) copy-start(bf16[1,128,2048]{2,1,0:T(8,128)(2,1)} %param.14) | copy-start | bytes 1572868
  1.7 4.4 %copy-start.3 = (bf16[1,128,128]{2,1,0:T(8,128)(2,1)S(1)}, bf16[1,128,128]{2,1,0:T(8,128)(2,1)}, u32[]{:S(2)}) copy-start(bf16[1,128,128]{2,1,0:T(8,128)(2,1)} %param.11) | copy-start | bytes 98308
  1.7 4.4 %copy-start.4 = (bf16[1,128,128]{2,1,0:T(8,128)(2,1)S(1)}, bf16[1,128,128]{2,1,0:T(8,128)(2,1)}, u32[]{:S(2)}) copy-start(bf16[1,128,128]{2,1,0:T(8,128)(2,1)} %param.12) | copy-start | bytes 98308
  1.7 4.4 %copy-start.7 = (s32[1,128]{1,0:T(1,128)S(1)}, s32[1,128]{1,0:T(1,128)}, u32[]{:S(2)}) copy-start(s32[1,128]{1,0:T(1,128)} %segment_ref.2) | copy-start | bytes 1540
  2.0 6.7 %collective-permute-start = (bf16[24,1024]{1,0:T(8,128)(2,1)S(1)}, bf16[24,1024]{1,0:T(8,128)(2,1)S(1)}, u32[]{:S(2)}, u32[]{:S(2)}) collective-permute-start(bf16[24,1024]{1,0:T(8,128)(2,1)S(1)} %get-tuple-element.21.after_ref), channel_id=1, source_target_pairs={{0,8},{4,12},{8,0},{12,4},{1,9},{5,13},{9,1},{13,5},{2,10},{6,14},... | collective-permute-start | bytes 147464 | tf_op jit(solution)/shard_map/ppermute | solution.py:21
  8.7 9.8 %copy-start = (bf16[1,1024,768]{2,1,0:T(8,128)(2,1)S(1)}, bf16[1,1024,768]{2,1,0:T(8,128)(2,1)}, u32[]{:S(2)}) copy-start(bf16[1,1024,768]{2,1,0:T(8,128)(2,1)} %param.17) | copy-start | bytes 4718596
  8.7 9.8 %copy-start.1 = (bf16[1,1024,768]{2,1,0:T(8,128)(2,1)S(1)}, bf16[1,1024,768]{2,1,0:T(8,128)(2,1)}, u32[]{:S(2)}) copy-start(bf16[1,1024,768]{2,1,0:T(8,128)(2,1)} %param.18) | copy-start | bytes 4718596
  8.9 6.0 %collective-permute-start.6 = (bf16[1,272,128]{2,1,0:T(8,128)(2,1)S(1)}, bf16[1,272,128]{2,1,0:T(8,128)(2,1)S(1)}, u32[]{:S(2)}, u32[]{:S(2)}) collective-permute-start(bf16[1,272,128]{2,1,0:T(8,128)(2,1)S(1)} %shard_map.118), channel_id=1, source_target_pairs={{0,8},{4,12},{8,0},{12,4},{1,9},{5,13},{9,1},{13,5},{2,10},{6,14},... | collective-permute-start | bytes 208904 | tf_op jit(solution)/shard_map/ppermute | solution.py:21
  11.4 5.5 %collective-permute-start.3 = (bf16[24,1024]{1,0:T(8,128)(2,1)S(1)}, bf16[24,1024]{1,0:T(8,128)(2,1)S(1)}, u32[]{:S(2)}, u32[]{:S(2)}) collective-permute-start(bf16[24,1024]{1,0:T(8,128)(2,1)S(1)} %get-tuple-element.23), channel_id=1, source_target_pairs={{0,6},{2,4},{4,2},{6,0},{8,14},{10,12},{12,10},{14,8},{1,7},{3,5},... | collective-permute-start | bytes 147464 | tf_op jit(solution)/shard_map/ppermute | solution.py:21
  14.3 4.1 %collective-permute-start.2 = (bf16[24,1024]{1,0:T(8,128)(2,1)S(1)}, bf16[24,1024]{1,0:T(8,128)(2,1)S(1)}, u32[]{:S(2)}, u32[]{:S(2)}) collective-permute-start(bf16[24,1024]{1,0:T(8,128)(2,1)S(1)} %get-tuple-element.23), channel_id=1, source_target_pairs={{0,4},{2,6},{4,0},{6,2},{8,12},{10,14},{12,8},{14,10},{1,5},{3,7},... | collective-permute-start | bytes 147464 | tf_op jit(solution)/shard_map/ppermute | solution.py:21
  14.4 4.1 %collective-permute-start.1 = (bf16[24,1024]{1,0:T(8,128)(2,1)S(1)}, bf16[24,1024]{1,0:T(8,128)(2,1)S(1)}, u32[]{:S(2)}, u32[]{:S(2)}) collective-permute-start(bf16[24,1024]{1,0:T(8,128)(2,1)S(1)} %get-tuple-element.22.refs_0_), channel_id=1, source_target_pairs={{0,2},{2,0},{4,6},{6,4},{8,10},{10,8},{12,14},{14,12},{1,3},{3,1},... | collective-permute-start | bytes 147464 | tf_op jit(solution)/shard_map/ppermute | solution.py:21
  14.9 6.8 %collective-permute-start.7 = (bf16[2,272,128]{2,1,0:T(8,128)(2,1)S(1)}, bf16[2,272,128]{2,1,0:T(8,128)(2,1)S(1)}, u32[]{:S(2)}, u32[]{:S(2)}) collective-permute-start(bf16[2,272,128]{2,1,0:T(8,128)(2,1)S(1)} %pad_maximum_fusion.1), channel_id=1, source_target_pairs={{0,4},{4,0},{8,12},{12,8},{1,5},{5,1},{9,13},{13,9},{2,6},{6,2},{1... | collective-permute-start | bytes 417800 | tf_op jit(solution)/shard_map/ppermute | solution.py:21
  18.5 3.2 %copy-start.9 = (bf16[1,128,2048]{2,1,0:T(8,128)(2,1)S(1)}, bf16[1,128,2048]{2,1,0:T(8,128)(2,1)}, u32[]{:S(2)}) copy-start(bf16[1,128,2048]{2,1,0:T(8,128)(2,1)} %param.10) | copy-start | bytes 1572868
  19.3 1.4 %collective-permute-start.4 = (bf16[40,1536]{1,0:T(8,128)(2,1)S(1)}, bf16[40,1536]{1,0:T(8,128)(2,1)S(1)}, u32[]{:S(2)}, u32[]{:S(2)}) collective-permute-start(bf16[40,1536]{1,0:T(8,128)(2,1)S(1)} %get-tuple-element.25), channel_id=1, source_target_pairs={{0,1},{1,0},{2,3},{3,2},{4,5},{5,4},{6,7},{7,6},{8,9},{9,8},{10,11... | collective-permute-start | bytes 368648 | tf_op jit(solution)/shard_map/ppermute | solution.py:21
  20.9 10.4 %copy-start.2 = (bf16[1,768,1024]{2,1,0:T(8,128)(2,1)S(1)}, bf16[1,768,1024]{2,1,0:T(8,128)(2,1)}, u32[]{:S(2)}) copy-start(bf16[1,768,1024]{2,1,0:T(8,128)(2,1)} %param.19) | copy-start | bytes 4718596
  20.9 9.0 %collective-permute-start.5 = (bf16[40,1536]{1,0:T(8,128)(2,1)S(1)}, bf16[40,1536]{1,0:T(8,128)(2,1)S(1)}, u32[]{:S(2)}, u32[]{:S(2)}) collective-permute-start(bf16[40,1536]{1,0:T(8,128)(2,1)S(1)} %get-tuple-element.26), channel_id=1, source_target_pairs={{0,8},{4,12},{8,0},{12,4},{1,9},{5,13},{9,1},{13,5},{2,10},{6,14},... | collective-permute-start | bytes 368648 | tf_op jit(solution)/shard_map/ppermute | solution.py:21
  26.9 13.0 %copy-start.6 = (f32[1,128,8]{1,2,0:T(8,128)S(1)}, f32[1,128,8]{1,2,0:T(8,128)}, u32[]{:S(2)}) copy-start(f32[1,128,8]{1,2,0:T(8,128)} %param.16) | copy-start | bytes 12292
  30.0 1.3 %collective-permute-start.8 = (bf16[40,768]{1,0:T(8,128)(2,1)S(1)}, bf16[40,768]{1,0:T(8,128)(2,1)S(1)}, u32[]{:S(2)}, u32[]{:S(2)}) collective-permute-start(bf16[40,768]{1,0:T(8,128)(2,1)S(1)} %shard_map.121.hidden_ref), channel_id=1, source_target_pairs={{0,1},{1,0},{2,3},{3,2},{4,5},{5,4},{6,7},{7,6},{8,9},{9,8},{10,11... | collective-permute-start | bytes 184328 | tf_op jit(solution)/shard_map/ppermute | solution.py:21
  31.8 4.2 %collective-permute-start.9 = (bf16[24,1024]{1,0:T(8,128)(2,1)S(1)}, bf16[24,1024]{1,0:T(8,128)(2,1)S(1)}, u32[]{:S(2)}, u32[]{:S(2)}) collective-permute-start(bf16[24,1024]{1,0:T(8,128)(2,1)S(1)} %get-tuple-element.33), channel_id=1, source_target_pairs={{0,2},{2,0},{4,6},{6,4},{8,10},{10,8},{12,14},{14,12},{1,3},{3,1},... | collective-permute-start | bytes 147464 | tf_op jit(solution)/shard_map/ppermute | solution.py:21
  32.4 4.4 %collective-permute-start.10 = (bf16[24,1024]{1,0:T(8,128)(2,1)S(1)}, bf16[24,1024]{1,0:T(8,128)(2,1)S(1)}, u32[]{:S(2)}, u32[]{:S(2)}) collective-permute-start(bf16[24,1024]{1,0:T(8,128)(2,1)S(1)} %get-tuple-element.34), channel_id=1, source_target_pairs={{0,4},{2,6},{4,0},{6,2},{8,12},{10,14},{12,8},{14,10},{1,5},{3,7},... | collective-permute-start | bytes 147464 | tf_op jit(solution)/shard_map/ppermute | solution.py:21
  32.4 5.5 %collective-permute-start.11 = (bf16[24,1024]{1,0:T(8,128)(2,1)S(1)}, bf16[24,1024]{1,0:T(8,128)(2,1)S(1)}, u32[]{:S(2)}, u32[]{:S(2)}) collective-permute-start(bf16[24,1024]{1,0:T(8,128)(2,1)S(1)} %get-tuple-element.35), channel_id=1, source_target_pairs={{0,6},{2,4},{4,2},{6,0},{8,14},{10,12},{12,10},{14,8},{1,7},{3,5},... | collective-permute-start | bytes 147464 | tf_op jit(solution)/shard_map/ppermute | solution.py:21
  38.2 5.1 %collective-permute-start.12 = (bf16[24,1024]{1,0:T(8,128)(2,1)S(1)}, bf16[24,1024]{1,0:T(8,128)(2,1)S(1)}, u32[]{:S(2)}, u32[]{:S(2)}) collective-permute-start(bf16[24,1024]{1,0:T(8,128)(2,1)S(1)} %get-tuple-element.36), channel_id=1, source_target_pairs={{0,8},{4,12},{8,0},{12,4},{1,9},{5,13},{9,1},{13,5},{2,10},{6,14},... | collective-permute-start | bytes 147464 | tf_op jit(solution)/shard_map/ppermute | solution.py:21

commit v3 on v2

--- a/solution.py
+++ b/solution.py
@@ -37,7 +37,7 @@
         scratch_shapes=scratch,
         input_output_aliases=aliases or {},
         compiler_params=pltpu.CompilerParams(vmem_limit_bytes=grant or 2 * moved + held + (2 << 20)),
-        cost_estimate=pl.CostEstimate(flops=flops, bytes_accessed=moved, transcendentals=exps),
+        cost_estimate=pl.CostEstimate(flops=flops, bytes_accessed=0 if flops == 0 else moved, transcendentals=exps),
     )(*ins)
 
 
@@ -212,7 +212,7 @@
         )
 
     for bit, stage in zip(plan.bits, plan.there):
-        received = swapped(send, "blk", bit)
+        received, held = lax.optimization_barrier((swapped(send, "blk", bit), held))
         keep, send = sort(stage, keep, received)
     part_rows = len(plan.sources) // 2 * CAP
     padded = keep.shape[0]
@@ -220,15 +220,23 @@
     other = [over_side(send, offset, 1) for offset in range(sides)]
 
     held, _ = lax.optimization_barrier((held, keep))
+    nearby = [1 << i for i in reversed(range(blocks.bit_length() - 1))]
     order = [0]
-    for bit in [1 << i for i in reversed(range(blocks.bit_length() - 1))]:
-        held = jnp.concatenate([held, swapped(held, "blk", bit)], axis=0)
-        order = order + [place ^ bit for place in order]
+    received_held = swapped(held, "blk", nearby[0])
+
+    def join(after_ref, held_ref, received_ref, both_ref):
+        both_ref[: held_ref.shape[0]] = held_ref[...]
+        both_ref[held_ref.shape[0] :] = received_ref[...]
+
+    def joined(after, held, received_held, flops):
+        both = jax.ShapeDtypeStruct((2 * held.shape[0], *held.shape[1:]), BF)
+        return call(join, [both], after, held, received_held, flops=flops)[0]
+
     side_rows = 2 * part_rows
     half = sides // 2 * side_rows
 
     def project(*refs):
-        own_refs, other_refs, (gate_ref, up_ref, send_ref, keep_ref) = refs[:sides], refs[sides : 2 * sides], refs[2 * sides :]
+        own_refs, other_refs, (gate_ref, up_ref, *out_refs) = refs[:sides], refs[sides : 2 * sides], refs[2 * sides :]
         groups = range(part_rows // CAP)
         halves = []
         for first in (0, sides // 2):
@@ -242,92 +250,47 @@
         mine = lax.axis_index("tp") == 0
         away, stay = jnp.where(mine, high, low), jnp.where(mine, low, high)
         both = jnp.concatenate([away, stay], axis=0)
-        for at, weight in ((0, gate_ref), (ff, up_ref)):
+        for weight, send_ref, keep_ref in ((gate_ref, *out_refs[:2]), (up_ref, *out_refs[2:])):
             terms = dot(both, weight[...])
-            send_ref[:, at : at + ff] = terms[:half].astype(BF)
-            keep_ref[:, at : at + ff] = terms[half:]
-
-    term_send, term_keep = call(
+            send_ref[...] = terms[:half].astype(BF)
+            keep_ref[...] = terms[half:]
+
+    gate_send, gate_keep, up_send, up_keep = call(
         project,
-        [shaped(half, 2 * ff), shaped(half, 2 * ff, F32)],
+        [shaped(half, ff), shaped(half, ff, F32)] * 2,
         *own,
         *other,
         w_gate[0],
         w_up[0],
-        flops=8 * half * quarter * ff,
-    )
-    term_received = swapped(term_send, "tp", 1)
+    )
+    gate_received, up_received = swapped(gate_send, "tp", 1), swapped(up_send, "tp", 1)
 
     moves = []
     for block in range(half // side_rows):
         for place, source in enumerate(plan.sources):
             moves.append((block * side_rows + place * CAP, block * side_rows + plan.sources.index(source ^ experts) * CAP))
 
-    def add_terms(keep_ref, received_ref, sum_ref, send_ref):
-        total = keep_ref[...] + received_ref[...].astype(F32)
-        sum_ref[...] = total
-        send_ref[...] = dot(mover(half, half, moves), total.astype(BF)).astype(BF)
+    def add_terms(gate_keep_ref, gate_received_ref, up_keep_ref, up_received_ref, sum_ref, send_ref):
+        for at, keep_ref, received_ref in ((0, gate_keep_ref, gate_received_ref), (ff, up_keep_ref, up_received_ref)):
+            total = keep_ref[...] + received_ref[...].astype(F32)
+            sum_ref[:, at : at + ff] = total
+            send_ref[:, at : at + ff] = dot(mover(half, half, moves), total.astype(BF)).astype(BF)
 
     sums, sums_send = call(
         add_terms,
         [shaped(half, 2 * ff, F32), shaped(half, 2 * ff)],
-        term_keep,
-        term_received,
-        flops=4 * half * half * ff,
+        gate_keep,
+        gate_received,
+        up_keep,
+        up_received,
     )
     sums_received = swapped(sums_send, "blk", experts)
-
-    heads = queries.shape[2] // HEAD_DIM
-    factor = 1.0 / math.sqrt(HEAD_DIM)
-    span = blocks * length
-
-    def attend(query_ref, held_ref, segment_ref, out_ref, keys, values, bias):
-        here = lax.axis_index("blk")
-        i = lax.broadcasted_iota(jnp.int32, (length, length), 0)
-        j = lax.broadcasted_iota(jnp.int32, (length, length), 1)
-        label_here = jnp.sum(jnp.where(i == j, segment_ref[...].astype(F32), 0.0), axis=1, keepdims=True)
-        for place, other_block in enumerate(order):
-            at = place * length
-            keys[at : at + length, :] = held_ref[place, :length, :]
-            values[at : at + length, :] = held_ref[place, length : 2 * length, :]
-            label = held_ref[place, 2 * length : 2 * length + 16, :].astype(F32)[:1]
-            same = label_here == label
-            if other_block == 0:
-                seen = same & (j <= i)
-            else:
-                seen = same & ((here ^ other_block) < here)
-            bias[:, at : at + length] = jnp.where(seen, 0.0, -1e30)
-
-        def one_head(head):
-            columns = pl.ds(pl.multiple_of(head * HEAD_DIM, HEAD_DIM), HEAD_DIM)
-            scores = lax.dot_general(
-                query_ref[:, columns], keys[...], (((1,), (1,)), ((), ())), preferred_element_type=F32
-            )
-            scores = scores + bias[...]
-            top = jnp.max(scores, axis=1, keepdims=True)
-            weights = jnp.exp((scores - top) * factor)
-            totals = jnp.sum(weights, axis=1, keepdims=True)
-            out = dot(weights.astype(BF), values[...])
-            out_ref[:, columns] = (out / totals).astype(BF)
-
-        if span <= 1024:
-            for head in range(heads):
-                one_head(head)
-        else:
-            lax.fori_loop(0, heads, lambda head, _: (one_head(head), 0)[1], 0)
-
-    segments_then, _ = lax.optimization_barrier((segments, sums_send))
-    (attended,) = call(
-        attend,
-        [shaped(length, heads * HEAD_DIM)],
-        queries[0],
-        held,
-        segments_then,
-        scratch=[pltpu.VMEM((span, HEAD_DIM), BF)] * 2 + [pltpu.VMEM((length, span), F32)],
-        flops=4 * heads * length * span * HEAD_DIM,
-        exps=heads * length * span,
-    )
-    sums_received, attended = lax.optimization_barrier((sums_received, attended))
+    for bit in nearby[1:]:
+        held = joined(sums_send, held, received_held, COST)
+        received_held = swapped(held, "blk", bit)
+    held = joined(sums_send, held, received_held, 0)
+    for bit in nearby:
+        order = order + [place ^ bit for place in order]
 
     def activate(sum_ref, received_ref, hidden_ref):
         gate = sum_ref[:, :ff] + received_ref[:, :ff].astype(F32)
@@ -366,6 +329,59 @@
     own = [outs[0]] + [over_side(outs[2 * offset], offset, 0) for offset in range(1, sides)]
     other = [over_side(outs[2 * offset + 1], offset, 1) for offset in range(sides)]
 
+    heads = queries.shape[2] // HEAD_DIM
+    factor = 1.0 / math.sqrt(HEAD_DIM)
+    span = blocks * length
+    batch = math.gcd(heads, max(1, 2048 // span))
+
+    def attend(query_ref, held_ref, segment_ref, out_ref, keys, values, bias):
+        here = lax.axis_index("blk")
+        i = lax.broadcasted_iota(jnp.int32, (length, length), 0)
+        j = lax.broadcasted_iota(jnp.int32, (length, length), 1)
+        label_here = jnp.sum(jnp.where(i == j, segment_ref[...].astype(F32), 0.0), axis=1, keepdims=True)
+        for place, other_block in enumerate(order):
+            at = place * length
+            keys[at : at + length, :] = held_ref[place, :length, :]
+            values[at : at + length, :] = held_ref[place, length : 2 * length, :]
+            label = held_ref[place, 2 * length : 2 * length + 16, :].astype(F32)[:1]
+            same = label_here == label
+            if other_block == 0:
+                seen = same & (j <= i)
+            else:
+                seen = same & ((here ^ other_block) < here)
+            bias[:, at : at + length] = jnp.where(seen, 0.0, -1e30)
+
+        def some_heads(first):
+            columns = [pl.ds(pl.multiple_of((first + h) * HEAD_DIM, HEAD_DIM), HEAD_DIM) for h in range(batch)]
+            query = jnp.concatenate([query_ref[:, c] for c in columns], axis=0)
+            scores = lax.dot_general(query, keys[...], (((1,), (1,)), ((), ())), preferred_element_type=F32)
+            scores = (scores.reshape(batch, length, span) + bias[...][None]).reshape(batch * length, span)
+            top = jnp.max(scores, axis=1, keepdims=True)
+            weights = jnp.exp((scores - top) * factor)
+            totals = jnp.sum(weights, axis=1, keepdims=True)
+            out = (dot(weights.astype(BF), values[...]) / totals).astype(BF)
+            for h, c in enumerate(columns):
+                out_ref[:, c] = out[h * length : (h + 1) * length]
+
+        if span <= 1024:
+            for first in range(0, heads, batch):
+                some_heads(first)
+        else:
+            lax.fori_loop(0, heads // batch, lambda step, _: (some_heads(step * batch), 0)[1], 0)
+
+    segments_then, _ = lax.optimization_barrier((segments, outs[1]))
+    (attended,) = call(
+        attend,
+        [shaped(length, heads * HEAD_DIM)],
+        queries[0],
+        held,
+        segments_then,
+        scratch=[pltpu.VMEM((span, HEAD_DIM), BF)] * 2 + [pltpu.VMEM((length, span), F32)],
+        flops=4 * heads * length * span * HEAD_DIM,
+        exps=heads * length * span,
+    )
+    other[-1], attended = lax.optimization_barrier((other[-1], attended))
+
     def add_parts(*refs):
         sums = []
         for part in (refs[:sides], refs[sides : 2 * sides]):

time: 44.4 us -> 43.1 us (0.971)
  starting transfers between devices: 18.3 us -> 21.2 us
  Pallas kernels: 9.7 us -> 7.16 us
  waiting for transfers between devices: 14.3 us -> 12.7 us
    ppermute x13 -> x14, starting transfers between devices: 18.3 us -> 21.2 us  [swapped(): return lax.ppermute(value, axis, [(i, i ^ bit) for i in range(count)])]
    pallas_call x13 -> x15, Pallas kernels: 9.7 us -> 7.16 us  [call(): pl.pallas_call(kernel, out_shape=list(outs), in_specs=[HBM if i in far_in...]
    ppermute x13 -> x14, waiting for transfers between devices: 14.3 us -> 12.7 us  [swapped(): return lax.ppermute(value, axis, [(i, i ^ bit) for i in range(count)])]
  transfers between devices with their start and end apart: 13 -> 14, of which waited for: 10 -> 9; matrix products, arithmetic and copies ran while one was open for 0% -> 0% of each run, Pallas kernels for 17% -> 12%
where the time goes in v3:
time: 43.1 us; the launch traced here: 42.9 us
  starting transfers between devices  21.2 us (49%)
  waiting for transfers between devices  12.7 us (29%)
  Pallas kernels  7.16 us (17%)
  local copies, waits for them, and re-layouts  1.06 us (2%)
  between operations  0.75 us (2%)
    ppermute x14, starting transfers between devices, swapped(): return lax.ppermute(value, axis, [(i, i ^ bit) for i in range(count)])  21.2 us
    ppermute x14, waiting for transfers between devices, swapped(): return lax.ppermute(value, axis, [(i, i ^ bit) for i in range(count)])  12.7 us
    pallas_call x15, Pallas kernels, call(): pl.pallas_call(kernel, out_shape=list(outs), in_specs=[HBM if i in far_in...  7.16 us
    unnamed x20, local copies, waits for them, and re-layouts  1.06 us
  transfers between devices with their start and end apart: 14, of which 9 were waited for; matrix products, arithmetic and copies ran while one was open for 0% of the time, Pallas kernels for 12%

profile of v3, /device:TPU:0, one launch (start us, length us, event | category | flops | bytes accessed | tf_op | source)
XLA Modules:
  0.0 42.9 jit_solution(9367968674549781105)
XLA Ops:
  0.7 0.6 %copy-done.5 = s32[1,128,8]{1,2,0:T(8,128)S(1)} copy-done((s32[1,128,8]{1,2,0:T(8,128)S(1)}, s32[1,128,8]{1,2,0:T(8,128)}, u32[]{:S(2)}) %copy-start.5) | copy-done | bytes 4120
  1.3 0.4 copy-done.8
  1.7 0.3 shard_map.114
  2.0 4.1 %collective-permute-start = (bf16[24,1024]{1,0:T(8,128)(2,1)S(1)}, bf16[24,1024]{1,0:T(8,128)(2,1)S(1)}, u32[]{:S(2)}, u32[]{:S(2)}) collective-permute-start(bf16[24,1024]{1,0:T(8,128)(2,1)S(1)} %get-tuple-element.25.after_ref), channel_id=1, source_target_pairs={{0,8},{4,12},{8,0},{12,4},{1,9},{5,13},{9,1},{13,5},{2,10},{6,14},... | collective-permute-start | bytes 147464 | tf_op jit(solution)/shard_map/ppermute | solution.py:21
  6.3 2.5 %collective-permute-done.refs_1_ = bf16[24,1024]{1,0:T(8,128)(2,1)S(1)} collective-permute-done((bf16[24,1024]{1,0:T(8,128)(2,1)S(1)}, bf16[24,1024]{1,0:T(8,128)(2,1)S(1)}, u32[]{:S(2)}, u32[]{:S(2)}) %collective-permute-start) | collective-permute-done | bytes 49184 | tf_op jit(solution)/shard_map/ppermute | solution.py:21
  8.7 0.2 shard_map.116
  8.9 2.4 %collective-permute-start.3 = (bf16[24,1024]{1,0:T(8,128)(2,1)S(1)}, bf16[24,1024]{1,0:T(8,128)(2,1)S(1)}, u32[]{:S(2)}, u32[]{:S(2)}) collective-permute-start(bf16[24,1024]{1,0:T(8,128)(2,1)S(1)} %get-tuple-element.28), channel_id=1, source_target_pairs={{0,6},{2,4},{4,2},{6,0},{8,14},{10,12},{12,10},{14,8},{1,7},{3,5},... | collective-permute-start | bytes 147464 | tf_op jit(solution)/shard_map/ppermute | solution.py:21
  11.3 0.9 %collective-permute-start.2 = (bf16[24,1024]{1,0:T(8,128)(2,1)S(1)}, bf16[24,1024]{1,0:T(8,128)(2,1)S(1)}, u32[]{:S(2)}, u32[]{:S(2)}) collective-permute-start(bf16[24,1024]{1,0:T(8,128)(2,1)S(1)} %get-tuple-element.28), channel_id=1, source_target_pairs={{0,4},{2,6},{4,0},{6,2},{8,12},{10,14},{12,8},{14,10},{1,5},{3,7},... | collective-permute-start | bytes 147464 | tf_op jit(solution)/shard_map/ppermute | solution.py:21
  12.2 0.3 collective-permute-start.1
  12.5 2.5 %collective-permute-start.9 = (bf16[1,272,128]{2,1,0:T(8,128)(2,1)S(1)}, bf16[1,272,128]{2,1,0:T(8,128)(2,1)S(1)}, u32[]{:S(2)}, u32[]{:S(2)}) collective-permute-start(bf16[1,272,128]{2,1,0:T(8,128)(2,1)S(1)} %shard_map.115.held_ref), channel_id=1, source_target_pairs={{0,8},{4,12},{8,0},{12,4},{1,9},{5,13},{9,1},{13,5},{2,10},{6,14},... | collective-permute-start | bytes 208904 | tf_op jit(solution)/shard_map/ppermute | solution.py:21
  15.0 0.5 %collective-permute-done.2.refs_2_ = bf16[24,1024]{1,0:T(8,128)(2,1)S(1)} collective-permute-done((bf16[24,1024]{1,0:T(8,128)(2,1)S(1)}, bf16[24,1024]{1,0:T(8,128)(2,1)S(1)}, u32[]{:S(2)}, u32[]{:S(2)}) %collective-permute-start.2) | collective-permute-done | bytes 49184 | tf_op jit(solution)/shard_map/ppermute | solution.py:21
  15.5 0.8 %collective-permute-done.1.refs_1_ = bf16[24,1024]{1,0:T(8,128)(2,1)S(1)} collective-permute-done((bf16[24,1024]{1,0:T(8,128)(2,1)S(1)}, bf16[24,1024]{1,0:T(8,128)(2,1)S(1)}, u32[]{:S(2)}, u32[]{:S(2)}) %collective-permute-start.1) | collective-permute-done | bytes 49184 | tf_op jit(solution)/shard_map/ppermute | solution.py:21
  16.3 0.9 %shard_map.117 = (bf16[40,768]{1,0:T(8,128)(2,1)S(1)}, f32[40,768]{1,0:T(8,128)S(1)}, bf16[40,768]{1,0:T(8,128)(2,1)S(1)}, f32[40,768]{1,0:T(8,128)S(1)}) custom-call(bf16[24,1024]{1,0:T(8,128)(2,1)S(1)} %get-tuple-element.27.refs_0_, bf16[24,1024]{1,0:T(8,128)(2,1)S(1)} %collective-permute-done.1.refs_1_, ...), custom_call_target="tpu_custom_call" | custom-call | tf_op jit(solution)/shard_map/pallas_call | solution.py:32
  17.2 0.5 %collective-permute-start.5 = (bf16[40,768]{1,0:T(8,128)(2,1)S(1)}, bf16[40,768]{1,0:T(8,128)(2,1)S(1)}, u32[]{:S(2)}, u32[]{:S(2)}) collective-permute-start(bf16[40,768]{1,0:T(8,128)(2,1)S(1)} %get-tuple-element.32), channel_id=1, source_target_pairs={{0,1},{1,0},{2,3},{3,2},{4,5},{5,4},{6,7},{7,6},{8,9},{9,8},{10,11... | collective-permute-start | bytes 184328 | tf_op jit(solution)/shard_map/ppermute | solution.py:21
  17.7 0.7 %collective-permute-done.4.gate_received_ref = bf16[40,768]{1,0:T(8,128)(2,1)S(1)} collective-permute-done((bf16[40,768]{1,0:T(8,128)(2,1)S(1)}, bf16[40,768]{1,0:T(8,128)(2,1)S(1)}, u32[]{:S(2)}, u32[]{:S(2)}) %collective-permute-start.4) | collective-permute-done | bytes 61472 | tf_op jit(solution)/shard_map/ppermute | solution.py:21
  18.4 0.2 collective-permute-done.5.up_received_ref
  18.6 0.2 shard_map.118
  18.8 2.3 %collective-permute-start.6 = (bf16[40,1536]{1,0:T(8,128)(2,1)S(1)}, bf16[40,1536]{1,0:T(8,128)(2,1)S(1)}, u32[]{:S(2)}, u32[]{:S(2)}) collective-permute-start(bf16[40,1536]{1,0:T(8,128)(2,1)S(1)} %get-tuple-element.34.after_ref), channel_id=1, source_target_pairs={{0,8},{4,12},{8,0},{12,4},{1,9},{5,13},{9,1},{13,5},{2,10},{6,14},... | collective-permute-start | bytes 368648 | tf_op jit(solution)/shard_map/ppermute | solution.py:21
  21.1 2.0 %collective-permute-start.10 = (bf16[2,272,128]{2,1,0:T(8,128)(2,1)S(1)}, bf16[2,272,128]{2,1,0:T(8,128)(2,1)S(1)}, u32[]{:S(2)}, u32[]{:S(2)}) collective-permute-start(bf16[2,272,128]{2,1,0:T(8,128)(2,1)S(1)} %shard_map.121.held_ref), channel_id=1, source_target_pairs={{0,4},{4,0},{8,12},{12,8},{1,5},{5,1},{9,13},{13,9},{2,6},{6,2},{1... | collective-permute-start | bytes 417800 | tf_op jit(solution)/shard_map/ppermute | solution.py:21
  23.1 4.9 %collective-permute-done.6.received_ref = bf16[40,1536]{1,0:T(8,128)(2,1)S(1)} collective-permute-done((bf16[40,1536]{1,0:T(8,128)(2,1)S(1)}, bf16[40,1536]{1,0:T(8,128)(2,1)S(1)}, u32[]{:S(2)}, u32[]{:S(2)}) %collective-permute-start.6) | collective-permute-done | bytes 122912 | tf_op jit(solution)/shard_map/ppermute | solution.py:21
  28.2 0.4 collective-permute-done.10.received_ref
  28.6 0.8 %collective-permute-done.7.received_ref = bf16[40,768]{1,0:T(8,128)(2,1)S(1)} collective-permute-done((bf16[40,768]{1,0:T(8,128)(2,1)S(1)}, bf16[40,768]{1,0:T(8,128)(2,1)S(1)}, u32[]{:S(2)}, u32[]{:S(2)}) %collective-permute-start.7) | collective-permute-done | bytes 61472 | tf_op jit(solution)/shard_map/ppermute | solution.py:21
  29.4 0.5 %shard_map.120 = (f32[24,1024]{1,0:T(8,128)S(1)}, bf16[24,1024]{1,0:T(8,128)(2,1)S(1)}, bf16[24,1024]{1,0:T(8,128)(2,1)S(1)}, bf16[24,1024]{1,0:T(8,128)(2,1)S(1)}) custom-call(bf16[40,768]{1,0:T(8,128)(2,1)S(1)} %shard_map.119.hidden_ref, bf16[40,768]{1,0:T(8,128)(2,1)S(1)} %collective-permute-done.7.received_ref, bf16[768,1024]{1,0:T(8,128)(2,1)S(1)} %bitcast.17), custom_call_target="tpu_custom_call" | custom-call | flops 125829120 | bytes 1941504 | tf_op jit(solution)/shard_map/pallas_call | solution.py:32
  30.0 0.3 collective-permute-start.12
  30.3 1.7 %collective-permute-start.8 = (bf16[24,1024]{1,0:T(8,128)(2,1)S(1)}, bf16[24,1024]{1,0:T(8,128)(2,1)S(1)}, u32[]{:S(2)}, u32[]{:S(2)}) collective-permute-start(bf16[24,1024]{1,0:T(8,128)(2,1)S(1)} %get-tuple-element.35), channel_id=1, source_target_pairs={{0,6},{2,4},{4,2},{6,0},{8,14},{10,12},{12,10},{14,8},{1,7},{3,5},... | collective-permute-start | bytes 147464 | tf_op jit(solution)/shard_map/ppermute | solution.py:21
  32.0 1.5 %collective-permute-start.11 = (bf16[24,1024]{1,0:T(8,128)(2,1)S(1)}, bf16[24,1024]{1,0:T(8,128)(2,1)S(1)}, u32[]{:S(2)}, u32[]{:S(2)}) collective-permute-start(bf16[24,1024]{1,0:T(8,128)(2,1)S(1)} %get-tuple-element.42), channel_id=1, source_target_pairs={{0,2},{2,0},{4,6},{6,4},{8,10},{10,8},{12,14},{14,12},{1,3},{3,1},... | collective-permute-start | bytes 147464 | tf_op jit(solution)/shard_map/ppermute | solution.py:21
  33.5 2.6 %shard_map.123 = bf16[128,2048]{1,0:T(8,128)(2,1)} custom-call(bf16[128,2048]{1,0:T(8,128)(2,1)S(1)} %bitcast.24, bf16[4,272,128]{2,1,0:T(8,128)(2,1)S(1)} %shard_map.122.held_ref, s32[1,128]{1,0:T(1,128)S(1)} %copy-done.7), custom_call_target="tpu_custom_call" | custom-call | flops 536870912 | bytes 1327616 | tf_op jit(solution)/shard_map/pallas_call | solution.py:32
  36.1 0.2 shard_map.125
  36.4 2.6 %collective-permute-start.13 = (bf16[24,1024]{1,0:T(8,128)(2,1)S(1)}, bf16[24,1024]{1,0:T(8,128)(2,1)S(1)}, u32[]{:S(2)}, u32[]{:S(2)}) collective-permute-start(bf16[24,1024]{1,0:T(8,128)(2,1)S(1)} %get-tuple-element.44), channel_id=1, source_target_pairs={{0,8},{4,12},{8,0},{12,4},{1,9},{5,13},{9,1},{13,5},{2,10},{6,14},... | collective-permute-start | bytes 147464 | tf_op jit(solution)/shard_map/ppermute | solution.py:21
  39.1 0.9 %shard_map.126.refs_0_ = bf16[128,2048]{1,0:T(8,128)(2,1)} custom-call(bf16[24,128]{1,0:T(8,128)(2,1)S(1)} %shard_map.124.share_ref, bf16[24,1024]{1,0:T(8,128)(2,1)S(1)} %get-tuple-element.45.rows_ref), custom_call_target="tpu_custom_call" | custom-call | flops 12582912 | bytes 579584 | tf_op jit(solution)/shard_map/pallas_call | solution.py:32
  40.1 1.9 %collective-permute-done.13.rows_ref = bf16[24,1024]{1,0:T(8,128)(2,1)S(1)} collective-permute-done((bf16[24,1024]{1,0:T(8,128)(2,1)S(1)}, bf16[24,1024]{1,0:T(8,128)(2,1)S(1)}, u32[]{:S(2)}, u32[]{:S(2)}) %collective-permute-start.13) | collective-permute-done | bytes 49184 | tf_op jit(solution)/shard_map/ppermute | solution.py:21
  41.9 0.9 %shard_map.127 = bf16[128,2048]{1,0:T(8,128)(2,1)} custom-call(bf16[24,128]{1,0:T(8,128)(2,1)S(1)} %shard_map.124.share_ref, bf16[24,1024]{1,0:T(8,128)(2,1)S(1)} %collective-permute-done.13.rows_ref, bf16[128,2048]{1,0:T(8,128)(2,1)} %shard_map.126.refs_0_), custom_call_target="tpu_custom_call", output_to_operand_aliasing={{}: (2, {})} | custom-call | flops 12582912 | bytes 1103872 | tf_op jit(solution)/shard_map/pallas_call | solution.py:32
  (31 shorter events, 0.6 us)
Async XLA Ops:
  0.6 0.7 %copy-start.5 = (s32[1,128,8]{1,2,0:T(8,128)S(1)}, s32[1,128,8]{1,2,0:T(8,128)}, u32[]{:S(2)}) copy-start(s32[1,128,8]{1,2,0:T(8,128)} %param.15) | copy-start | bytes 12292
  0.6 1.0 %copy-start.8 = (bf16[1,128,2048]{2,1,0:T(8,128)(2,1)S(1)}, bf16[1,128,2048]{2,1,0:T(8,128)(2,1)}, u32[]{:S(2)}) copy-start(bf16[1,128,2048]{2,1,0:T(8,128)(2,1)} %param.14) | copy-start | bytes 1572868
  1.7 4.4 %copy-start.3 = (bf16[1,128,128]{2,1,0:T(8,128)(2,1)S(1)}, bf16[1,128,128]{2,1,0:T(8,128)(2,1)}, u32[]{:S(2)}) copy-start(bf16[1,128,128]{2,1,0:T(8,128)(2,1)} %param.11) | copy-start | bytes 98308
  1.7 4.4 %copy-start.4 = (bf16[1,128,128]{2,1,0:T(8,128)(2,1)S(1)}, bf16[1,128,128]{2,1,0:T(8,128)(2,1)}, u32[]{:S(2)}) copy-start(bf16[1,128,128]{2,1,0:T(8,128)(2,1)} %param.12) | copy-start | bytes 98308
  1.7 4.4 %copy-start.7 = (s32[1,128]{1,0:T(1,128)S(1)}, s32[1,128]{1,0:T(1,128)}, u32[]{:S(2)}) copy-start(s32[1,128]{1,0:T(1,128)} %segment_ref.2) | copy-start | bytes 1540
  2.0 6.7 %collective-permute-start = (bf16[24,1024]{1,0:T(8,128)(2,1)S(1)}, bf16[24,1024]{1,0:T(8,128)(2,1)S(1)}, u32[]{:S(2)}, u32[]{:S(2)}) collective-permute-start(bf16[24,1024]{1,0:T(8,128)(2,1)S(1)} %get-tuple-element.25.after_ref), channel_id=1, source_target_pairs={{0,8},{4,12},{8,0},{12,4},{1,9},{5,13},{9,1},{13,5},{2,10},{6,14},... | collective-permute-start | bytes 147464 | tf_op jit(solution)/shard_map/ppermute | solution.py:21
  8.7 7.5 %copy-start = (bf16[1,1024,768]{2,1,0:T(8,128)(2,1)S(1)}, bf16[1,1024,768]{2,1,0:T(8,128)(2,1)}, u32[]{:S(2)}) copy-start(bf16[1,1024,768]{2,1,0:T(8,128)(2,1)} %param.17) | copy-start | bytes 4718596
  8.7 7.5 %copy-start.1 = (bf16[1,1024,768]{2,1,0:T(8,128)(2,1)S(1)}, bf16[1,1024,768]{2,1,0:T(8,128)(2,1)}, u32[]{:S(2)}) copy-start(bf16[1,1024,768]{2,1,0:T(8,128)(2,1)} %param.18) | copy-start | bytes 4718596
  8.9 6.0 %collective-permute-start.3 = (bf16[24,1024]{1,0:T(8,128)(2,1)S(1)}, bf16[24,1024]{1,0:T(8,128)(2,1)S(1)}, u32[]{:S(2)}, u32[]{:S(2)}) collective-permute-start(bf16[24,1024]{1,0:T(8,128)(2,1)S(1)} %get-tuple-element.28), channel_id=1, source_target_pairs={{0,6},{2,4},{4,2},{6,0},{8,14},{10,12},{12,10},{14,8},{1,7},{3,5},... | collective-permute-start | bytes 147464 | tf_op jit(solution)/shard_map/ppermute | solution.py:21
  11.3 4.2 %collective-permute-start.2 = (bf16[24,1024]{1,0:T(8,128)(2,1)S(1)}, bf16[24,1024]{1,0:T(8,128)(2,1)S(1)}, u32[]{:S(2)}, u32[]{:S(2)}) collective-permute-start(bf16[24,1024]{1,0:T(8,128)(2,1)S(1)} %get-tuple-element.28), channel_id=1, source_target_pairs={{0,4},{2,6},{4,0},{6,2},{8,12},{10,14},{12,8},{14,10},{1,5},{3,7},... | collective-permute-start | bytes 147464 | tf_op jit(solution)/shard_map/ppermute | solution.py:21
  12.2 4.1 %collective-permute-start.1 = (bf16[24,1024]{1,0:T(8,128)(2,1)S(1)}, bf16[24,1024]{1,0:T(8,128)(2,1)S(1)}, u32[]{:S(2)}, u32[]{:S(2)}) collective-permute-start(bf16[24,1024]{1,0:T(8,128)(2,1)S(1)} %get-tuple-element.27.refs_0_), channel_id=1, source_target_pairs={{0,2},{2,0},{4,6},{6,4},{8,10},{10,8},{12,14},{14,12},{1,3},{3,1},... | collective-permute-start | bytes 147464 | tf_op jit(solution)/shard_map/ppermute | solution.py:21
  12.5 8.6 %collective-permute-start.9 = (bf16[1,272,128]{2,1,0:T(8,128)(2,1)S(1)}, bf16[1,272,128]{2,1,0:T(8,128)(2,1)S(1)}, u32[]{:S(2)}, u32[]{:S(2)}) collective-permute-start(bf16[1,272,128]{2,1,0:T(8,128)(2,1)S(1)} %shard_map.115.held_ref), channel_id=1, source_target_pairs={{0,8},{4,12},{8,0},{12,4},{1,9},{5,13},{9,1},{13,5},{2,10},{6,14},... | collective-permute-start | bytes 208904 | tf_op jit(solution)/shard_map/ppermute | solution.py:21
  17.1 1.3 %collective-permute-start.4 = (bf16[40,768]{1,0:T(8,128)(2,1)S(1)}, bf16[40,768]{1,0:T(8,128)(2,1)S(1)}, u32[]{:S(2)}, u32[]{:S(2)}) collective-permute-start(bf16[40,768]{1,0:T(8,128)(2,1)S(1)} %get-tuple-element.30), channel_id=1, source_target_pairs={{0,1},{1,0},{2,3},{3,2},{4,5},{5,4},{6,7},{7,6},{8,9},{9,8},{10,11... | collective-permute-start | bytes 184328 | tf_op jit(solution)/shard_map/ppermute | solution.py:21
  17.2 1.4 %collective-permute-start.5 = (bf16[40,768]{1,0:T(8,128)(2,1)S(1)}, bf16[40,768]{1,0:T(8,128)(2,1)S(1)}, u32[]{:S(2)}, u32[]{:S(2)}) collective-permute-start(bf16[40,768]{1,0:T(8,128)(2,1)S(1)} %get-tuple-element.32), channel_id=1, source_target_pairs={{0,1},{1,0},{2,3},{3,2},{4,5},{5,4},{6,7},{7,6},{8,9},{9,8},{10,11... | collective-permute-start | bytes 184328 | tf_op jit(solution)/shard_map/ppermute | solution.py:21
  18.8 9.3 %collective-permute-start.6 = (bf16[40,1536]{1,0:T(8,128)(2,1)S(1)}, bf16[40,1536]{1,0:T(8,128)(2,1)S(1)}, u32[]{:S(2)}, u32[]{:S(2)}) collective-permute-start(bf16[40,1536]{1,0:T(8,128)(2,1)S(1)} %get-tuple-element.34.after_ref), channel_id=1, source_target_pairs={{0,8},{4,12},{8,0},{12,4},{1,9},{5,13},{9,1},{13,5},{2,10},{6,14},... | collective-permute-start | bytes 368648 | tf_op jit(solution)/shard_map/ppermute | solution.py:21
  21.1 8.4 %copy-start.2 = (bf16[1,768,1024]{2,1,0:T(8,128)(2,1)S(1)}, bf16[1,768,1024]{2,1,0:T(8,128)(2,1)}, u32[]{:S(2)}) copy-start(bf16[1,768,1024]{2,1,0:T(8,128)(2,1)} %param.19) | copy-start | bytes 4718596
  21.1 12.4 %copy-start.9 = (bf16[1,128,2048]{2,1,0:T(8,128)(2,1)S(1)}, bf16[1,128,2048]{2,1,0:T(8,128)(2,1)}, u32[]{:S(2)}) copy-start(bf16[1,128,2048]{2,1,0:T(8,128)(2,1)} %param.10) | copy-start | bytes 1572868
  21.1 7.5 %collective-permute-start.10 = (bf16[2,272,128]{2,1,0:T(8,128)(2,1)S(1)}, bf16[2,272,128]{2,1,0:T(8,128)(2,1)S(1)}, u32[]{:S(2)}, u32[]{:S(2)}) collective-permute-start(bf16[2,272,128]{2,1,0:T(8,128)(2,1)S(1)} %shard_map.121.held_ref), channel_id=1, source_target_pairs={{0,4},{4,0},{8,12},{12,8},{1,5},{5,1},{9,13},{13,9},{2,6},{6,2},{1... | collective-permute-start | bytes 417800 | tf_op jit(solution)/shard_map/ppermute | solution.py:21
  28.1 1.3 %collective-permute-start.7 = (bf16[40,768]{1,0:T(8,128)(2,1)S(1)}, bf16[40,768]{1,0:T(8,128)(2,1)S(1)}, u32[]{:S(2)}, u32[]{:S(2)}) collective-permute-start(bf16[40,768]{1,0:T(8,128)(2,1)S(1)} %shard_map.119.hidden_ref), channel_id=1, source_target_pairs={{0,1},{1,0},{2,3},{3,2},{4,5},{5,4},{6,7},{7,6},{8,9},{9,8},{10,11... | collective-permute-start | bytes 184328 | tf_op jit(solution)/shard_map/ppermute | solution.py:21
  29.4 9.5 %copy-start.6 = (f32[1,128,8]{1,2,0:T(8,128)S(1)}, f32[1,128,8]{1,2,0:T(8,128)}, u32[]{:S(2)}) copy-start(f32[1,128,8]{1,2,0:T(8,128)} %param.16) | copy-start | bytes 12292
  30.0 6.2 %collective-permute-start.12 = (bf16[24,1024]{1,0:T(8,128)(2,1)S(1)}, bf16[24,1024]{1,0:T(8,128)(2,1)S(1)}, u32[]{:S(2)}, u32[]{:S(2)}) collective-permute-start(bf16[24,1024]{1,0:T(8,128)(2,1)S(1)} %get-tuple-element.38), channel_id=1, source_target_pairs={{0,4},{2,6},{4,0},{6,2},{8,12},{10,14},{12,8},{14,10},{1,5},{3,7},... | collective-permute-start | bytes 147464 | tf_op jit(solution)/shard_map/ppermute | solution.py:21
  30.3 5.8 %collective-permute-start.8 = (bf16[24,1024]{1,0:T(8,128)(2,1)S(1)}, bf16[24,1024]{1,0:T(8,128)(2,1)S(1)}, u32[]{:S(2)}, u32[]{:S(2)}) collective-permute-start(bf16[24,1024]{1,0:T(8,128)(2,1)S(1)} %get-tuple-element.35), channel_id=1, source_target_pairs={{0,6},{2,4},{4,2},{6,0},{8,14},{10,12},{12,10},{14,8},{1,7},{3,5},... | collective-permute-start | bytes 147464 | tf_op jit(solution)/shard_map/ppermute | solution.py:21
  32.0 4.1 %collective-permute-start.11 = (bf16[24,1024]{1,0:T(8,128)(2,1)S(1)}, bf16[24,1024]{1,0:T(8,128)(2,1)S(1)}, u32[]{:S(2)}, u32[]{:S(2)}) collective-permute-start(bf16[24,1024]{1,0:T(8,128)(2,1)S(1)} %get-tuple-element.42), channel_id=1, source_target_pairs={{0,2},{2,0},{4,6},{6,4},{8,10},{10,8},{12,14},{14,12},{1,3},{3,1},... | collective-permute-start | bytes 147464 | tf_op jit(solution)/shard_map/ppermute | solution.py:21
  36.4 5.6 %collective-permute-start.13 = (bf16[24,1024]{1,0:T(8,128)(2,1)S(1)}, bf16[24,1024]{1,0:T(8,128)(2,1)S(1)}, u32[]{:S(2)}, u32[]{:S(2)}) collective-permute-start(bf16[24,1024]{1,0:T(8,128)(2,1)S(1)} %get-tuple-element.44), channel_id=1, source_target_pairs={{0,8},{4,12},{8,0},{12,4},{1,9},{5,13},{9,1},{13,5},{2,10},{6,14},... | collective-permute-start | bytes 147464 | tf_op jit(solution)/shard_map/ppermute | solution.py:21

commit v4 on v3

--- a/solution.py
+++ b/solution.py
@@ -63,28 +63,29 @@
 
 
 class Plan:
-    def __init__(self, count):
-        self.count, self.experts = count, count // 2
+    def __init__(self, count, cuts):
+        self.experts = count // 2
         self.bits = [1 << i for i in reversed(range(1, count.bit_length() - 1))]
-        keep = [(0, d) for d in range(self.experts)]
-        send = [(0, d) for d in range(self.experts, count)]
+        self.first = keep = [(0, d, c) for c in range(cuts) for d in range(self.experts)]
+        send = [(0, d + self.experts, c) for _, d, c in keep]
         self.there = []
         for bit, later in zip(self.bits, self.bits[1:] + [1]):
-            pool = self.pool(keep, send, bit)
-            stage, keep, send = self.split(pool, lambda group: group[1] & later)
+            stage, keep, send = self.split(self.pool(keep, send, bit), lambda group: group[1] & later)
             self.there.append(stage)
-        near = [s for s, _ in keep]
-        self.sources = near + [s ^ 1 for s in near]
+        self.arrived = [(s, c) for s, _, c in keep]
+        near = [s for s, c in self.arrived if c == 0]
+        self.near, self.sources = near, near + [s ^ 1 for s in near]
+        self.leaving = [(s, c) for c in range(cuts) for s in near]
         self.back = []
-        pool = [(i, j, (s, i)) for i in range(2) for j, s in enumerate(near)]
+        pool = [(i, j, (s, i, c)) for i in range(2) for j, (s, c) in enumerate(self.leaving)]
         for bit in reversed(self.bits):
             stage, keep, send = self.split(pool, lambda group: group[0] & bit)
             self.back.append(stage)
             pool = self.pool(keep, send, bit)
-        self.ranked = [d for _, d in keep]
+        self.last = keep
 
     def pool(self, keep, send, bit):
-        received = [(s ^ bit, d ^ bit) for s, d in send]
+        received = [(s ^ bit, d ^ bit, c) for s, d, c in send]
         return [(0, i, g) for i, g in enumerate(keep)] + [(1, i, g) for i, g in enumerate(received)]
 
     def split(self, pool, goes):
@@ -105,12 +106,12 @@
     return total.astype(BF)
 
 
-def ranked(ids, weight, earlier, rows, here, wanted):
+def ranked(ids, weight, earlier, rows, here, groups):
     length = ids.shape[1]
     row = lax.broadcasted_iota(jnp.int32, (rows, 1), 0)
     expert = jnp.full((rows, 1), -1, jnp.int32)
     level = jnp.zeros((rows, 1), jnp.int32)
-    for place, target in enumerate(wanted):
+    for place, (_, target, _) in enumerate(groups):
         inside = (row >= place * CAP) & (row < (place + 1) * CAP)
         expert = jnp.where(inside, here ^ target, expert)
         level = jnp.where(inside, row - place * CAP, level)
@@ -126,18 +127,29 @@
     return jnp.where(chosen, 1.0 if weight is None else share, 0.0)
 
 
+def cut_rows(matrix, groups, cut):
+    row = lax.broadcasted_iota(jnp.int32, (matrix.shape[0], 1), 0)
+    inside = jnp.zeros(row.shape, jnp.bool_)
+    for place, (_, _, c) in enumerate(groups):
+        if c == cut:
+            inside = inside | ((row >= place * CAP) & (row < (place + 1) * CAP))
+    return jnp.where(inside, matrix, 0.0).astype(BF)
+
+
 def body(queries, key_rows, value_rows, segments, hidden_entry_rows, expert_ids, route_weight, w_gate, w_up, w_down):
     length = queries.shape[1]
     blocks, sides, cores = lax.axis_size("blk"), lax.axis_size("side"), lax.axis_size("tp")
-    plan = Plan(blocks)
-    experts = plan.experts
     quarter, ff = w_gate.shape[1], w_gate.shape[2]
+    cuts = next((c for c in (1, 2, 4) if blocks // 2 * CAP * c % 8 == 0 and quarter % (c * 128) == 0), 1)
+    plan = Plan(blocks, cuts)
+    experts, narrow = plan.experts, quarter // cuts
     ids, shares = expert_ids[0].T, route_weight[0].T
     picks = ids.shape[0]
 
-    def columns_of(run):
-        half = (lax.axis_index("blk") // experts) ^ run
-        return pl.ds(pl.multiple_of(half * quarter, quarter), quarter)
+    def columns_of(run, piece, pieces):
+        place = ((lax.axis_index("blk") // experts) ^ run) * pieces + piece
+        width = quarter // pieces
+        return pl.ds(pl.multiple_of(place * width, width), width)
 
     def own_expert():
         return lax.axis_index("blk") % experts
@@ -145,7 +157,7 @@
     def over_side(value, offset, low):
         return swapped(value, ("blk", "side"), low * sides + offset)
 
-    first_rows = up_to(experts * CAP, 8)
+    first_rows = up_to(len(plan.first) * CAP, 8)
     wide = hidden_entry_rows.shape[2]
 
     def before(before_ref):
@@ -155,17 +167,26 @@
 
     (earlier,) = call(before, [shaped(length, length)], flops=COST)
 
-    def choose(earlier_ref, ids_ref, x_ref, send_ref, keep_ref):
-        chosen = ranked(ids_ref[...], None, earlier_ref[...], first_rows, own_expert(), range(experts)).astype(BF)
-        send_ref[...] = dot(chosen, x_ref[:, columns_of(1)]).astype(BF)
-        keep_ref[...] = dot(chosen, x_ref[:, columns_of(0)]).astype(BF)
-
-    send, keep = call(
-        choose, [shaped(first_rows, quarter)] * 2, earlier, ids, hidden_entry_rows[0], flops=COST
-    )
+    def rank(earlier_ref, ids_ref, out_ref):
+        chosen = ranked(ids_ref[...], None, earlier_ref[...], first_rows, own_expert(), plan.first)
+        for cut in range(cuts):
+            out_ref[cut] = cut_rows(chosen, plan.first, cut)
+
+    (chosen,) = call(rank, [jax.ShapeDtypeStruct((cuts, first_rows, length), BF)], earlier, ids)
+
+    def choose(run):
+        def kernel(chosen_ref, x_ref, out_ref):
+            total = 0.0
+            for cut in range(cuts):
+                total = total + dot(chosen_ref[cut], x_ref[:, columns_of(run, cut, cuts)])
+            out_ref[...] = total.astype(BF)
+
+        return call(kernel, [shaped(first_rows, narrow)], chosen, hidden_entry_rows[0], flops=COST)[0]
+
+    send, keep = choose(1), choose(0)
 
     def share_out(earlier_ref, ids_ref, weight_ref, share_ref):
-        share = ranked(ids_ref[...], weight_ref[...], earlier_ref[...], first_rows, own_expert(), plan.ranked)
+        share = ranked(ids_ref[...], weight_ref[...], earlier_ref[...], first_rows, own_expert(), plan.last)
         share_ref[...] = share.astype(BF)
 
     (share,) = call(share_out, [shaped(first_rows, length)], earlier, ids, shares)
@@ -206,7 +227,7 @@
 
         return call(
             kernel,
-            [shaped(size, quarter) for size in sizes],
+            [shaped(size, narrow) for size in sizes],
             *parts,
             flops=COST,
         )
@@ -214,7 +235,7 @@
     for bit, stage in zip(plan.bits, plan.there):
         received, held = lax.optimization_barrier((swapped(send, "blk", bit), held))
         keep, send = sort(stage, keep, received)
-    part_rows = len(plan.sources) // 2 * CAP
+    part_rows = len(plan.near) * CAP
     padded = keep.shape[0]
     own = [keep] + [over_side(keep, offset, 0) for offset in range(1, sides)]
     other = [over_side(send, offset, 1) for offset in range(sides)]
@@ -237,19 +258,27 @@
 
     def project(*refs):
         own_refs, other_refs, (gate_ref, up_ref, *out_refs) = refs[:sides], refs[sides : 2 * sides], refs[2 * sides :]
-        groups = range(part_rows // CAP)
-        halves = []
-        for first in (0, sides // 2):
-            total = 0.0
+        mine = lax.axis_index("tp") == 0
+        away, stay = [], []
+        for refs_of in (own_refs, other_refs):
             for at in range(sides // 2):
-                for refs_of, shift in ((own_refs, 0), (other_refs, part_rows)):
-                    moves = [(at * side_rows + shift + g * CAP, g * CAP) for g in groups]
-                    total = total + dot(mover(half, padded, moves), refs_of[first + at][...])
-            halves.append(total.astype(BF))
-        low, high = halves
-        mine = lax.axis_index("tp") == 0
-        away, stay = jnp.where(mine, high, low), jnp.where(mine, low, high)
-        both = jnp.concatenate([away, stay], axis=0)
+                low, high = refs_of[at][...], refs_of[sides // 2 + at][...]
+                away.append(jnp.where(mine, high, low))
+                stay.append(jnp.where(mine, low, high))
+        stacked = jnp.concatenate([jnp.concatenate(away, axis=0), jnp.concatenate(stay, axis=0)], axis=1)
+        columns = []
+        for cut in range(cuts):
+            moves = []
+            for part in range(2):
+                for at in range(sides // 2):
+                    for place, (source, c) in enumerate(plan.arrived):
+                        if c == cut:
+                            to = at * side_rows + part * part_rows + plan.near.index(source) * CAP
+                            moves.append((to, (part * (sides // 2) + at) * padded + place * CAP))
+            columns.append(dot(mover(half, stacked.shape[0], moves), stacked).astype(BF))
+        both = jnp.concatenate(
+            [jnp.concatenate([c[:, at : at + narrow] for c in columns], axis=1) for at in (0, narrow)], axis=0
+        )
         for weight, send_ref, keep_ref in ((gate_ref, *out_refs[:2]), (up_ref, *out_refs[2:])):
             terms = dot(both, weight[...])
             send_ref[...] = terms[:half].astype(BF)
@@ -304,23 +333,25 @@
         mine = lax.axis_index("tp") == 0
         here, there = hidden_ref[...], received_ref[...]
         low, high = jnp.where(mine, here, there), jnp.where(mine, there, here)
-        groups = range(part_rows // CAP)
+        spaced = up_to(part_rows, 8)
         total = 0.0
         for first, rows in ((0, low), (sides // 2, high)):
             moves = []
             for at in range(sides // 2):
                 for part in range(2):
-                    for g in groups:
-                        to = (2 * (first + at) + part) * padded + g * CAP
-                        moves.append((to, at * side_rows + part * part_rows + g * CAP))
-            total = total + dot(mover(2 * sides * padded, half, moves), rows)
+                    for place in range(part_rows // CAP):
+                        to = (2 * (first + at) + part) * spaced + place * CAP
+                        moves.append((to, at * side_rows + part * part_rows + place * CAP))
+            total = total + dot(mover(2 * sides * spaced, half, moves), rows)
         out = dot(total.astype(BF), down_ref[...])
         for place, out_ref in enumerate(out_refs):
-            out_ref[...] = out[place * padded : (place + 1) * padded].astype(out_ref.dtype)
+            rows = out[place * spaced : place * spaced + part_rows]
+            pieces = [rows[:, cut * narrow : (cut + 1) * narrow] for cut in range(cuts)]
+            out_ref[...] = jnp.concatenate(pieces, axis=0).astype(out_ref.dtype)
 
     outs = call(
         project_back,
-        [shaped(padded, quarter, BF if place else F32) for place in range(2 * sides)],
+        [shaped(padded, narrow, BF if place else F32) for place in range(2 * sides)],
         hidden,
         hidden_received,
         w_down[0],
@@ -394,7 +425,7 @@
 
     keep, send = call(
         add_parts,
-        [shaped(up_to(len(pieces) * CAP, 8), quarter) for pieces in plan.back[0]],
+        [shaped(up_to(len(pieces) * CAP, 8), narrow) for pieces in plan.back[0]],
         *own,
         *other,
         flops=8 * padded * padded * quarter,
@@ -406,14 +437,13 @@
     def mix(run):
         def kernel(share_ref, rows_ref, *refs):
             out_ref, here, sems = refs[-3:]
-            piece = quarter // 4
             copies = []
             for at in range(4):
-                columns = pl.ds(at * piece, piece)
-                here[at] = dot_rows(share_ref[...], rows_ref[:, columns]).astype(BF)
-                half_at = ((lax.axis_index("blk") // experts) ^ run) * 4 + at
-                target = pl.ds(pl.multiple_of(half_at * piece, piece), piece)
-                copies.append(pltpu.make_async_copy(here.at[at], out_ref.at[:, target], sems.at[at]))
+                cut, within = at * cuts // 4, at % (4 // cuts)
+                rows = rows_ref[:, within * (quarter // 4) : (within + 1) * (quarter // 4)]
+                here[at] = dot_rows(cut_rows(share_ref[...].astype(F32), plan.last, cut), rows).astype(BF)
+                target = out_ref.at[:, columns_of(run, at, 4)]
+                copies.append(pltpu.make_async_copy(here.at[at], target, sems.at[at]))
                 copies[-1].start()
             for copy in copies:
                 copy.wait()

time: 43.1 us -> 42.3 us (0.981)
  waiting for transfers between devices: 12.7 us -> 12 us
    ppermute x14, waiting for transfers between devices: 12.7 us -> 12 us  [swapped(): return lax.ppermute(value, axis, [(i, i ^ bit) for i in range(count)])]
    pallas_call x15 -> x17, Pallas kernels: 7.16 us -> 7.12 us  [call(): pl.pallas_call(kernel, out_shape=list(outs), in_specs=[HBM if i in far_in...]
where the time goes in v4:
time: 42.3 us; the launch traced here: 42.1 us
  starting transfers between devices  21.2 us (50%)
  waiting for transfers between devices  12 us (28%)
  Pallas kernels  7.12 us (17%)
  local copies, waits for them, and re-layouts  0.95 us (2%)
  between operations  0.82 us (2%)
    ppermute x14, starting transfers between devices, swapped(): return lax.ppermute(value, axis, [(i, i ^ bit) for i in range(count)])  21.2 us
    ppermute x14, waiting for transfers between devices, swapped(): return lax.ppermute(value, axis, [(i, i ^ bit) for i in range(count)])  12 us
    pallas_call x17, Pallas kernels, call(): pl.pallas_call(kernel, out_shape=list(outs), in_specs=[HBM if i in far_in...  7.12 us
    unnamed x20, local copies, waits for them, and re-layouts  0.95 us
  transfers between devices with their start and end apart: 14, of which 9 were waited for; matrix products, arithmetic and copies ran while one was open for 0% of the time, Pallas kernels for 12%

profile of v4, /device:TPU:0, one launch (start us, length us, event | category | flops | bytes accessed | tf_op | source)
XLA Modules:
  0.0 42.1 jit_solution(14983561757402789118)
XLA Ops:
  0.7 0.6 %copy-done.5 = s32[1,128,8]{1,2,0:T(8,128)S(1)} copy-done((s32[1,128,8]{1,2,0:T(8,128)S(1)}, s32[1,128,8]{1,2,0:T(8,128)}, u32[]{:S(2)}) %copy-start.5) | copy-done | bytes 4120
  1.5 0.2 copy-done.8
  1.9 4.1 %collective-permute-start = (bf16[40,512]{1,0:T(8,128)(2,1)S(1)}, bf16[40,512]{1,0:T(8,128)(2,1)S(1)}, u32[]{:S(2)}, u32[]{:S(2)}) collective-permute-start(bf16[40,512]{1,0:T(8,128)(2,1)S(1)} %shard_map.116.after_ref), channel_id=1, source_target_pairs={{0,8},{4,12},{8,0},{12,4},{1,9},{5,13},{9,1},{13,5},{2,10},{6,14},... | collective-permute-start | bytes 122888 | tf_op jit(solution)/shard_map/ppermute | solution.py:21
  6.3 2.1 %collective-permute-done.refs_1_ = bf16[40,512]{1,0:T(8,128)(2,1)S(1)} collective-permute-done((bf16[40,512]{1,0:T(8,128)(2,1)S(1)}, bf16[40,512]{1,0:T(8,128)(2,1)S(1)}, u32[]{:S(2)}, u32[]{:S(2)}) %collective-permute-start) | collective-permute-done | bytes 40992 | tf_op jit(solution)/shard_map/ppermute | solution.py:21
  8.4 0.2 shard_map.118
  8.6 2.5 %collective-permute-start.3 = (bf16[40,512]{1,0:T(8,128)(2,1)S(1)}, bf16[40,512]{1,0:T(8,128)(2,1)S(1)}, u32[]{:S(2)}, u32[]{:S(2)}) collective-permute-start(bf16[40,512]{1,0:T(8,128)(2,1)S(1)} %get-tuple-element.24), channel_id=1, source_target_pairs={{0,6},{2,4},{4,2},{6,0},{8,14},{10,12},{12,10},{14,8},{1,7},{3,5},... | collective-permute-start | bytes 122888 | tf_op jit(solution)/shard_map/ppermute | solution.py:21
  11.1 0.8 %collective-permute-start.2 = (bf16[40,512]{1,0:T(8,128)(2,1)S(1)}, bf16[40,512]{1,0:T(8,128)(2,1)S(1)}, u32[]{:S(2)}, u32[]{:S(2)}) collective-permute-start(bf16[40,512]{1,0:T(8,128)(2,1)S(1)} %get-tuple-element.24), channel_id=1, source_target_pairs={{0,4},{2,6},{4,0},{6,2},{8,12},{10,14},{12,8},{14,10},{1,5},{3,7},... | collective-permute-start | bytes 122888 | tf_op jit(solution)/shard_map/ppermute | solution.py:21
  11.8 0.3 collective-permute-start.1
  12.1 2.5 %collective-permute-start.9 = (bf16[1,272,128]{2,1,0:T(8,128)(2,1)S(1)}, bf16[1,272,128]{2,1,0:T(8,128)(2,1)S(1)}, u32[]{:S(2)}, u32[]{:S(2)}) collective-permute-start(bf16[1,272,128]{2,1,0:T(8,128)(2,1)S(1)} %shard_map.117.held_ref), channel_id=1, source_target_pairs={{0,8},{4,12},{8,0},{12,4},{1,9},{5,13},{9,1},{13,5},{2,10},{6,14},... | collective-permute-start | bytes 208904 | tf_op jit(solution)/shard_map/ppermute | solution.py:21
  14.7 0.4 collective-permute-done.2.refs_2_
  15.1 0.8 %collective-permute-done.1.refs_1_ = bf16[40,512]{1,0:T(8,128)(2,1)S(1)} collective-permute-done((bf16[40,512]{1,0:T(8,128)(2,1)S(1)}, bf16[40,512]{1,0:T(8,128)(2,1)S(1)}, u32[]{:S(2)}, u32[]{:S(2)}) %collective-permute-start.1) | collective-permute-done | bytes 40992 | tf_op jit(solution)/shard_map/ppermute | solution.py:21
  15.8 0.8 %shard_map.119 = (bf16[40,768]{1,0:T(8,128)(2,1)S(1)}, f32[40,768]{1,0:T(8,128)S(1)}, bf16[40,768]{1,0:T(8,128)(2,1)S(1)}, f32[40,768]{1,0:T(8,128)S(1)}) custom-call(bf16[40,512]{1,0:T(8,128)(2,1)S(1)} %get-tuple-element.23.refs_0_, bf16[40,512]{1,0:T(8,128)(2,1)S(1)} %collective-permute-done.1.refs_1_, bf16[40,512]{1,0:T(8,128)(2,1)S(1)} %collective-permute-done.2.refs_2_, ...), custom_call_target="tpu_custom_call" | custom-call | tf_op jit(solution)/shard_map/pallas_call | solution.py:32
  16.7 0.5 %collective-permute-start.5 = (bf16[40,768]{1,0:T(8,128)(2,1)S(1)}, bf16[40,768]{1,0:T(8,128)(2,1)S(1)}, u32[]{:S(2)}, u32[]{:S(2)}) collective-permute-start(bf16[40,768]{1,0:T(8,128)(2,1)S(1)} %get-tuple-element.28), channel_id=1, source_target_pairs={{0,1},{1,0},{2,3},{3,2},{4,5},{5,4},{6,7},{7,6},{8,9},{9,8},{10,11... | collective-permute-start | bytes 184328 | tf_op jit(solution)/shard_map/ppermute | solution.py:21
  17.2 0.7 %collective-permute-done.4.gate_received_ref = bf16[40,768]{1,0:T(8,128)(2,1)S(1)} collective-permute-done((bf16[40,768]{1,0:T(8,128)(2,1)S(1)}, bf16[40,768]{1,0:T(8,128)(2,1)S(1)}, u32[]{:S(2)}, u32[]{:S(2)}) %collective-permute-start.4) | collective-permute-done | bytes 61472 | tf_op jit(solution)/shard_map/ppermute | solution.py:21
  17.9 0.2 collective-permute-done.5.up_received_ref
  18.1 0.2 shard_map.120
  18.3 2.4 %collective-permute-start.6 = (bf16[40,1536]{1,0:T(8,128)(2,1)S(1)}, bf16[40,1536]{1,0:T(8,128)(2,1)S(1)}, u32[]{:S(2)}, u32[]{:S(2)}) collective-permute-start(bf16[40,1536]{1,0:T(8,128)(2,1)S(1)} %get-tuple-element.30.after_ref), channel_id=1, source_target_pairs={{0,8},{4,12},{8,0},{12,4},{1,9},{5,13},{9,1},{13,5},{2,10},{6,14},... | collective-permute-start | bytes 368648 | tf_op jit(solution)/shard_map/ppermute | solution.py:21
  20.7 1.9 %collective-permute-start.10 = (bf16[2,272,128]{2,1,0:T(8,128)(2,1)S(1)}, bf16[2,272,128]{2,1,0:T(8,128)(2,1)S(1)}, u32[]{:S(2)}, u32[]{:S(2)}) collective-permute-start(bf16[2,272,128]{2,1,0:T(8,128)(2,1)S(1)} %shard_map.123.held_ref), channel_id=1, source_target_pairs={{0,4},{4,0},{8,12},{12,8},{1,5},{5,1},{9,13},{13,9},{2,6},{6,2},{1... | collective-permute-start | bytes 417800 | tf_op jit(solution)/shard_map/ppermute | solution.py:21
  22.6 4.9 %collective-permute-done.6.received_ref = bf16[40,1536]{1,0:T(8,128)(2,1)S(1)} collective-permute-done((bf16[40,1536]{1,0:T(8,128)(2,1)S(1)}, bf16[40,1536]{1,0:T(8,128)(2,1)S(1)}, u32[]{:S(2)}, u32[]{:S(2)}) %collective-permute-start.6) | collective-permute-done | bytes 122912 | tf_op jit(solution)/shard_map/ppermute | solution.py:21
  27.7 0.4 collective-permute-done.10.received_ref
  28.1 0.8 %collective-permute-done.7.received_ref = bf16[40,768]{1,0:T(8,128)(2,1)S(1)} collective-permute-done((bf16[40,768]{1,0:T(8,128)(2,1)S(1)}, bf16[40,768]{1,0:T(8,128)(2,1)S(1)}, u32[]{:S(2)}, u32[]{:S(2)}) %collective-permute-start.7) | collective-permute-done | bytes 61472 | tf_op jit(solution)/shard_map/ppermute | solution.py:21
  28.9 0.5 %shard_map.122 = (f32[40,512]{1,0:T(8,128)S(1)}, bf16[40,512]{1,0:T(8,128)(2,1)S(1)}, bf16[40,512]{1,0:T(8,128)(2,1)S(1)}, bf16[40,512]{1,0:T(8,128)(2,1)S(1)}) custom-call(bf16[40,768]{1,0:T(8,128)(2,1)S(1)} %shard_map.121.hidden_ref, bf16[40,768]{1,0:T(8,128)(2,1)S(1)} %collective-permute-done.7.received_ref, bf16[768,1024]{1,0:T(8,128)(2,1)S(1)} %bitcast.17), custom_call_target="tpu_custom_call" | custom-call | flops 125829120 | bytes 1900544 | tf_op jit(solution)/shard_map/pallas_call | solution.py:32
  29.5 0.4 %collective-permute-start.12 = (bf16[40,512]{1,0:T(8,128)(2,1)S(1)}, bf16[40,512]{1,0:T(8,128)(2,1)S(1)}, u32[]{:S(2)}, u32[]{:S(2)}) collective-permute-start(bf16[40,512]{1,0:T(8,128)(2,1)S(1)} %get-tuple-element.34), channel_id=1, source_target_pairs={{0,4},{2,6},{4,0},{6,2},{8,12},{10,14},{12,8},{14,10},{1,5},{3,7},... | collective-permute-start | bytes 122888 | tf_op jit(solution)/shard_map/ppermute | solution.py:21
  29.9 1.5 %collective-permute-start.8 = (bf16[40,512]{1,0:T(8,128)(2,1)S(1)}, bf16[40,512]{1,0:T(8,128)(2,1)S(1)}, u32[]{:S(2)}, u32[]{:S(2)}) collective-permute-start(bf16[40,512]{1,0:T(8,128)(2,1)S(1)} %get-tuple-element.31), channel_id=1, source_target_pairs={{0,6},{2,4},{4,2},{6,0},{8,14},{10,12},{12,10},{14,8},{1,7},{3,5},... | collective-permute-start | bytes 122888 | tf_op jit(solution)/shard_map/ppermute | solution.py:21
  31.4 1.6 %collective-permute-start.11 = (bf16[40,512]{1,0:T(8,128)(2,1)S(1)}, bf16[40,512]{1,0:T(8,128)(2,1)S(1)}, u32[]{:S(2)}, u32[]{:S(2)}) collective-permute-start(bf16[40,512]{1,0:T(8,128)(2,1)S(1)} %get-tuple-element.38), channel_id=1, source_target_pairs={{0,2},{2,0},{4,6},{6,4},{8,10},{10,8},{12,14},{14,12},{1,3},{3,1},... | collective-permute-start | bytes 122888 | tf_op jit(solution)/shard_map/ppermute | solution.py:21
  33.0 2.6 %shard_map.125 = bf16[128,2048]{1,0:T(8,128)(2,1)} custom-call(bf16[128,2048]{1,0:T(8,128)(2,1)S(1)} %bitcast.25, bf16[4,272,128]{2,1,0:T(8,128)(2,1)S(1)} %shard_map.124.held_ref, s32[1,128]{1,0:T(1,128)S(1)} %copy-done.7), custom_call_target="tpu_custom_call" | custom-call | flops 536870912 | bytes 1327616 | tf_op jit(solution)/shard_map/pallas_call | solution.py:32
  35.6 0.2 shard_map.127
  35.8 2.6 %collective-permute-start.13 = (bf16[40,512]{1,0:T(8,128)(2,1)S(1)}, bf16[40,512]{1,0:T(8,128)(2,1)S(1)}, u32[]{:S(2)}, u32[]{:S(2)}) collective-permute-start(bf16[40,512]{1,0:T(8,128)(2,1)S(1)} %get-tuple-element.40), channel_id=1, source_target_pairs={{0,8},{4,12},{8,0},{12,4},{1,9},{5,13},{9,1},{13,5},{2,10},{6,14},... | collective-permute-start | bytes 122888 | tf_op jit(solution)/shard_map/ppermute | solution.py:21
  38.4 0.2 shard_map.126.share_ref
  38.5 0.9 %shard_map.128.refs_0_ = bf16[128,2048]{1,0:T(8,128)(2,1)} custom-call(bf16[40,128]{1,0:T(8,128)(2,1)S(1)} %shard_map.126.share_ref, bf16[40,512]{1,0:T(8,128)(2,1)S(1)} %get-tuple-element.41.rows_ref), custom_call_target="tpu_custom_call" | custom-call | flops 20971520 | bytes 575488 | tf_op jit(solution)/shard_map/pallas_call | solution.py:32
  39.5 1.7 %collective-permute-done.13.rows_ref = bf16[40,512]{1,0:T(8,128)(2,1)S(1)} collective-permute-done((bf16[40,512]{1,0:T(8,128)(2,1)S(1)}, bf16[40,512]{1,0:T(8,128)(2,1)S(1)}, u32[]{:S(2)}, u32[]{:S(2)}) %collective-permute-start.13) | collective-permute-done | bytes 40992 | tf_op jit(solution)/shard_map/ppermute | solution.py:21
  41.2 0.9 %shard_map.129 = bf16[128,2048]{1,0:T(8,128)(2,1)} custom-call(bf16[40,128]{1,0:T(8,128)(2,1)S(1)} %shard_map.126.share_ref, bf16[40,512]{1,0:T(8,128)(2,1)S(1)} %collective-permute-done.13.rows_ref, bf16[128,2048]{1,0:T(8,128)(2,1)} %shard_map.128.refs_0_), custom_call_target="tpu_custom_call", output_to_operand_aliasing={{}: (2, {})} | custom-call | flops 20971520 | bytes 1099776 | tf_op jit(solution)/shard_map/pallas_call | solution.py:32
  (33 shorter events, 0.9 us)
Async XLA Ops:
  0.6 0.7 %copy-start.5 = (s32[1,128,8]{1,2,0:T(8,128)S(1)}, s32[1,128,8]{1,2,0:T(8,128)}, u32[]{:S(2)}) copy-start(s32[1,128,8]{1,2,0:T(8,128)} %param.15) | copy-start | bytes 12292
  0.6 1.0 %copy-start.8 = (bf16[1,128,2048]{2,1,0:T(8,128)(2,1)S(1)}, bf16[1,128,2048]{2,1,0:T(8,128)(2,1)}, u32[]{:S(2)}) copy-start(bf16[1,128,2048]{2,1,0:T(8,128)(2,1)} %param.14) | copy-start | bytes 1572868
  1.8 4.3 %copy-start.3 = (bf16[1,128,128]{2,1,0:T(8,128)(2,1)S(1)}, bf16[1,128,128]{2,1,0:T(8,128)(2,1)}, u32[]{:S(2)}) copy-start(bf16[1,128,128]{2,1,0:T(8,128)(2,1)} %param.11) | copy-start | bytes 98308
  1.9 4.3 %copy-start.4 = (bf16[1,128,128]{2,1,0:T(8,128)(2,1)S(1)}, bf16[1,128,128]{2,1,0:T(8,128)(2,1)}, u32[]{:S(2)}) copy-start(bf16[1,128,128]{2,1,0:T(8,128)(2,1)} %param.12) | copy-start | bytes 98308
  1.9 4.3 %copy-start.7 = (s32[1,128]{1,0:T(1,128)S(1)}, s32[1,128]{1,0:T(1,128)}, u32[]{:S(2)}) copy-start(s32[1,128]{1,0:T(1,128)} %segment_ref.2) | copy-start | bytes 1540
  1.9 6.5 %collective-permute-start = (bf16[40,512]{1,0:T(8,128)(2,1)S(1)}, bf16[40,512]{1,0:T(8,128)(2,1)S(1)}, u32[]{:S(2)}, u32[]{:S(2)}) collective-permute-start(bf16[40,512]{1,0:T(8,128)(2,1)S(1)} %shard_map.116.after_ref), channel_id=1, source_target_pairs={{0,8},{4,12},{8,0},{12,4},{1,9},{5,13},{9,1},{13,5},{2,10},{6,14},... | collective-permute-start | bytes 122888 | tf_op jit(solution)/shard_map/ppermute | solution.py:21
  6.3 9.5 %copy-start = (bf16[1,1024,768]{2,1,0:T(8,128)(2,1)S(1)}, bf16[1,1024,768]{2,1,0:T(8,128)(2,1)}, u32[]{:S(2)}) copy-start(bf16[1,1024,768]{2,1,0:T(8,128)(2,1)} %param.17) | copy-start | bytes 4718596
  6.3 9.5 %copy-start.1 = (bf16[1,1024,768]{2,1,0:T(8,128)(2,1)S(1)}, bf16[1,1024,768]{2,1,0:T(8,128)(2,1)}, u32[]{:S(2)}) copy-start(bf16[1,1024,768]{2,1,0:T(8,128)(2,1)} %param.18) | copy-start | bytes 4718596
  8.6 6.1 %collective-permute-start.3 = (bf16[40,512]{1,0:T(8,128)(2,1)S(1)}, bf16[40,512]{1,0:T(8,128)(2,1)S(1)}, u32[]{:S(2)}, u32[]{:S(2)}) collective-permute-start(bf16[40,512]{1,0:T(8,128)(2,1)S(1)} %get-tuple-element.24), channel_id=1, source_target_pairs={{0,6},{2,4},{4,2},{6,0},{8,14},{10,12},{12,10},{14,8},{1,7},{3,5},... | collective-permute-start | bytes 122888 | tf_op jit(solution)/shard_map/ppermute | solution.py:21
  11.1 4.0 %collective-permute-start.2 = (bf16[40,512]{1,0:T(8,128)(2,1)S(1)}, bf16[40,512]{1,0:T(8,128)(2,1)S(1)}, u32[]{:S(2)}, u32[]{:S(2)}) collective-permute-start(bf16[40,512]{1,0:T(8,128)(2,1)S(1)} %get-tuple-element.24), channel_id=1, source_target_pairs={{0,4},{2,6},{4,0},{6,2},{8,12},{10,14},{12,8},{14,10},{1,5},{3,7},... | collective-permute-start | bytes 122888 | tf_op jit(solution)/shard_map/ppermute | solution.py:21
  11.8 4.0 %collective-permute-start.1 = (bf16[40,512]{1,0:T(8,128)(2,1)S(1)}, bf16[40,512]{1,0:T(8,128)(2,1)S(1)}, u32[]{:S(2)}, u32[]{:S(2)}) collective-permute-start(bf16[40,512]{1,0:T(8,128)(2,1)S(1)} %get-tuple-element.23.refs_0_), channel_id=1, source_target_pairs={{0,2},{2,0},{4,6},{6,4},{8,10},{10,8},{12,14},{14,12},{1,3},{3,1},... | collective-permute-start | bytes 122888 | tf_op jit(solution)/shard_map/ppermute | solution.py:21
  12.1 8.5 %collective-permute-start.9 = (bf16[1,272,128]{2,1,0:T(8,128)(2,1)S(1)}, bf16[1,272,128]{2,1,0:T(8,128)(2,1)S(1)}, u32[]{:S(2)}, u32[]{:S(2)}) collective-permute-start(bf16[1,272,128]{2,1,0:T(8,128)(2,1)S(1)} %shard_map.117.held_ref), channel_id=1, source_target_pairs={{0,8},{4,12},{8,0},{12,4},{1,9},{5,13},{9,1},{13,5},{2,10},{6,14},... | collective-permute-start | bytes 208904 | tf_op jit(solution)/shard_map/ppermute | solution.py:21
  16.6 1.3 %collective-permute-start.4 = (bf16[40,768]{1,0:T(8,128)(2,1)S(1)}, bf16[40,768]{1,0:T(8,128)(2,1)S(1)}, u32[]{:S(2)}, u32[]{:S(2)}) collective-permute-start(bf16[40,768]{1,0:T(8,128)(2,1)S(1)} %get-tuple-element.26), channel_id=1, source_target_pairs={{0,1},{1,0},{2,3},{3,2},{4,5},{5,4},{6,7},{7,6},{8,9},{9,8},{10,11... | collective-permute-start | bytes 184328 | tf_op jit(solution)/shard_map/ppermute | solution.py:21
  16.7 1.4 %collective-permute-start.5 = (bf16[40,768]{1,0:T(8,128)(2,1)S(1)}, bf16[40,768]{1,0:T(8,128)(2,1)S(1)}, u32[]{:S(2)}, u32[]{:S(2)}) collective-permute-start(bf16[40,768]{1,0:T(8,128)(2,1)S(1)} %get-tuple-element.28), channel_id=1, source_target_pairs={{0,1},{1,0},{2,3},{3,2},{4,5},{5,4},{6,7},{7,6},{8,9},{9,8},{10,11... | collective-permute-start | bytes 184328 | tf_op jit(solution)/shard_map/ppermute | solution.py:21
  18.3 9.3 %collective-permute-start.6 = (bf16[40,1536]{1,0:T(8,128)(2,1)S(1)}, bf16[40,1536]{1,0:T(8,128)(2,1)S(1)}, u32[]{:S(2)}, u32[]{:S(2)}) collective-permute-start(bf16[40,1536]{1,0:T(8,128)(2,1)S(1)} %get-tuple-element.30.after_ref), channel_id=1, source_target_pairs={{0,8},{4,12},{8,0},{12,4},{1,9},{5,13},{9,1},{13,5},{2,10},{6,14},... | collective-permute-start | bytes 368648 | tf_op jit(solution)/shard_map/ppermute | solution.py:21
  20.6 8.3 %copy-start.2 = (bf16[1,768,1024]{2,1,0:T(8,128)(2,1)S(1)}, bf16[1,768,1024]{2,1,0:T(8,128)(2,1)}, u32[]{:S(2)}) copy-start(bf16[1,768,1024]{2,1,0:T(8,128)(2,1)} %param.19) | copy-start | bytes 4718596
  20.7 12.4 %copy-start.9 = (bf16[1,128,2048]{2,1,0:T(8,128)(2,1)S(1)}, bf16[1,128,2048]{2,1,0:T(8,128)(2,1)}, u32[]{:S(2)}) copy-start(bf16[1,128,2048]{2,1,0:T(8,128)(2,1)} %param.10) | copy-start | bytes 1572868
  20.7 7.4 %collective-permute-start.10 = (bf16[2,272,128]{2,1,0:T(8,128)(2,1)S(1)}, bf16[2,272,128]{2,1,0:T(8,128)(2,1)S(1)}, u32[]{:S(2)}, u32[]{:S(2)}) collective-permute-start(bf16[2,272,128]{2,1,0:T(8,128)(2,1)S(1)} %shard_map.123.held_ref), channel_id=1, source_target_pairs={{0,4},{4,0},{8,12},{12,8},{1,5},{5,1},{9,13},{13,9},{2,6},{6,2},{1... | collective-permute-start | bytes 417800 | tf_op jit(solution)/shard_map/ppermute | solution.py:21
  27.6 1.3 %collective-permute-start.7 = (bf16[40,768]{1,0:T(8,128)(2,1)S(1)}, bf16[40,768]{1,0:T(8,128)(2,1)S(1)}, u32[]{:S(2)}, u32[]{:S(2)}) collective-permute-start(bf16[40,768]{1,0:T(8,128)(2,1)S(1)} %shard_map.121.hidden_ref), channel_id=1, source_target_pairs={{0,1},{1,0},{2,3},{3,2},{4,5},{5,4},{6,7},{7,6},{8,9},{9,8},{10,11... | collective-permute-start | bytes 184328 | tf_op jit(solution)/shard_map/ppermute | solution.py:21
  28.9 9.4 %copy-start.6 = (f32[1,128,8]{1,2,0:T(8,128)S(1)}, f32[1,128,8]{1,2,0:T(8,128)}, u32[]{:S(2)}) copy-start(f32[1,128,8]{1,2,0:T(8,128)} %param.16) | copy-start | bytes 12292
  29.5 6.1 %collective-permute-start.12 = (bf16[40,512]{1,0:T(8,128)(2,1)S(1)}, bf16[40,512]{1,0:T(8,128)(2,1)S(1)}, u32[]{:S(2)}, u32[]{:S(2)}) collective-permute-start(bf16[40,512]{1,0:T(8,128)(2,1)S(1)} %get-tuple-element.34), channel_id=1, source_target_pairs={{0,4},{2,6},{4,0},{6,2},{8,12},{10,14},{12,8},{14,10},{1,5},{3,7},... | collective-permute-start | bytes 122888 | tf_op jit(solution)/shard_map/ppermute | solution.py:21
  29.9 5.7 %collective-permute-start.8 = (bf16[40,512]{1,0:T(8,128)(2,1)S(1)}, bf16[40,512]{1,0:T(8,128)(2,1)S(1)}, u32[]{:S(2)}, u32[]{:S(2)}) collective-permute-start(bf16[40,512]{1,0:T(8,128)(2,1)S(1)} %get-tuple-element.31), channel_id=1, source_target_pairs={{0,6},{2,4},{4,2},{6,0},{8,14},{10,12},{12,10},{14,8},{1,7},{3,5},... | collective-permute-start | bytes 122888 | tf_op jit(solution)/shard_map/ppermute | solution.py:21
  31.4 4.2 %collective-permute-start.11 = (bf16[40,512]{1,0:T(8,128)(2,1)S(1)}, bf16[40,512]{1,0:T(8,128)(2,1)S(1)}, u32[]{:S(2)}, u32[]{:S(2)}) collective-permute-start(bf16[40,512]{1,0:T(8,128)(2,1)S(1)} %get-tuple-element.38), channel_id=1, source_target_pairs={{0,2},{2,0},{4,6},{6,4},{8,10},{10,8},{12,14},{14,12},{1,3},{3,1},... | collective-permute-start | bytes 122888 | tf_op jit(solution)/shard_map/ppermute | solution.py:21
  35.8 5.4 %collective-permute-start.13 = (bf16[40,512]{1,0:T(8,128)(2,1)S(1)}, bf16[40,512]{1,0:T(8,128)(2,1)S(1)}, u32[]{:S(2)}, u32[]{:S(2)}) collective-permute-start(bf16[40,512]{1,0:T(8,128)(2,1)S(1)} %get-tuple-element.40), channel_id=1, source_target_pairs={{0,8},{4,12},{8,0},{12,4},{1,9},{5,13},{9,1},{13,5},{2,10},{6,14},... | collective-permute-start | bytes 122888 | tf_op jit(solution)/shard_map/ppermute | solution.py:21

commit v5 on v4

--- a/solution.py
+++ b/solution.py
@@ -49,17 +49,21 @@
     return jnp.dot(a, b, preferred_element_type=F32)
 
 
-def dot_rows(a, b):
-    return lax.dot_general(a, b, (((0,), (0,)), ((), ())), preferred_element_type=F32)
-
-
-def mover(rows_out, rows_in, pieces):
-    i = lax.broadcasted_iota(jnp.int32, (rows_out, rows_in), 0)
-    j = lax.broadcasted_iota(jnp.int32, (rows_out, rows_in), 1)
-    hit = jnp.zeros((rows_out, rows_in), jnp.bool_)
-    for to, start in pieces:
-        hit = hit | ((j - i == start - to) & (i >= to) & (i < to + CAP))
-    return jnp.where(hit, 1.0, 0.0).astype(BF)
+def arranged(parts, pieces, rows):
+    runs = []
+    for which, to, start in sorted(pieces, key=lambda piece: piece[1]):
+        if runs and runs[-1][0] == which and runs[-1][1] + runs[-1][3] == to and runs[-1][2] + runs[-1][3] == start:
+            runs[-1][3] += CAP
+        else:
+            runs.append([which, to, start, CAP])
+    out, at, width = [], 0, parts[0].shape[1]
+    for which, to, start, count in runs + [[None, rows, 0, 0]]:
+        if to > at:
+            out.append(jnp.zeros((to - at, width), F32))
+        if count:
+            out.append(parts[which][start : start + count])
+        at = to + count
+    return jnp.concatenate(out, axis=0) if len(out) > 1 else out[0]
 
 
 class Plan:
@@ -97,15 +101,6 @@
         return stage, groups[0], groups[1]
 
 
-def sorted_rows(pieces, size, parts):
-    total = 0.0
-    for which, part in enumerate(parts):
-        moves = [(to, start) for w, to, start in pieces if w == which]
-        if moves:
-            total = total + dot(mover(size, part.shape[0], moves), part)
-    return total.astype(BF)
-
-
 def ranked(ids, weight, earlier, rows, here, groups):
     length = ids.shape[1]
     row = lax.broadcasted_iota(jnp.int32, (rows, 1), 0)
@@ -187,9 +182,10 @@
 
     def share_out(earlier_ref, ids_ref, weight_ref, share_ref):
         share = ranked(ids_ref[...], weight_ref[...], earlier_ref[...], first_rows, own_expert(), plan.last)
-        share_ref[...] = share.astype(BF)
-
-    (share,) = call(share_out, [shaped(first_rows, length)], earlier, ids, shares)
+        for cut in range(cuts):
+            share_ref[cut] = cut_rows(share, plan.last, cut).astype(F32).T.astype(BF)
+
+    (share,) = call(share_out, [jax.ShapeDtypeStruct((cuts, length, first_rows), BF)], earlier, ids, shares)
 
     def pack(after_ref, key_ref, value_ref, segment_ref, held_ref, segment_here, sems):
         copies = [
@@ -221,9 +217,9 @@
         sizes = [up_to(len(pieces) * CAP, 8) for pieces in stage]
 
         def kernel(*refs):
-            values = [ref[...] for ref in refs[: len(parts)]]
+            values = [ref[...].astype(F32) for ref in refs[: len(parts)]]
             for pieces, size, out in zip(stage, sizes, refs[len(parts) :]):
-                out[...] = sorted_rows(pieces, size, values)
+                out[...] = arranged(values, pieces, size).astype(BF)
 
         return call(
             kernel,
@@ -254,7 +250,13 @@
         return call(join, [both], after, held, received_held, flops=flops)[0]
 
     side_rows = 2 * part_rows
+
     half = sides // 2 * side_rows
+
+    def by_source(build):
+        here = build(lambda source: plan.near.index(source) * CAP)
+        there = build(lambda source: plan.near.index(source ^ experts) * CAP)
+        return jnp.where(lax.axis_index("blk") >= experts, there, here)
 
     def project(*refs):
         own_refs, other_refs, (gate_ref, up_ref, *out_refs) = refs[:sides], refs[sides : 2 * sides], refs[2 * sides :]
@@ -262,23 +264,27 @@
         away, stay = [], []
         for refs_of in (own_refs, other_refs):
             for at in range(sides // 2):
-                low, high = refs_of[at][...], refs_of[sides // 2 + at][...]
+                low, high = refs_of[at][...].astype(F32), refs_of[sides // 2 + at][...].astype(F32)
                 away.append(jnp.where(mine, high, low))
                 stay.append(jnp.where(mine, low, high))
-        stacked = jnp.concatenate([jnp.concatenate(away, axis=0), jnp.concatenate(stay, axis=0)], axis=1)
-        columns = []
-        for cut in range(cuts):
-            moves = []
+
+        def build(row_of, rows, cut):
+            pieces = []
             for part in range(2):
                 for at in range(sides // 2):
                     for place, (source, c) in enumerate(plan.arrived):
                         if c == cut:
-                            to = at * side_rows + part * part_rows + plan.near.index(source) * CAP
-                            moves.append((to, (part * (sides // 2) + at) * padded + place * CAP))
-            columns.append(dot(mover(half, stacked.shape[0], moves), stacked).astype(BF))
+                            to = at * side_rows + part * part_rows + row_of(source)
+                            pieces.append((part * (sides // 2) + at, to, place * CAP))
+            return arranged(rows, pieces, half)
+
         both = jnp.concatenate(
-            [jnp.concatenate([c[:, at : at + narrow] for c in columns], axis=1) for at in (0, narrow)], axis=0
-        )
+            [
+                jnp.concatenate([by_source(lambda row_of: build(row_of, rows, cut)) for cut in range(cuts)], axis=1)
+                for rows in (away, stay)
+            ],
+            axis=0,
+        ).astype(BF)
         for weight, send_ref, keep_ref in ((gate_ref, *out_refs[:2]), (up_ref, *out_refs[2:])):
             terms = dot(both, weight[...])
             send_ref[...] = terms[:half].astype(BF)
@@ -294,16 +300,11 @@
     )
     gate_received, up_received = swapped(gate_send, "tp", 1), swapped(up_send, "tp", 1)
 
-    moves = []
-    for block in range(half // side_rows):
-        for place, source in enumerate(plan.sources):
-            moves.append((block * side_rows + place * CAP, block * side_rows + plan.sources.index(source ^ experts) * CAP))
-
     def add_terms(gate_keep_ref, gate_received_ref, up_keep_ref, up_received_ref, sum_ref, send_ref):
         for at, keep_ref, received_ref in ((0, gate_keep_ref, gate_received_ref), (ff, up_keep_ref, up_received_ref)):
             total = keep_ref[...] + received_ref[...].astype(F32)
             sum_ref[:, at : at + ff] = total
-            send_ref[:, at : at + ff] = dot(mover(half, half, moves), total.astype(BF)).astype(BF)
+            send_ref[:, at : at + ff] = total.astype(BF)
 
     sums, sums_send = call(
         add_terms,
@@ -331,18 +332,21 @@
 
     def project_back(hidden_ref, received_ref, down_ref, *out_refs):
         mine = lax.axis_index("tp") == 0
-        here, there = hidden_ref[...], received_ref[...]
-        low, high = jnp.where(mine, here, there), jnp.where(mine, there, here)
+        here, there = hidden_ref[...].astype(F32), received_ref[...].astype(F32)
+        ordered = [jnp.where(mine, here, there), jnp.where(mine, there, here)]
         spaced = up_to(part_rows, 8)
-        total = 0.0
-        for first, rows in ((0, low), (sides // 2, high)):
-            moves = []
-            for at in range(sides // 2):
+
+        def build(row_of):
+            pieces = []
+            for at in range(sides):
                 for part in range(2):
-                    for place in range(part_rows // CAP):
-                        to = (2 * (first + at) + part) * spaced + place * CAP
-                        moves.append((to, at * side_rows + part * part_rows + place * CAP))
-            total = total + dot(mover(2 * sides * spaced, half, moves), rows)
+                    for place, source in enumerate(plan.near):
+                        to = (2 * at + part) * spaced + place * CAP
+                        start = at % (sides // 2) * side_rows + part * part_rows + row_of(source)
+                        pieces.append((at // (sides // 2), to, start))
+            return arranged(ordered, pieces, 2 * sides * spaced)
+
+        total = by_source(build)
         out = dot(total.astype(BF), down_ref[...])
         for place, out_ref in enumerate(out_refs):
             rows = out[place * spaced : place * spaced + part_rows]
@@ -419,9 +423,9 @@
             total = part[0][...].astype(F32)
             for ref in part[1:]:
                 total = total + ref[...].astype(F32)
-            sums.append(total.astype(BF))
+            sums.append(total)
         for pieces, out in zip(plan.back[0], refs[2 * sides :]):
-            out[...] = sorted_rows(pieces, out.shape[0], sums)
+            out[...] = arranged(sums, pieces, out.shape[0]).astype(BF)
 
     keep, send = call(
         add_parts,
@@ -441,7 +445,7 @@
             for at in range(4):
                 cut, within = at * cuts // 4, at % (4 // cuts)
                 rows = rows_ref[:, within * (quarter // 4) : (within + 1) * (quarter // 4)]
-                here[at] = dot_rows(cut_rows(share_ref[...].astype(F32), plan.last, cut), rows).astype(BF)
+                here[at] = dot(share_ref[cut], rows).astype(BF)
                 target = out_ref.at[:, columns_of(run, at, 4)]
                 copies.append(pltpu.make_async_copy(here.at[at], target, sems.at[at]))
                 copies[-1].start()

time: 42.3 us -> 41.6 us (0.983)
  Pallas kernels: 7.12 us -> 6.44 us
    pallas_call x17, Pallas kernels: 7.12 us -> 6.44 us  [call(): pl.pallas_call(kernel, out_shape=list(outs), in_specs=[HBM if i in far_in...]
where the time goes in v5:
time: 41.6 us; the launch traced here: 41.4 us
  starting transfers between devices  21.2 us (51%)
  waiting for transfers between devices  12 us (29%)
  Pallas kernels  6.44 us (15%)
  local copies, waits for them, and re-layouts  0.95 us (2%)
  between operations  0.82 us (2%)
    ppermute x14, starting transfers between devices, swapped(): return lax.ppermute(value, axis, [(i, i ^ bit) for i in range(count)])  21.2 us
    ppermute x14, waiting for transfers between devices, swapped(): return lax.ppermute(value, axis, [(i, i ^ bit) for i in range(count)])  12 us
    pallas_call x17, Pallas kernels, call(): pl.pallas_call(kernel, out_shape=list(outs), in_specs=[HBM if i in far_in...  6.44 us
    unnamed x20, local copies, waits for them, and re-layouts  0.95 us
  transfers between devices with their start and end apart: 14, of which 9 were waited for; matrix products, arithmetic and copies ran while one was open for 0% of the time, Pallas kernels for 12%

profile of v5, /device:TPU:0, one launch (start us, length us, event | category | flops | bytes accessed | tf_op | source)
XLA Modules:
  0.0 41.4 jit_solution(18129617056783968085)
XLA Ops:
  0.7 0.6 %copy-done.5 = s32[1,128,8]{1,2,0:T(8,128)S(1)} copy-done((s32[1,128,8]{1,2,0:T(8,128)S(1)}, s32[1,128,8]{1,2,0:T(8,128)}, u32[]{:S(2)}) %copy-start.5) | copy-done | bytes 4120
  1.3 0.2 shard_map.114.chosen_ref
  1.5 0.2 copy-done.8
  1.7 0.1 shard_map.116.after_ref
  1.9 4.1 %collective-permute-start = (bf16[40,512]{1,0:T(8,128)(2,1)S(1)}, bf16[40,512]{1,0:T(8,128)(2,1)S(1)}, u32[]{:S(2)}, u32[]{:S(2)}) collective-permute-start(bf16[40,512]{1,0:T(8,128)(2,1)S(1)} %shard_map.116.after_ref), channel_id=1, source_target_pairs={{0,8},{4,12},{8,0},{12,4},{1,9},{5,13},{9,1},{13,5},{2,10},{6,14},... | collective-permute-start | bytes 122888 | tf_op jit(solution)/shard_map/ppermute | solution.py:21
  6.0 0.1 shard_map.115.refs_0_
  6.3 2.1 %collective-permute-done.refs_1_ = bf16[40,512]{1,0:T(8,128)(2,1)S(1)} collective-permute-done((bf16[40,512]{1,0:T(8,128)(2,1)S(1)}, bf16[40,512]{1,0:T(8,128)(2,1)S(1)}, u32[]{:S(2)}, u32[]{:S(2)}) %collective-permute-start) | collective-permute-done | bytes 40992 | tf_op jit(solution)/shard_map/ppermute | solution.py:21
  8.4 2.5 %collective-permute-start.3 = (bf16[40,512]{1,0:T(8,128)(2,1)S(1)}, bf16[40,512]{1,0:T(8,128)(2,1)S(1)}, u32[]{:S(2)}, u32[]{:S(2)}) collective-permute-start(bf16[40,512]{1,0:T(8,128)(2,1)S(1)} %get-tuple-element.24), channel_id=1, source_target_pairs={{0,6},{2,4},{4,2},{6,0},{8,14},{10,12},{12,10},{14,8},{1,7},{3,5},... | collective-permute-start | bytes 122888 | tf_op jit(solution)/shard_map/ppermute | solution.py:21
  10.9 0.8 %collective-permute-start.2 = (bf16[40,512]{1,0:T(8,128)(2,1)S(1)}, bf16[40,512]{1,0:T(8,128)(2,1)S(1)}, u32[]{:S(2)}, u32[]{:S(2)}) collective-permute-start(bf16[40,512]{1,0:T(8,128)(2,1)S(1)} %get-tuple-element.24), channel_id=1, source_target_pairs={{0,4},{2,6},{4,0},{6,2},{8,12},{10,14},{12,8},{14,10},{1,5},{3,7},... | collective-permute-start | bytes 122888 | tf_op jit(solution)/shard_map/ppermute | solution.py:21
  11.7 0.3 collective-permute-start.1
  12.0 2.5 %collective-permute-start.9 = (bf16[1,272,128]{2,1,0:T(8,128)(2,1)S(1)}, bf16[1,272,128]{2,1,0:T(8,128)(2,1)S(1)}, u32[]{:S(2)}, u32[]{:S(2)}) collective-permute-start(bf16[1,272,128]{2,1,0:T(8,128)(2,1)S(1)} %shard_map.117.held_ref), channel_id=1, source_target_pairs={{0,8},{4,12},{8,0},{12,4},{1,9},{5,13},{9,1},{13,5},{2,10},{6,14},... | collective-permute-start | bytes 208904 | tf_op jit(solution)/shard_map/ppermute | solution.py:21
  14.5 0.4 collective-permute-done.2.refs_2_
  14.9 0.8 %collective-permute-done.1.refs_1_ = bf16[40,512]{1,0:T(8,128)(2,1)S(1)} collective-permute-done((bf16[40,512]{1,0:T(8,128)(2,1)S(1)}, bf16[40,512]{1,0:T(8,128)(2,1)S(1)}, u32[]{:S(2)}, u32[]{:S(2)}) %collective-permute-start.1) | collective-permute-done | bytes 40992 | tf_op jit(solution)/shard_map/ppermute | solution.py:21
  15.7 0.7 %shard_map.119 = (bf16[40,768]{1,0:T(8,128)(2,1)S(1)}, f32[40,768]{1,0:T(8,128)S(1)}, bf16[40,768]{1,0:T(8,128)(2,1)S(1)}, f32[40,768]{1,0:T(8,128)S(1)}) custom-call(bf16[40,512]{1,0:T(8,128)(2,1)S(1)} %get-tuple-element.23.refs_0_, bf16[40,512]{1,0:T(8,128)(2,1)S(1)} %collective-permute-done.1.refs_1_, bf16[40,512]{1,0:T(8,128)(2,1)S(1)} %collective-permute-done.2.refs_2_, ...), custom_call_target="tpu_custom_call" | custom-call | tf_op jit(solution)/shard_map/pallas_call | solution.py:32
  16.4 0.5 %collective-permute-start.5 = (bf16[40,768]{1,0:T(8,128)(2,1)S(1)}, bf16[40,768]{1,0:T(8,128)(2,1)S(1)}, u32[]{:S(2)}, u32[]{:S(2)}) collective-permute-start(bf16[40,768]{1,0:T(8,128)(2,1)S(1)} %get-tuple-element.28), channel_id=1, source_target_pairs={{0,1},{1,0},{2,3},{3,2},{4,5},{5,4},{6,7},{7,6},{8,9},{9,8},{10,11... | collective-permute-start | bytes 184328 | tf_op jit(solution)/shard_map/ppermute | solution.py:21
  16.9 0.7 %collective-permute-done.4.gate_received_ref = bf16[40,768]{1,0:T(8,128)(2,1)S(1)} collective-permute-done((bf16[40,768]{1,0:T(8,128)(2,1)S(1)}, bf16[40,768]{1,0:T(8,128)(2,1)S(1)}, u32[]{:S(2)}, u32[]{:S(2)}) %collective-permute-start.4) | collective-permute-done | bytes 61472 | tf_op jit(solution)/shard_map/ppermute | solution.py:21
  17.6 0.2 collective-permute-done.5.up_received_ref
  17.8 2.4 %collective-permute-start.6 = (bf16[40,1536]{1,0:T(8,128)(2,1)S(1)}, bf16[40,1536]{1,0:T(8,128)(2,1)S(1)}, u32[]{:S(2)}, u32[]{:S(2)}) collective-permute-start(bf16[40,1536]{1,0:T(8,128)(2,1)S(1)} %get-tuple-element.30.after_ref), channel_id=1, source_target_pairs={{0,8},{4,12},{8,0},{12,4},{1,9},{5,13},{9,1},{13,5},{2,10},{6,14},... | collective-permute-start | bytes 368648 | tf_op jit(solution)/shard_map/ppermute | solution.py:21
  20.2 1.9 %collective-permute-start.10 = (bf16[2,272,128]{2,1,0:T(8,128)(2,1)S(1)}, bf16[2,272,128]{2,1,0:T(8,128)(2,1)S(1)}, u32[]{:S(2)}, u32[]{:S(2)}) collective-permute-start(bf16[2,272,128]{2,1,0:T(8,128)(2,1)S(1)} %shard_map.123.held_ref), channel_id=1, source_target_pairs={{0,4},{4,0},{8,12},{12,8},{1,5},{5,1},{9,13},{13,9},{2,6},{6,2},{1... | collective-permute-start | bytes 417800 | tf_op jit(solution)/shard_map/ppermute | solution.py:21
  22.2 4.9 %collective-permute-done.6.received_ref = bf16[40,1536]{1,0:T(8,128)(2,1)S(1)} collective-permute-done((bf16[40,1536]{1,0:T(8,128)(2,1)S(1)}, bf16[40,1536]{1,0:T(8,128)(2,1)S(1)}, u32[]{:S(2)}, u32[]{:S(2)}) %collective-permute-start.6) | collective-permute-done | bytes 122912 | tf_op jit(solution)/shard_map/ppermute | solution.py:21
  27.3 0.4 collective-permute-done.10.received_ref
  27.7 0.8 %collective-permute-done.7.received_ref = bf16[40,768]{1,0:T(8,128)(2,1)S(1)} collective-permute-done((bf16[40,768]{1,0:T(8,128)(2,1)S(1)}, bf16[40,768]{1,0:T(8,128)(2,1)S(1)}, u32[]{:S(2)}, u32[]{:S(2)}) %collective-permute-start.7) | collective-permute-done | bytes 61472 | tf_op jit(solution)/shard_map/ppermute | solution.py:21
  28.5 0.4 %shard_map.122 = (f32[40,512]{1,0:T(8,128)S(1)}, bf16[40,512]{1,0:T(8,128)(2,1)S(1)}, bf16[40,512]{1,0:T(8,128)(2,1)S(1)}, bf16[40,512]{1,0:T(8,128)(2,1)S(1)}) custom-call(bf16[40,768]{1,0:T(8,128)(2,1)S(1)} %shard_map.121.hidden_ref, bf16[40,768]{1,0:T(8,128)(2,1)S(1)} %collective-permute-done.7.received_ref, bf16[768,1024]{1,0:T(8,128)(2,1)S(1)} %bitcast.17), custom_call_target="tpu_custom_call" | custom-call | flops 125829120 | bytes 1900544 | tf_op jit(solution)/shard_map/pallas_call | solution.py:32
  28.9 0.4 collective-permute-start.12
  29.3 1.6 %collective-permute-start.8 = (bf16[40,512]{1,0:T(8,128)(2,1)S(1)}, bf16[40,512]{1,0:T(8,128)(2,1)S(1)}, u32[]{:S(2)}, u32[]{:S(2)}) collective-permute-start(bf16[40,512]{1,0:T(8,128)(2,1)S(1)} %get-tuple-element.31), channel_id=1, source_target_pairs={{0,6},{2,4},{4,2},{6,0},{8,14},{10,12},{12,10},{14,8},{1,7},{3,5},... | collective-permute-start | bytes 122888 | tf_op jit(solution)/shard_map/ppermute | solution.py:21
  30.9 1.6 %collective-permute-start.11 = (bf16[40,512]{1,0:T(8,128)(2,1)S(1)}, bf16[40,512]{1,0:T(8,128)(2,1)S(1)}, u32[]{:S(2)}, u32[]{:S(2)}) collective-permute-start(bf16[40,512]{1,0:T(8,128)(2,1)S(1)} %get-tuple-element.38), channel_id=1, source_target_pairs={{0,2},{2,0},{4,6},{6,4},{8,10},{10,8},{12,14},{14,12},{1,3},{3,1},... | collective-permute-start | bytes 122888 | tf_op jit(solution)/shard_map/ppermute | solution.py:21
  32.5 2.6 %shard_map.125 = bf16[128,2048]{1,0:T(8,128)(2,1)} custom-call(bf16[128,2048]{1,0:T(8,128)(2,1)S(1)} %bitcast.25, bf16[4,272,128]{2,1,0:T(8,128)(2,1)S(1)} %shard_map.124.held_ref, s32[1,128]{1,0:T(1,128)S(1)} %copy-done.7), custom_call_target="tpu_custom_call" | custom-call | flops 536870912 | bytes 1327616 | tf_op jit(solution)/shard_map/pallas_call | solution.py:32
  35.1 2.6 %collective-permute-start.13 = (bf16[40,512]{1,0:T(8,128)(2,1)S(1)}, bf16[40,512]{1,0:T(8,128)(2,1)S(1)}, u32[]{:S(2)}, u32[]{:S(2)}) collective-permute-start(bf16[40,512]{1,0:T(8,128)(2,1)S(1)} %get-tuple-element.40), channel_id=1, source_target_pairs={{0,8},{4,12},{8,0},{12,4},{1,9},{5,13},{9,1},{13,5},{2,10},{6,14},... | collective-permute-start | bytes 122888 | tf_op jit(solution)/shard_map/ppermute | solution.py:21
  37.7 0.2 shard_map.126.share_ref
  37.9 0.9 %shard_map.128.refs_0_ = bf16[128,2048]{1,0:T(8,128)(2,1)} custom-call(bf16[2,128,40]{2,1,0:T(8,128)(2,1)S(1)} %shard_map.126.share_ref, bf16[40,512]{1,0:T(8,128)(2,1)S(1)} %get-tuple-element.41.rows_ref), custom_call_target="tpu_custom_call" | custom-call | flops 20971520 | bytes 585728 | tf_op jit(solution)/shard_map/pallas_call | solution.py:32
  38.8 1.7 %collective-permute-done.13.rows_ref = bf16[40,512]{1,0:T(8,128)(2,1)S(1)} collective-permute-done((bf16[40,512]{1,0:T(8,128)(2,1)S(1)}, bf16[40,512]{1,0:T(8,128)(2,1)S(1)}, u32[]{:S(2)}, u32[]{:S(2)}) %collective-permute-start.13) | collective-permute-done | bytes 40992 | tf_op jit(solution)/shard_map/ppermute | solution.py:21
  40.5 0.9 %shard_map.129 = bf16[128,2048]{1,0:T(8,128)(2,1)} custom-call(bf16[2,128,40]{2,1,0:T(8,128)(2,1)S(1)} %shard_map.126.share_ref, bf16[40,512]{1,0:T(8,128)(2,1)S(1)} %collective-permute-done.13.rows_ref, bf16[128,2048]{1,0:T(8,128)(2,1)} %shard_map.128.refs_0_), custom_call_target="tpu_custom_call", output_to_operand_aliasing={{}: (2, {})} | custom-call | flops 20971520 | bytes 1110016 | tf_op jit(solution)/shard_map/pallas_call | solution.py:32
  (33 shorter events, 0.6 us)
Async XLA Ops:
  0.6 0.7 %copy-start.5 = (s32[1,128,8]{1,2,0:T(8,128)S(1)}, s32[1,128,8]{1,2,0:T(8,128)}, u32[]{:S(2)}) copy-start(s32[1,128,8]{1,2,0:T(8,128)} %param.15) | copy-start | bytes 12292
  0.6 1.0 %copy-start.8 = (bf16[1,128,2048]{2,1,0:T(8,128)(2,1)S(1)}, bf16[1,128,2048]{2,1,0:T(8,128)(2,1)}, u32[]{:S(2)}) copy-start(bf16[1,128,2048]{2,1,0:T(8,128)(2,1)} %param.14) | copy-start | bytes 1572868
  1.8 4.3 %copy-start.3 = (bf16[1,128,128]{2,1,0:T(8,128)(2,1)S(1)}, bf16[1,128,128]{2,1,0:T(8,128)(2,1)}, u32[]{:S(2)}) copy-start(bf16[1,128,128]{2,1,0:T(8,128)(2,1)} %param.11) | copy-start | bytes 98308
  1.9 4.3 %copy-start.4 = (bf16[1,128,128]{2,1,0:T(8,128)(2,1)S(1)}, bf16[1,128,128]{2,1,0:T(8,128)(2,1)}, u32[]{:S(2)}) copy-start(bf16[1,128,128]{2,1,0:T(8,128)(2,1)} %param.12) | copy-start | bytes 98308
  1.9 4.3 %copy-start.7 = (s32[1,128]{1,0:T(1,128)S(1)}, s32[1,128]{1,0:T(1,128)}, u32[]{:S(2)}) copy-start(s32[1,128]{1,0:T(1,128)} %segment_ref.2) | copy-start | bytes 1540
  1.9 6.5 %collective-permute-start = (bf16[40,512]{1,0:T(8,128)(2,1)S(1)}, bf16[40,512]{1,0:T(8,128)(2,1)S(1)}, u32[]{:S(2)}, u32[]{:S(2)}) collective-permute-start(bf16[40,512]{1,0:T(8,128)(2,1)S(1)} %shard_map.116.after_ref), channel_id=1, source_target_pairs={{0,8},{4,12},{8,0},{12,4},{1,9},{5,13},{9,1},{13,5},{2,10},{6,14},... | collective-permute-start | bytes 122888 | tf_op jit(solution)/shard_map/ppermute | solution.py:21
  6.3 9.3 %copy-start = (bf16[1,1024,768]{2,1,0:T(8,128)(2,1)S(1)}, bf16[1,1024,768]{2,1,0:T(8,128)(2,1)}, u32[]{:S(2)}) copy-start(bf16[1,1024,768]{2,1,0:T(8,128)(2,1)} %param.17) | copy-start | bytes 4718596
  6.3 9.3 %copy-start.1 = (bf16[1,1024,768]{2,1,0:T(8,128)(2,1)S(1)}, bf16[1,1024,768]{2,1,0:T(8,128)(2,1)}, u32[]{:S(2)}) copy-start(bf16[1,1024,768]{2,1,0:T(8,128)(2,1)} %param.18) | copy-start | bytes 4718596
  8.4 6.1 %collective-permute-start.3 = (bf16[40,512]{1,0:T(8,128)(2,1)S(1)}, bf16[40,512]{1,0:T(8,128)(2,1)S(1)}, u32[]{:S(2)}, u32[]{:S(2)}) collective-permute-start(bf16[40,512]{1,0:T(8,128)(2,1)S(1)} %get-tuple-element.24), channel_id=1, source_target_pairs={{0,6},{2,4},{4,2},{6,0},{8,14},{10,12},{12,10},{14,8},{1,7},{3,5},... | collective-permute-start | bytes 122888 | tf_op jit(solution)/shard_map/ppermute | solution.py:21
  10.9 4.0 %collective-permute-start.2 = (bf16[40,512]{1,0:T(8,128)(2,1)S(1)}, bf16[40,512]{1,0:T(8,128)(2,1)S(1)}, u32[]{:S(2)}, u32[]{:S(2)}) collective-permute-start(bf16[40,512]{1,0:T(8,128)(2,1)S(1)} %get-tuple-element.24), channel_id=1, source_target_pairs={{0,4},{2,6},{4,0},{6,2},{8,12},{10,14},{12,8},{14,10},{1,5},{3,7},... | collective-permute-start | bytes 122888 | tf_op jit(solution)/shard_map/ppermute | solution.py:21
  11.7 4.0 %collective-permute-start.1 = (bf16[40,512]{1,0:T(8,128)(2,1)S(1)}, bf16[40,512]{1,0:T(8,128)(2,1)S(1)}, u32[]{:S(2)}, u32[]{:S(2)}) collective-permute-start(bf16[40,512]{1,0:T(8,128)(2,1)S(1)} %get-tuple-element.23.refs_0_), channel_id=1, source_target_pairs={{0,2},{2,0},{4,6},{6,4},{8,10},{10,8},{12,14},{14,12},{1,3},{3,1},... | collective-permute-start | bytes 122888 | tf_op jit(solution)/shard_map/ppermute | solution.py:21
  12.0 8.2 %collective-permute-start.9 = (bf16[1,272,128]{2,1,0:T(8,128)(2,1)S(1)}, bf16[1,272,128]{2,1,0:T(8,128)(2,1)S(1)}, u32[]{:S(2)}, u32[]{:S(2)}) collective-permute-start(bf16[1,272,128]{2,1,0:T(8,128)(2,1)S(1)} %shard_map.117.held_ref), channel_id=1, source_target_pairs={{0,8},{4,12},{8,0},{12,4},{1,9},{5,13},{9,1},{13,5},{2,10},{6,14},... | collective-permute-start | bytes 208904 | tf_op jit(solution)/shard_map/ppermute | solution.py:21
  16.3 1.3 %collective-permute-start.4 = (bf16[40,768]{1,0:T(8,128)(2,1)S(1)}, bf16[40,768]{1,0:T(8,128)(2,1)S(1)}, u32[]{:S(2)}, u32[]{:S(2)}) collective-permute-start(bf16[40,768]{1,0:T(8,128)(2,1)S(1)} %get-tuple-element.26), channel_id=1, source_target_pairs={{0,1},{1,0},{2,3},{3,2},{4,5},{5,4},{6,7},{7,6},{8,9},{9,8},{10,11... | collective-permute-start | bytes 184328 | tf_op jit(solution)/shard_map/ppermute | solution.py:21
  16.4 1.4 %collective-permute-start.5 = (bf16[40,768]{1,0:T(8,128)(2,1)S(1)}, bf16[40,768]{1,0:T(8,128)(2,1)S(1)}, u32[]{:S(2)}, u32[]{:S(2)}) collective-permute-start(bf16[40,768]{1,0:T(8,128)(2,1)S(1)} %get-tuple-element.28), channel_id=1, source_target_pairs={{0,1},{1,0},{2,3},{3,2},{4,5},{5,4},{6,7},{7,6},{8,9},{9,8},{10,11... | collective-permute-start | bytes 184328 | tf_op jit(solution)/shard_map/ppermute | solution.py:21
  17.8 9.3 %collective-permute-start.6 = (bf16[40,1536]{1,0:T(8,128)(2,1)S(1)}, bf16[40,1536]{1,0:T(8,128)(2,1)S(1)}, u32[]{:S(2)}, u32[]{:S(2)}) collective-permute-start(bf16[40,1536]{1,0:T(8,128)(2,1)S(1)} %get-tuple-element.30.after_ref), channel_id=1, source_target_pairs={{0,8},{4,12},{8,0},{12,4},{1,9},{5,13},{9,1},{13,5},{2,10},{6,14},... | collective-permute-start | bytes 368648 | tf_op jit(solution)/shard_map/ppermute | solution.py:21
  20.2 8.3 %copy-start.2 = (bf16[1,768,1024]{2,1,0:T(8,128)(2,1)S(1)}, bf16[1,768,1024]{2,1,0:T(8,128)(2,1)}, u32[]{:S(2)}) copy-start(bf16[1,768,1024]{2,1,0:T(8,128)(2,1)} %param.19) | copy-start | bytes 4718596
  20.2 12.3 %copy-start.9 = (bf16[1,128,2048]{2,1,0:T(8,128)(2,1)S(1)}, bf16[1,128,2048]{2,1,0:T(8,128)(2,1)}, u32[]{:S(2)}) copy-start(bf16[1,128,2048]{2,1,0:T(8,128)(2,1)} %param.10) | copy-start | bytes 1572868
  20.2 7.4 %collective-permute-start.10 = (bf16[2,272,128]{2,1,0:T(8,128)(2,1)S(1)}, bf16[2,272,128]{2,1,0:T(8,128)(2,1)S(1)}, u32[]{:S(2)}, u32[]{:S(2)}) collective-permute-start(bf16[2,272,128]{2,1,0:T(8,128)(2,1)S(1)} %shard_map.123.held_ref), channel_id=1, source_target_pairs={{0,4},{4,0},{8,12},{12,8},{1,5},{5,1},{9,13},{13,9},{2,6},{6,2},{1... | collective-permute-start | bytes 417800 | tf_op jit(solution)/shard_map/ppermute | solution.py:21
  27.2 1.3 %collective-permute-start.7 = (bf16[40,768]{1,0:T(8,128)(2,1)S(1)}, bf16[40,768]{1,0:T(8,128)(2,1)S(1)}, u32[]{:S(2)}, u32[]{:S(2)}) collective-permute-start(bf16[40,768]{1,0:T(8,128)(2,1)S(1)} %shard_map.121.hidden_ref), channel_id=1, source_target_pairs={{0,1},{1,0},{2,3},{3,2},{4,5},{5,4},{6,7},{7,6},{8,9},{9,8},{10,11... | collective-permute-start | bytes 184328 | tf_op jit(solution)/shard_map/ppermute | solution.py:21
  28.5 9.2 %copy-start.6 = (f32[1,128,8]{1,2,0:T(8,128)S(1)}, f32[1,128,8]{1,2,0:T(8,128)}, u32[]{:S(2)}) copy-start(f32[1,128,8]{1,2,0:T(8,128)} %param.16) | copy-start | bytes 12292
  28.9 6.1 %collective-permute-start.12 = (bf16[40,512]{1,0:T(8,128)(2,1)S(1)}, bf16[40,512]{1,0:T(8,128)(2,1)S(1)}, u32[]{:S(2)}, u32[]{:S(2)}) collective-permute-start(bf16[40,512]{1,0:T(8,128)(2,1)S(1)} %get-tuple-element.34), channel_id=1, source_target_pairs={{0,4},{2,6},{4,0},{6,2},{8,12},{10,14},{12,8},{14,10},{1,5},{3,7},... | collective-permute-start | bytes 122888 | tf_op jit(solution)/shard_map/ppermute | solution.py:21
  29.3 5.7 %collective-permute-start.8 = (bf16[40,512]{1,0:T(8,128)(2,1)S(1)}, bf16[40,512]{1,0:T(8,128)(2,1)S(1)}, u32[]{:S(2)}, u32[]{:S(2)}) collective-permute-start(bf16[40,512]{1,0:T(8,128)(2,1)S(1)} %get-tuple-element.31), channel_id=1, source_target_pairs={{0,6},{2,4},{4,2},{6,0},{8,14},{10,12},{12,10},{14,8},{1,7},{3,5},... | collective-permute-start | bytes 122888 | tf_op jit(solution)/shard_map/ppermute | solution.py:21
  30.9 4.2 %collective-permute-start.11 = (bf16[40,512]{1,0:T(8,128)(2,1)S(1)}, bf16[40,512]{1,0:T(8,128)(2,1)S(1)}, u32[]{:S(2)}, u32[]{:S(2)}) collective-permute-start(bf16[40,512]{1,0:T(8,128)(2,1)S(1)} %get-tuple-element.38), channel_id=1, source_target_pairs={{0,2},{2,0},{4,6},{6,4},{8,10},{10,8},{12,14},{14,12},{1,3},{3,1},... | collective-permute-start | bytes 122888 | tf_op jit(solution)/shard_map/ppermute | solution.py:21
  35.1 5.4 %collective-permute-start.13 = (bf16[40,512]{1,0:T(8,128)(2,1)S(1)}, bf16[40,512]{1,0:T(8,128)(2,1)S(1)}, u32[]{:S(2)}, u32[]{:S(2)}) collective-permute-start(bf16[40,512]{1,0:T(8,128)(2,1)S(1)} %get-tuple-element.40), channel_id=1, source_target_pairs={{0,8},{4,12},{8,0},{12,4},{1,9},{5,13},{9,1},{13,5},{2,10},{6,14},... | collective-permute-start | bytes 122888 | tf_op jit(solution)/shard_map/ppermute | solution.py:21

commit v6 on v5

--- a/solution.py
+++ b/solution.py
@@ -361,8 +361,8 @@
         w_down[0],
         flops=4 * half * ff * quarter,
     )
+    other = [over_side(outs[2 * offset + 1], offset, 1) for offset in reversed(range(sides))][::-1]
     own = [outs[0]] + [over_side(outs[2 * offset], offset, 0) for offset in range(1, sides)]
-    other = [over_side(outs[2 * offset + 1], offset, 1) for offset in range(sides)]
 
     heads = queries.shape[2] // HEAD_DIM
     factor = 1.0 / math.sqrt(HEAD_DIM)
@@ -415,7 +415,7 @@
         flops=4 * heads * length * span * HEAD_DIM,
         exps=heads * length * span,
     )
-    other[-1], attended = lax.optimization_barrier((other[-1], attended))
+    own[0], attended = lax.optimization_barrier((own[0], attended))
 
     def add_parts(*refs):
         sums = []

time: 41.6 us -> 41.4 us (level)
  waiting for transfers between devices: 12 us -> 11.1 us
  starting transfers between devices: 21.2 us -> 21.9 us
    ppermute x14, waiting for transfers between devices: 12 us -> 11.1 us  [swapped(): return lax.ppermute(value, axis, [(i, i ^ bit) for i in range(count)])]
    ppermute x14, starting transfers between devices: 21.2 us -> 21.9 us  [swapped(): return lax.ppermute(value, axis, [(i, i ^ bit) for i in range(count)])]
where the time goes in v6:
time: 41.4 us; the launch traced here: 41.2 us
  starting transfers between devices  21.9 us (53%)
  waiting for transfers between devices  11.1 us (27%)
  Pallas kernels  6.44 us (16%)
  local copies, waits for them, and re-layouts  0.95 us (2%)
  between operations  0.82 us (2%)
    ppermute x14, starting transfers between devices, swapped(): return lax.ppermute(value, axis, [(i, i ^ bit) for i in range(count)])  21.9 us
    ppermute x14, waiting for transfers between devices, swapped(): return lax.ppermute(value, axis, [(i, i ^ bit) for i in range(count)])  11.1 us
    pallas_call x17, Pallas kernels, call(): pl.pallas_call(kernel, out_shape=list(outs), in_specs=[HBM if i in far_in...  6.44 us
    unnamed x20, local copies, waits for them, and re-layouts  0.95 us
  transfers between devices with their start and end apart: 14, of which 9 were waited for; matrix products, arithmetic and copies ran while one was open for 0% of the time, Pallas kernels for 12%

profile of v6, /device:TPU:0, one launch (start us, length us, event | category | flops | bytes accessed | tf_op | source)
XLA Modules:
  0.0 41.2 jit_solution(5807473547584303077)
XLA Ops:
  0.7 0.6 %copy-done.5 = s32[1,128,8]{1,2,0:T(8,128)S(1)} copy-done((s32[1,128,8]{1,2,0:T(8,128)S(1)}, s32[1,128,8]{1,2,0:T(8,128)}, u32[]{:S(2)}) %copy-start.5) | copy-done | bytes 4120
  1.3 0.2 shard_map.114.chosen_ref
  1.5 0.2 copy-done.8
  1.7 0.1 shard_map.116.after_ref
  1.9 4.1 %collective-permute-start = (bf16[40,512]{1,0:T(8,128)(2,1)S(1)}, bf16[40,512]{1,0:T(8,128)(2,1)S(1)}, u32[]{:S(2)}, u32[]{:S(2)}) collective-permute-start(bf16[40,512]{1,0:T(8,128)(2,1)S(1)} %shard_map.116.after_ref), channel_id=1, source_target_pairs={{0,8},{4,12},{8,0},{12,4},{1,9},{5,13},{9,1},{13,5},{2,10},{6,14},... | collective-permute-start | bytes 122888 | tf_op jit(solution)/shard_map/ppermute | solution.py:21
  6.0 0.1 shard_map.115.refs_0_
  6.3 2.1 %collective-permute-done.refs_1_ = bf16[40,512]{1,0:T(8,128)(2,1)S(1)} collective-permute-done((bf16[40,512]{1,0:T(8,128)(2,1)S(1)}, bf16[40,512]{1,0:T(8,128)(2,1)S(1)}, u32[]{:S(2)}, u32[]{:S(2)}) %collective-permute-start) | collective-permute-done | bytes 40992 | tf_op jit(solution)/shard_map/ppermute | solution.py:21
  8.4 2.5 %collective-permute-start.3 = (bf16[40,512]{1,0:T(8,128)(2,1)S(1)}, bf16[40,512]{1,0:T(8,128)(2,1)S(1)}, u32[]{:S(2)}, u32[]{:S(2)}) collective-permute-start(bf16[40,512]{1,0:T(8,128)(2,1)S(1)} %get-tuple-element.24), channel_id=1, source_target_pairs={{0,6},{2,4},{4,2},{6,0},{8,14},{10,12},{12,10},{14,8},{1,7},{3,5},... | collective-permute-start | bytes 122888 | tf_op jit(solution)/shard_map/ppermute | solution.py:21
  10.9 0.8 %collective-permute-start.2 = (bf16[40,512]{1,0:T(8,128)(2,1)S(1)}, bf16[40,512]{1,0:T(8,128)(2,1)S(1)}, u32[]{:S(2)}, u32[]{:S(2)}) collective-permute-start(bf16[40,512]{1,0:T(8,128)(2,1)S(1)} %get-tuple-element.24), channel_id=1, source_target_pairs={{0,4},{2,6},{4,0},{6,2},{8,12},{10,14},{12,8},{14,10},{1,5},{3,7},... | collective-permute-start | bytes 122888 | tf_op jit(solution)/shard_map/ppermute | solution.py:21
  11.7 0.3 collective-permute-start.1
  12.0 2.5 %collective-permute-start.8 = (bf16[1,272,128]{2,1,0:T(8,128)(2,1)S(1)}, bf16[1,272,128]{2,1,0:T(8,128)(2,1)S(1)}, u32[]{:S(2)}, u32[]{:S(2)}) collective-permute-start(bf16[1,272,128]{2,1,0:T(8,128)(2,1)S(1)} %shard_map.117.held_ref), channel_id=1, source_target_pairs={{0,8},{4,12},{8,0},{12,4},{1,9},{5,13},{9,1},{13,5},{2,10},{6,14},... | collective-permute-start | bytes 208904 | tf_op jit(solution)/shard_map/ppermute | solution.py:21
  14.5 0.4 collective-permute-done.2.refs_2_
  14.9 0.8 %collective-permute-done.1.refs_1_ = bf16[40,512]{1,0:T(8,128)(2,1)S(1)} collective-permute-done((bf16[40,512]{1,0:T(8,128)(2,1)S(1)}, bf16[40,512]{1,0:T(8,128)(2,1)S(1)}, u32[]{:S(2)}, u32[]{:S(2)}) %collective-permute-start.1) | collective-permute-done | bytes 40992 | tf_op jit(solution)/shard_map/ppermute | solution.py:21
  15.7 0.7 %shard_map.119 = (bf16[40,768]{1,0:T(8,128)(2,1)S(1)}, f32[40,768]{1,0:T(8,128)S(1)}, bf16[40,768]{1,0:T(8,128)(2,1)S(1)}, f32[40,768]{1,0:T(8,128)S(1)}) custom-call(bf16[40,512]{1,0:T(8,128)(2,1)S(1)} %get-tuple-element.23.refs_0_, bf16[40,512]{1,0:T(8,128)(2,1)S(1)} %collective-permute-done.1.refs_1_, bf16[40,512]{1,0:T(8,128)(2,1)S(1)} %collective-permute-done.2.refs_2_, ...), custom_call_target="tpu_custom_call" | custom-call | tf_op jit(solution)/shard_map/pallas_call | solution.py:32
  16.4 0.5 %collective-permute-start.5 = (bf16[40,768]{1,0:T(8,128)(2,1)S(1)}, bf16[40,768]{1,0:T(8,128)(2,1)S(1)}, u32[]{:S(2)}, u32[]{:S(2)}) collective-permute-start(bf16[40,768]{1,0:T(8,128)(2,1)S(1)} %get-tuple-element.28), channel_id=1, source_target_pairs={{0,1},{1,0},{2,3},{3,2},{4,5},{5,4},{6,7},{7,6},{8,9},{9,8},{10,11... | collective-permute-start | bytes 184328 | tf_op jit(solution)/shard_map/ppermute | solution.py:21
  16.9 0.7 %collective-permute-done.4.gate_received_ref = bf16[40,768]{1,0:T(8,128)(2,1)S(1)} collective-permute-done((bf16[40,768]{1,0:T(8,128)(2,1)S(1)}, bf16[40,768]{1,0:T(8,128)(2,1)S(1)}, u32[]{:S(2)}, u32[]{:S(2)}) %collective-permute-start.4) | collective-permute-done | bytes 61472 | tf_op jit(solution)/shard_map/ppermute | solution.py:21
  17.6 0.2 collective-permute-done.5.up_received_ref
  17.8 2.4 %collective-permute-start.6 = (bf16[40,1536]{1,0:T(8,128)(2,1)S(1)}, bf16[40,1536]{1,0:T(8,128)(2,1)S(1)}, u32[]{:S(2)}, u32[]{:S(2)}) collective-permute-start(bf16[40,1536]{1,0:T(8,128)(2,1)S(1)} %get-tuple-element.30.after_ref), channel_id=1, source_target_pairs={{0,8},{4,12},{8,0},{12,4},{1,9},{5,13},{9,1},{13,5},{2,10},{6,14},... | collective-permute-start | bytes 368648 | tf_op jit(solution)/shard_map/ppermute | solution.py:21
  20.2 1.9 %collective-permute-start.9 = (bf16[2,272,128]{2,1,0:T(8,128)(2,1)S(1)}, bf16[2,272,128]{2,1,0:T(8,128)(2,1)S(1)}, u32[]{:S(2)}, u32[]{:S(2)}) collective-permute-start(bf16[2,272,128]{2,1,0:T(8,128)(2,1)S(1)} %shard_map.123.held_ref), channel_id=1, source_target_pairs={{0,4},{4,0},{8,12},{12,8},{1,5},{5,1},{9,13},{13,9},{2,6},{6,2},{1... | collective-permute-start | bytes 417800 | tf_op jit(solution)/shard_map/ppermute | solution.py:21
  22.2 4.9 %collective-permute-done.6.received_ref = bf16[40,1536]{1,0:T(8,128)(2,1)S(1)} collective-permute-done((bf16[40,1536]{1,0:T(8,128)(2,1)S(1)}, bf16[40,1536]{1,0:T(8,128)(2,1)S(1)}, u32[]{:S(2)}, u32[]{:S(2)}) %collective-permute-start.6) | collective-permute-done | bytes 122912 | tf_op jit(solution)/shard_map/ppermute | solution.py:21
  27.3 0.4 collective-permute-done.9.received_ref
  27.7 0.8 %collective-permute-done.7.received_ref = bf16[40,768]{1,0:T(8,128)(2,1)S(1)} collective-permute-done((bf16[40,768]{1,0:T(8,128)(2,1)S(1)}, bf16[40,768]{1,0:T(8,128)(2,1)S(1)}, u32[]{:S(2)}, u32[]{:S(2)}) %collective-permute-start.7) | collective-permute-done | bytes 61472 | tf_op jit(solution)/shard_map/ppermute | solution.py:21
  28.5 0.4 %shard_map.122 = (f32[40,512]{1,0:T(8,128)S(1)}, bf16[40,512]{1,0:T(8,128)(2,1)S(1)}, bf16[40,512]{1,0:T(8,128)(2,1)S(1)}, bf16[40,512]{1,0:T(8,128)(2,1)S(1)}) custom-call(bf16[40,768]{1,0:T(8,128)(2,1)S(1)} %shard_map.121.hidden_ref, bf16[40,768]{1,0:T(8,128)(2,1)S(1)} %collective-permute-done.7.received_ref, bf16[768,1024]{1,0:T(8,128)(2,1)S(1)} %bitcast.17), custom_call_target="tpu_custom_call" | custom-call | flops 125829120 | bytes 1900544 | tf_op jit(solution)/shard_map/pallas_call | solution.py:32
  28.9 0.4 collective-permute-start.11
  29.3 0.5 %collective-permute-start.10 = (bf16[40,512]{1,0:T(8,128)(2,1)S(1)}, bf16[40,512]{1,0:T(8,128)(2,1)S(1)}, u32[]{:S(2)}, u32[]{:S(2)}) collective-permute-start(bf16[40,512]{1,0:T(8,128)(2,1)S(1)} %get-tuple-element.38), channel_id=1, source_target_pairs={{0,2},{2,0},{4,6},{6,4},{8,10},{10,8},{12,14},{14,12},{1,3},{3,1},... | collective-permute-start | bytes 122888 | tf_op jit(solution)/shard_map/ppermute | solution.py:21
  29.9 2.6 %collective-permute-start.12 = (bf16[40,512]{1,0:T(8,128)(2,1)S(1)}, bf16[40,512]{1,0:T(8,128)(2,1)S(1)}, u32[]{:S(2)}, u32[]{:S(2)}) collective-permute-start(bf16[40,512]{1,0:T(8,128)(2,1)S(1)} %get-tuple-element.39), channel_id=1, source_target_pairs={{0,6},{2,4},{4,2},{6,0},{8,14},{10,12},{12,10},{14,8},{1,7},{3,5},... | collective-permute-start | bytes 122888 | tf_op jit(solution)/shard_map/ppermute | solution.py:21
  32.5 2.6 %shard_map.125 = bf16[128,2048]{1,0:T(8,128)(2,1)} custom-call(bf16[128,2048]{1,0:T(8,128)(2,1)S(1)} %bitcast.25, bf16[4,272,128]{2,1,0:T(8,128)(2,1)S(1)} %shard_map.124.held_ref, s32[1,128]{1,0:T(1,128)S(1)} %copy-done.7), custom_call_target="tpu_custom_call" | custom-call | flops 536870912 | bytes 1327616 | tf_op jit(solution)/shard_map/pallas_call | solution.py:32
  35.1 3.2 %collective-permute-start.13 = (bf16[40,512]{1,0:T(8,128)(2,1)S(1)}, bf16[40,512]{1,0:T(8,128)(2,1)S(1)}, u32[]{:S(2)}, u32[]{:S(2)}) collective-permute-start(bf16[40,512]{1,0:T(8,128)(2,1)S(1)} %get-tuple-element.40), channel_id=1, source_target_pairs={{0,8},{4,12},{8,0},{12,4},{1,9},{5,13},{9,1},{13,5},{2,10},{6,14},... | collective-permute-start | bytes 122888 | tf_op jit(solution)/shard_map/ppermute | solution.py:21
  38.3 0.2 shard_map.126.share_ref
  38.6 0.9 %shard_map.128.refs_0_ = bf16[128,2048]{1,0:T(8,128)(2,1)} custom-call(bf16[2,128,40]{2,1,0:T(8,128)(2,1)S(1)} %shard_map.126.share_ref, bf16[40,512]{1,0:T(8,128)(2,1)S(1)} %get-tuple-element.41.rows_ref), custom_call_target="tpu_custom_call" | custom-call | flops 20971520 | bytes 585728 | tf_op jit(solution)/shard_map/pallas_call | solution.py:32
  39.5 0.8 %collective-permute-done.13.rows_ref = bf16[40,512]{1,0:T(8,128)(2,1)S(1)} collective-permute-done((bf16[40,512]{1,0:T(8,128)(2,1)S(1)}, bf16[40,512]{1,0:T(8,128)(2,1)S(1)}, u32[]{:S(2)}, u32[]{:S(2)}) %collective-permute-start.13) | collective-permute-done | bytes 40992 | tf_op jit(solution)/shard_map/ppermute | solution.py:21
  40.3 0.9 %shard_map.129 = bf16[128,2048]{1,0:T(8,128)(2,1)} custom-call(bf16[2,128,40]{2,1,0:T(8,128)(2,1)S(1)} %shard_map.126.share_ref, bf16[40,512]{1,0:T(8,128)(2,1)S(1)} %collective-permute-done.13.rows_ref, bf16[128,2048]{1,0:T(8,128)(2,1)} %shard_map.128.refs_0_), custom_call_target="tpu_custom_call", output_to_operand_aliasing={{}: (2, {})} | custom-call | flops 20971520 | bytes 1110016 | tf_op jit(solution)/shard_map/pallas_call | solution.py:32
  (33 shorter events, 0.6 us)
Async XLA Ops:
  0.6 0.7 %copy-start.5 = (s32[1,128,8]{1,2,0:T(8,128)S(1)}, s32[1,128,8]{1,2,0:T(8,128)}, u32[]{:S(2)}) copy-start(s32[1,128,8]{1,2,0:T(8,128)} %param.15) | copy-start | bytes 12292
  0.6 1.0 %copy-start.8 = (bf16[1,128,2048]{2,1,0:T(8,128)(2,1)S(1)}, bf16[1,128,2048]{2,1,0:T(8,128)(2,1)}, u32[]{:S(2)}) copy-start(bf16[1,128,2048]{2,1,0:T(8,128)(2,1)} %param.14) | copy-start | bytes 1572868
  1.8 4.3 %copy-start.3 = (bf16[1,128,128]{2,1,0:T(8,128)(2,1)S(1)}, bf16[1,128,128]{2,1,0:T(8,128)(2,1)}, u32[]{:S(2)}) copy-start(bf16[1,128,128]{2,1,0:T(8,128)(2,1)} %param.11) | copy-start | bytes 98308
  1.9 4.3 %copy-start.4 = (bf16[1,128,128]{2,1,0:T(8,128)(2,1)S(1)}, bf16[1,128,128]{2,1,0:T(8,128)(2,1)}, u32[]{:S(2)}) copy-start(bf16[1,128,128]{2,1,0:T(8,128)(2,1)} %param.12) | copy-start | bytes 98308
  1.9 4.3 %copy-start.7 = (s32[1,128]{1,0:T(1,128)S(1)}, s32[1,128]{1,0:T(1,128)}, u32[]{:S(2)}) copy-start(s32[1,128]{1,0:T(1,128)} %segment_ref.2) | copy-start | bytes 1540
  1.9 6.5 %collective-permute-start = (bf16[40,512]{1,0:T(8,128)(2,1)S(1)}, bf16[40,512]{1,0:T(8,128)(2,1)S(1)}, u32[]{:S(2)}, u32[]{:S(2)}) collective-permute-start(bf16[40,512]{1,0:T(8,128)(2,1)S(1)} %shard_map.116.after_ref), channel_id=1, source_target_pairs={{0,8},{4,12},{8,0},{12,4},{1,9},{5,13},{9,1},{13,5},{2,10},{6,14},... | collective-permute-start | bytes 122888 | tf_op jit(solution)/shard_map/ppermute | solution.py:21
  6.3 9.3 %copy-start = (bf16[1,1024,768]{2,1,0:T(8,128)(2,1)S(1)}, bf16[1,1024,768]{2,1,0:T(8,128)(2,1)}, u32[]{:S(2)}) copy-start(bf16[1,1024,768]{2,1,0:T(8,128)(2,1)} %param.17) | copy-start | bytes 4718596
  6.3 9.3 %copy-start.1 = (bf16[1,1024,768]{2,1,0:T(8,128)(2,1)S(1)}, bf16[1,1024,768]{2,1,0:T(8,128)(2,1)}, u32[]{:S(2)}) copy-start(bf16[1,1024,768]{2,1,0:T(8,128)(2,1)} %param.18) | copy-start | bytes 4718596
  8.4 6.1 %collective-permute-start.3 = (bf16[40,512]{1,0:T(8,128)(2,1)S(1)}, bf16[40,512]{1,0:T(8,128)(2,1)S(1)}, u32[]{:S(2)}, u32[]{:S(2)}) collective-permute-start(bf16[40,512]{1,0:T(8,128)(2,1)S(1)} %get-tuple-element.24), channel_id=1, source_target_pairs={{0,6},{2,4},{4,2},{6,0},{8,14},{10,12},{12,10},{14,8},{1,7},{3,5},... | collective-permute-start | bytes 122888 | tf_op jit(solution)/shard_map/ppermute | solution.py:21
  10.9 4.0 %collective-permute-start.2 = (bf16[40,512]{1,0:T(8,128)(2,1)S(1)}, bf16[40,512]{1,0:T(8,128)(2,1)S(1)}, u32[]{:S(2)}, u32[]{:S(2)}) collective-permute-start(bf16[40,512]{1,0:T(8,128)(2,1)S(1)} %get-tuple-element.24), channel_id=1, source_target_pairs={{0,4},{2,6},{4,0},{6,2},{8,12},{10,14},{12,8},{14,10},{1,5},{3,7},... | collective-permute-start | bytes 122888 | tf_op jit(solution)/shard_map/ppermute | solution.py:21
  11.7 4.0 %collective-permute-start.1 = (bf16[40,512]{1,0:T(8,128)(2,1)S(1)}, bf16[40,512]{1,0:T(8,128)(2,1)S(1)}, u32[]{:S(2)}, u32[]{:S(2)}) collective-permute-start(bf16[40,512]{1,0:T(8,128)(2,1)S(1)} %get-tuple-element.23.refs_0_), channel_id=1, source_target_pairs={{0,2},{2,0},{4,6},{6,4},{8,10},{10,8},{12,14},{14,12},{1,3},{3,1},... | collective-permute-start | bytes 122888 | tf_op jit(solution)/shard_map/ppermute | solution.py:21
  12.0 8.2 %collective-permute-start.8 = (bf16[1,272,128]{2,1,0:T(8,128)(2,1)S(1)}, bf16[1,272,128]{2,1,0:T(8,128)(2,1)S(1)}, u32[]{:S(2)}, u32[]{:S(2)}) collective-permute-start(bf16[1,272,128]{2,1,0:T(8,128)(2,1)S(1)} %shard_map.117.held_ref), channel_id=1, source_target_pairs={{0,8},{4,12},{8,0},{12,4},{1,9},{5,13},{9,1},{13,5},{2,10},{6,14},... | collective-permute-start | bytes 208904 | tf_op jit(solution)/shard_map/ppermute | solution.py:21
  16.3 1.3 %collective-permute-start.4 = (bf16[40,768]{1,0:T(8,128)(2,1)S(1)}, bf16[40,768]{1,0:T(8,128)(2,1)S(1)}, u32[]{:S(2)}, u32[]{:S(2)}) collective-permute-start(bf16[40,768]{1,0:T(8,128)(2,1)S(1)} %get-tuple-element.26), channel_id=1, source_target_pairs={{0,1},{1,0},{2,3},{3,2},{4,5},{5,4},{6,7},{7,6},{8,9},{9,8},{10,11... | collective-permute-start | bytes 184328 | tf_op jit(solution)/shard_map/ppermute | solution.py:21
  16.4 1.4 %collective-permute-start.5 = (bf16[40,768]{1,0:T(8,128)(2,1)S(1)}, bf16[40,768]{1,0:T(8,128)(2,1)S(1)}, u32[]{:S(2)}, u32[]{:S(2)}) collective-permute-start(bf16[40,768]{1,0:T(8,128)(2,1)S(1)} %get-tuple-element.28), channel_id=1, source_target_pairs={{0,1},{1,0},{2,3},{3,2},{4,5},{5,4},{6,7},{7,6},{8,9},{9,8},{10,11... | collective-permute-start | bytes 184328 | tf_op jit(solution)/shard_map/ppermute | solution.py:21
  17.8 9.3 %collective-permute-start.6 = (bf16[40,1536]{1,0:T(8,128)(2,1)S(1)}, bf16[40,1536]{1,0:T(8,128)(2,1)S(1)}, u32[]{:S(2)}, u32[]{:S(2)}) collective-permute-start(bf16[40,1536]{1,0:T(8,128)(2,1)S(1)} %get-tuple-element.30.after_ref), channel_id=1, source_target_pairs={{0,8},{4,12},{8,0},{12,4},{1,9},{5,13},{9,1},{13,5},{2,10},{6,14},... | collective-permute-start | bytes 368648 | tf_op jit(solution)/shard_map/ppermute | solution.py:21
  20.2 8.3 %copy-start.2 = (bf16[1,768,1024]{2,1,0:T(8,128)(2,1)S(1)}, bf16[1,768,1024]{2,1,0:T(8,128)(2,1)}, u32[]{:S(2)}) copy-start(bf16[1,768,1024]{2,1,0:T(8,128)(2,1)} %param.19) | copy-start | bytes 4718596
  20.2 12.3 %copy-start.9 = (bf16[1,128,2048]{2,1,0:T(8,128)(2,1)S(1)}, bf16[1,128,2048]{2,1,0:T(8,128)(2,1)}, u32[]{:S(2)}) copy-start(bf16[1,128,2048]{2,1,0:T(8,128)(2,1)} %param.10) | copy-start | bytes 1572868
  20.2 7.4 %collective-permute-start.9 = (bf16[2,272,128]{2,1,0:T(8,128)(2,1)S(1)}, bf16[2,272,128]{2,1,0:T(8,128)(2,1)S(1)}, u32[]{:S(2)}, u32[]{:S(2)}) collective-permute-start(bf16[2,272,128]{2,1,0:T(8,128)(2,1)S(1)} %shard_map.123.held_ref), channel_id=1, source_target_pairs={{0,4},{4,0},{8,12},{12,8},{1,5},{5,1},{9,13},{13,9},{2,6},{6,2},{1... | collective-permute-start | bytes 417800 | tf_op jit(solution)/shard_map/ppermute | solution.py:21
  27.2 1.3 %collective-permute-start.7 = (bf16[40,768]{1,0:T(8,128)(2,1)S(1)}, bf16[40,768]{1,0:T(8,128)(2,1)S(1)}, u32[]{:S(2)}, u32[]{:S(2)}) collective-permute-start(bf16[40,768]{1,0:T(8,128)(2,1)S(1)} %shard_map.121.hidden_ref), channel_id=1, source_target_pairs={{0,1},{1,0},{2,3},{3,2},{4,5},{5,4},{6,7},{7,6},{8,9},{9,8},{10,11... | collective-permute-start | bytes 184328 | tf_op jit(solution)/shard_map/ppermute | solution.py:21
  28.5 9.8 %copy-start.6 = (f32[1,128,8]{1,2,0:T(8,128)S(1)}, f32[1,128,8]{1,2,0:T(8,128)}, u32[]{:S(2)}) copy-start(f32[1,128,8]{1,2,0:T(8,128)} %param.16) | copy-start | bytes 12292
  28.9 6.1 %collective-permute-start.11 = (bf16[40,512]{1,0:T(8,128)(2,1)S(1)}, bf16[40,512]{1,0:T(8,128)(2,1)S(1)}, u32[]{:S(2)}, u32[]{:S(2)}) collective-permute-start(bf16[40,512]{1,0:T(8,128)(2,1)S(1)} %get-tuple-element.34), channel_id=1, source_target_pairs={{0,4},{2,6},{4,0},{6,2},{8,12},{10,14},{12,8},{14,10},{1,5},{3,7},... | collective-permute-start | bytes 122888 | tf_op jit(solution)/shard_map/ppermute | solution.py:21
  29.3 5.7 %collective-permute-start.10 = (bf16[40,512]{1,0:T(8,128)(2,1)S(1)}, bf16[40,512]{1,0:T(8,128)(2,1)S(1)}, u32[]{:S(2)}, u32[]{:S(2)}) collective-permute-start(bf16[40,512]{1,0:T(8,128)(2,1)S(1)} %get-tuple-element.38), channel_id=1, source_target_pairs={{0,2},{2,0},{4,6},{6,4},{8,10},{10,8},{12,14},{14,12},{1,3},{3,1},... | collective-permute-start | bytes 122888 | tf_op jit(solution)/shard_map/ppermute | solution.py:21
  29.9 5.2 %collective-permute-start.12 = (bf16[40,512]{1,0:T(8,128)(2,1)S(1)}, bf16[40,512]{1,0:T(8,128)(2,1)S(1)}, u32[]{:S(2)}, u32[]{:S(2)}) collective-permute-start(bf16[40,512]{1,0:T(8,128)(2,1)S(1)} %get-tuple-element.39), channel_id=1, source_target_pairs={{0,6},{2,4},{4,2},{6,0},{8,14},{10,12},{12,10},{14,8},{1,7},{3,5},... | collective-permute-start | bytes 122888 | tf_op jit(solution)/shard_map/ppermute | solution.py:21
  35.1 5.2 %collective-permute-start.13 = (bf16[40,512]{1,0:T(8,128)(2,1)S(1)}, bf16[40,512]{1,0:T(8,128)(2,1)S(1)}, u32[]{:S(2)}, u32[]{:S(2)}) collective-permute-start(bf16[40,512]{1,0:T(8,128)(2,1)S(1)} %get-tuple-element.40), channel_id=1, source_target_pairs={{0,8},{4,12},{8,0},{12,4},{1,9},{5,13},{9,1},{13,5},{2,10},{6,14},... | collective-permute-start | bytes 122888 | tf_op jit(solution)/shard_map/ppermute | solution.py:21

commit v7 on v6

--- a/solution.py
+++ b/solution.py
@@ -365,11 +365,11 @@
     own = [outs[0]] + [over_side(outs[2 * offset], offset, 0) for offset in range(1, sides)]
 
     heads = queries.shape[2] // HEAD_DIM
-    factor = 1.0 / math.sqrt(HEAD_DIM)
+    factor = math.log2(math.e) / math.sqrt(HEAD_DIM)
     span = blocks * length
-    batch = math.gcd(heads, max(1, 2048 // span))
-
-    def attend(query_ref, held_ref, segment_ref, out_ref, keys, values, bias):
+    batch = math.gcd(heads, 4)
+
+    def attend(query_ref, held_ref, segment_ref, out_ref, keys, values, bias, done, sems):
         here = lax.axis_index("blk")
         i = lax.broadcasted_iota(jnp.int32, (length, length), 0)
         j = lax.broadcasted_iota(jnp.int32, (length, length), 1)
@@ -377,7 +377,7 @@
         for place, other_block in enumerate(order):
             at = place * length
             keys[at : at + length, :] = held_ref[place, :length, :]
-            values[at : at + length, :] = held_ref[place, length : 2 * length, :]
+            values[at : at + length, :HEAD_DIM] = held_ref[place, length : 2 * length, :]
             label = held_ref[place, 2 * length : 2 * length + 16, :].astype(F32)[:1]
             same = label_here == label
             if other_block == 0:
@@ -386,23 +386,33 @@
                 seen = same & ((here ^ other_block) < here)
             bias[:, at : at + length] = jnp.where(seen, 0.0, -1e30)
 
-        def some_heads(first):
-            columns = [pl.ds(pl.multiple_of((first + h) * HEAD_DIM, HEAD_DIM), HEAD_DIM) for h in range(batch)]
-            query = jnp.concatenate([query_ref[:, c] for c in columns], axis=0)
-            scores = lax.dot_general(query, keys[...], (((1,), (1,)), ((), ())), preferred_element_type=F32)
-            scores = (scores.reshape(batch, length, span) + bias[...][None]).reshape(batch * length, span)
-            top = jnp.max(scores, axis=1, keepdims=True)
-            weights = jnp.exp((scores - top) * factor)
-            totals = jnp.sum(weights, axis=1, keepdims=True)
-            out = (dot(weights.astype(BF), values[...]) / totals).astype(BF)
-            for h, c in enumerate(columns):
-                out_ref[:, c] = out[h * length : (h + 1) * length]
+        values[:, HEAD_DIM:] = jnp.ones((span, HEAD_DIM), BF)
+
+        def one_head(head):
+            columns = pl.ds(pl.multiple_of(head * HEAD_DIM, HEAD_DIM), HEAD_DIM)
+            scores = lax.dot_general(
+                query_ref[:, columns], keys[...], (((1,), (1,)), ((), ())), preferred_element_type=F32
+            )
+            scores = scores + bias[...]
+            weights = jnp.exp2((scores - jnp.max(scores, axis=1, keepdims=True)) * factor)
+            out = dot(weights.astype(BF), values[...])
+            done[:, columns] = (out[:, :HEAD_DIM] / out[:, HEAD_DIM:]).astype(BF)
+
+        def copied(first):
+            columns = pl.ds(first * HEAD_DIM, batch * HEAD_DIM)
+            return pltpu.make_async_copy(done.at[:, columns], out_ref.at[:, columns], sems.at[first // batch])
 
         if span <= 1024:
+            for head in range(heads):
+                one_head(head)
+                if (head + 1) % batch == 0:
+                    copied(head + 1 - batch).start()
+        else:
+            lax.fori_loop(0, heads, lambda head, _: (one_head(head), 0)[1], 0)
             for first in range(0, heads, batch):
-                some_heads(first)
-        else:
-            lax.fori_loop(0, heads // batch, lambda step, _: (some_heads(step * batch), 0)[1], 0)
+                copied(first).start()
+        for first in range(0, heads, batch):
+            copied(first).wait()
 
     segments_then, _ = lax.optimization_barrier((segments, outs[1]))
     (attended,) = call(
@@ -411,9 +421,14 @@
         queries[0],
         held,
         segments_then,
-        scratch=[pltpu.VMEM((span, HEAD_DIM), BF)] * 2 + [pltpu.VMEM((length, span), F32)],
-        flops=4 * heads * length * span * HEAD_DIM,
-        exps=heads * length * span,
+        scratch=[
+            pltpu.VMEM((span, HEAD_DIM), BF),
+            pltpu.VMEM((span, 2 * HEAD_DIM), BF),
+            pltpu.VMEM((length, span), F32),
+            pltpu.VMEM((length, heads * HEAD_DIM), BF),
+        ],
+        semaphores=heads // batch,
+        far_out=(0,),
     )
     own[0], attended = lax.optimization_barrier((own[0], attended))
 

time: 41.4 us -> 41.3 us (level)
  no operation moved by 1% of the time
where the time goes in v7:
time: 41.3 us; the launch traced here: 41.1 us
  starting transfers between devices  22 us (53%)
  waiting for transfers between devices  11.3 us (27%)
  Pallas kernels  6.1 us (15%)
  local copies, waits for them, and re-layouts  0.95 us (2%)
  between operations  0.86 us (2%)
    ppermute x14, starting transfers between devices, swapped(): return lax.ppermute(value, axis, [(i, i ^ bit) for i in range(count)])  22 us
    ppermute x14, waiting for transfers between devices, swapped(): return lax.ppermute(value, axis, [(i, i ^ bit) for i in range(count)])  11.3 us
    pallas_call x17, Pallas kernels, call(): pl.pallas_call(kernel, out_shape=list(outs), in_specs=[HBM if i in far_in...  6.1 us
    unnamed x20, local copies, waits for them, and re-layouts  0.95 us
  transfers between devices with their start and end apart: 14, of which 9 were waited for; matrix products, arithmetic and copies ran while one was open for 0% of the time, Pallas kernels for 12%

profile of v7, /device:TPU:0, one launch (start us, length us, event | category | flops | bytes accessed | tf_op | source)
XLA Modules:
  0.0 41.1 jit_solution(16454916480080629194)
XLA Ops:
  0.7 0.6 %copy-done.6 = s32[1,128,8]{1,2,0:T(8,128)S(1)} copy-done((s32[1,128,8]{1,2,0:T(8,128)S(1)}, s32[1,128,8]{1,2,0:T(8,128)}, u32[]{:S(2)}) %copy-start.6) | copy-done | bytes 4120
  1.3 0.2 shard_map.114.chosen_ref
  1.5 0.2 copy-done.9
  1.7 0.1 shard_map.116.after_ref
  1.9 4.1 %collective-permute-start = (bf16[40,512]{1,0:T(8,128)(2,1)S(1)}, bf16[40,512]{1,0:T(8,128)(2,1)S(1)}, u32[]{:S(2)}, u32[]{:S(2)}) collective-permute-start(bf16[40,512]{1,0:T(8,128)(2,1)S(1)} %shard_map.116.after_ref), channel_id=1, source_target_pairs={{0,8},{4,12},{8,0},{12,4},{1,9},{5,13},{9,1},{13,5},{2,10},{6,14},... | collective-permute-start | bytes 122888 | tf_op jit(solution)/shard_map/ppermute | solution.py:21
  6.0 0.1 shard_map.115.refs_0_
  6.2 0.1 shard_map.117.held_ref
  6.3 2.1 %collective-permute-done.refs_1_ = bf16[40,512]{1,0:T(8,128)(2,1)S(1)} collective-permute-done((bf16[40,512]{1,0:T(8,128)(2,1)S(1)}, bf16[40,512]{1,0:T(8,128)(2,1)S(1)}, u32[]{:S(2)}, u32[]{:S(2)}) %collective-permute-start) | collective-permute-done | bytes 40992 | tf_op jit(solution)/shard_map/ppermute | solution.py:21
  8.4 2.5 %collective-permute-start.3 = (bf16[40,512]{1,0:T(8,128)(2,1)S(1)}, bf16[40,512]{1,0:T(8,128)(2,1)S(1)}, u32[]{:S(2)}, u32[]{:S(2)}) collective-permute-start(bf16[40,512]{1,0:T(8,128)(2,1)S(1)} %get-tuple-element.24), channel_id=1, source_target_pairs={{0,6},{2,4},{4,2},{6,0},{8,14},{10,12},{12,10},{14,8},{1,7},{3,5},... | collective-permute-start | bytes 122888 | tf_op jit(solution)/shard_map/ppermute | solution.py:21
  10.9 0.8 %collective-permute-start.2 = (bf16[40,512]{1,0:T(8,128)(2,1)S(1)}, bf16[40,512]{1,0:T(8,128)(2,1)S(1)}, u32[]{:S(2)}, u32[]{:S(2)}) collective-permute-start(bf16[40,512]{1,0:T(8,128)(2,1)S(1)} %get-tuple-element.24), channel_id=1, source_target_pairs={{0,4},{2,6},{4,0},{6,2},{8,12},{10,14},{12,8},{14,10},{1,5},{3,7},... | collective-permute-start | bytes 122888 | tf_op jit(solution)/shard_map/ppermute | solution.py:21
  11.7 0.3 collective-permute-start.1
  12.0 2.5 %collective-permute-start.8 = (bf16[1,272,128]{2,1,0:T(8,128)(2,1)S(1)}, bf16[1,272,128]{2,1,0:T(8,128)(2,1)S(1)}, u32[]{:S(2)}, u32[]{:S(2)}) collective-permute-start(bf16[1,272,128]{2,1,0:T(8,128)(2,1)S(1)} %shard_map.117.held_ref), channel_id=1, source_target_pairs={{0,8},{4,12},{8,0},{12,4},{1,9},{5,13},{9,1},{13,5},{2,10},{6,14},... | collective-permute-start | bytes 208904 | tf_op jit(solution)/shard_map/ppermute | solution.py:21
  14.5 0.4 collective-permute-done.2.refs_2_
  14.9 0.8 %collective-permute-done.1.refs_1_ = bf16[40,512]{1,0:T(8,128)(2,1)S(1)} collective-permute-done((bf16[40,512]{1,0:T(8,128)(2,1)S(1)}, bf16[40,512]{1,0:T(8,128)(2,1)S(1)}, u32[]{:S(2)}, u32[]{:S(2)}) %collective-permute-start.1) | collective-permute-done | bytes 40992 | tf_op jit(solution)/shard_map/ppermute | solution.py:21
  15.7 0.7 %shard_map.119 = (bf16[40,768]{1,0:T(8,128)(2,1)S(1)}, f32[40,768]{1,0:T(8,128)S(1)}, bf16[40,768]{1,0:T(8,128)(2,1)S(1)}, f32[40,768]{1,0:T(8,128)S(1)}) custom-call(bf16[40,512]{1,0:T(8,128)(2,1)S(1)} %get-tuple-element.23.refs_0_, bf16[40,512]{1,0:T(8,128)(2,1)S(1)} %collective-permute-done.1.refs_1_, bf16[40,512]{1,0:T(8,128)(2,1)S(1)} %collective-permute-done.2.refs_2_, ...), custom_call_target="tpu_custom_call" | custom-call | tf_op jit(solution)/shard_map/pallas_call | solution.py:32
  16.4 0.5 %collective-permute-start.5 = (bf16[40,768]{1,0:T(8,128)(2,1)S(1)}, bf16[40,768]{1,0:T(8,128)(2,1)S(1)}, u32[]{:S(2)}, u32[]{:S(2)}) collective-permute-start(bf16[40,768]{1,0:T(8,128)(2,1)S(1)} %get-tuple-element.28), channel_id=1, source_target_pairs={{0,1},{1,0},{2,3},{3,2},{4,5},{5,4},{6,7},{7,6},{8,9},{9,8},{10,11... | collective-permute-start | bytes 184328 | tf_op jit(solution)/shard_map/ppermute | solution.py:21
  16.9 0.7 %collective-permute-done.4.gate_received_ref = bf16[40,768]{1,0:T(8,128)(2,1)S(1)} collective-permute-done((bf16[40,768]{1,0:T(8,128)(2,1)S(1)}, bf16[40,768]{1,0:T(8,128)(2,1)S(1)}, u32[]{:S(2)}, u32[]{:S(2)}) %collective-permute-start.4) | collective-permute-done | bytes 61472 | tf_op jit(solution)/shard_map/ppermute | solution.py:21
  17.6 0.2 collective-permute-done.5.up_received_ref
  17.9 2.4 %collective-permute-start.6 = (bf16[40,1536]{1,0:T(8,128)(2,1)S(1)}, bf16[40,1536]{1,0:T(8,128)(2,1)S(1)}, u32[]{:S(2)}, u32[]{:S(2)}) collective-permute-start(bf16[40,1536]{1,0:T(8,128)(2,1)S(1)} %get-tuple-element.30.after_ref), channel_id=1, source_target_pairs={{0,8},{4,12},{8,0},{12,4},{1,9},{5,13},{9,1},{13,5},{2,10},{6,14},... | collective-permute-start | bytes 368648 | tf_op jit(solution)/shard_map/ppermute | solution.py:21
  20.3 1.9 %collective-permute-start.9 = (bf16[2,272,128]{2,1,0:T(8,128)(2,1)S(1)}, bf16[2,272,128]{2,1,0:T(8,128)(2,1)S(1)}, u32[]{:S(2)}, u32[]{:S(2)}) collective-permute-start(bf16[2,272,128]{2,1,0:T(8,128)(2,1)S(1)} %shard_map.123.held_ref), channel_id=1, source_target_pairs={{0,4},{4,0},{8,12},{12,8},{1,5},{5,1},{9,13},{13,9},{2,6},{6,2},{1... | collective-permute-start | bytes 417800 | tf_op jit(solution)/shard_map/ppermute | solution.py:21
  22.2 4.9 %collective-permute-done.6.received_ref = bf16[40,1536]{1,0:T(8,128)(2,1)S(1)} collective-permute-done((bf16[40,1536]{1,0:T(8,128)(2,1)S(1)}, bf16[40,1536]{1,0:T(8,128)(2,1)S(1)}, u32[]{:S(2)}, u32[]{:S(2)}) %collective-permute-start.6) | collective-permute-done | bytes 122912 | tf_op jit(solution)/shard_map/ppermute | solution.py:21
  27.3 1.2 %collective-permute-done.7.received_ref = bf16[40,768]{1,0:T(8,128)(2,1)S(1)} collective-permute-done((bf16[40,768]{1,0:T(8,128)(2,1)S(1)}, bf16[40,768]{1,0:T(8,128)(2,1)S(1)}, u32[]{:S(2)}, u32[]{:S(2)}) %collective-permute-start.7) | collective-permute-done | bytes 61472 | tf_op jit(solution)/shard_map/ppermute | solution.py:21
  28.5 0.4 %shard_map.122 = (f32[40,512]{1,0:T(8,128)S(1)}, bf16[40,512]{1,0:T(8,128)(2,1)S(1)}, bf16[40,512]{1,0:T(8,128)(2,1)S(1)}, bf16[40,512]{1,0:T(8,128)(2,1)S(1)}) custom-call(bf16[40,768]{1,0:T(8,128)(2,1)S(1)} %shard_map.121.hidden_ref, bf16[40,768]{1,0:T(8,128)(2,1)S(1)} %collective-permute-done.7.received_ref, bf16[768,1024]{1,0:T(8,128)(2,1)S(1)} %bitcast.17), custom_call_target="tpu_custom_call" | custom-call | flops 125829120 | bytes 1900544 | tf_op jit(solution)/shard_map/pallas_call | solution.py:32
  28.9 0.5 %collective-permute-start.10 = (bf16[40,512]{1,0:T(8,128)(2,1)S(1)}, bf16[40,512]{1,0:T(8,128)(2,1)S(1)}, u32[]{:S(2)}, u32[]{:S(2)}) collective-permute-start(bf16[40,512]{1,0:T(8,128)(2,1)S(1)} %get-tuple-element.38), channel_id=1, source_target_pairs={{0,2},{2,0},{4,6},{6,4},{8,10},{10,8},{12,14},{14,12},{1,3},{3,1},... | collective-permute-start | bytes 122888 | tf_op jit(solution)/shard_map/ppermute | solution.py:21
  29.4 1.3 %collective-permute-start.12 = (bf16[40,512]{1,0:T(8,128)(2,1)S(1)}, bf16[40,512]{1,0:T(8,128)(2,1)S(1)}, u32[]{:S(2)}, u32[]{:S(2)}) collective-permute-start(bf16[40,512]{1,0:T(8,128)(2,1)S(1)} %get-tuple-element.39), channel_id=1, source_target_pairs={{0,6},{2,4},{4,2},{6,0},{8,14},{10,12},{12,10},{14,8},{1,7},{3,5},... | collective-permute-start | bytes 122888 | tf_op jit(solution)/shard_map/ppermute | solution.py:21
  30.8 1.7 %collective-permute-start.11 = (bf16[40,512]{1,0:T(8,128)(2,1)S(1)}, bf16[40,512]{1,0:T(8,128)(2,1)S(1)}, u32[]{:S(2)}, u32[]{:S(2)}) collective-permute-start(bf16[40,512]{1,0:T(8,128)(2,1)S(1)} %get-tuple-element.34), channel_id=1, source_target_pairs={{0,4},{2,6},{4,0},{6,2},{8,12},{10,14},{12,8},{14,10},{1,5},{3,7},... | collective-permute-start | bytes 122888 | tf_op jit(solution)/shard_map/ppermute | solution.py:21
  32.5 2.2 %shard_map.125 = bf16[128,2048]{1,0:T(8,128)(2,1)} custom-call(bf16[128,2048]{1,0:T(8,128)(2,1)S(1)} %bitcast.18, bf16[4,272,128]{2,1,0:T(8,128)(2,1)S(1)} %shard_map.124.held_ref, s32[1,128]{1,0:T(1,128)S(1)} %copy-done.8), custom_call_target="tpu_custom_call" | custom-call | tf_op jit(solution)/shard_map/pallas_call | solution.py:32
  35.0 3.3 %collective-permute-start.13 = (bf16[40,512]{1,0:T(8,128)(2,1)S(1)}, bf16[40,512]{1,0:T(8,128)(2,1)S(1)}, u32[]{:S(2)}, u32[]{:S(2)}) collective-permute-start(bf16[40,512]{1,0:T(8,128)(2,1)S(1)} %get-tuple-element.40), channel_id=1, source_target_pairs={{0,8},{4,12},{8,0},{12,4},{1,9},{5,13},{9,1},{13,5},{2,10},{6,14},... | collective-permute-start | bytes 122888 | tf_op jit(solution)/shard_map/ppermute | solution.py:21
  38.2 0.2 shard_map.126.share_ref
  38.5 0.9 %shard_map.128.refs_0_ = bf16[128,2048]{1,0:T(8,128)(2,1)} custom-call(bf16[2,128,40]{2,1,0:T(8,128)(2,1)S(1)} %shard_map.126.share_ref, bf16[40,512]{1,0:T(8,128)(2,1)S(1)} %get-tuple-element.41.rows_ref), custom_call_target="tpu_custom_call" | custom-call | flops 20971520 | bytes 585728 | tf_op jit(solution)/shard_map/pallas_call | solution.py:32
  39.4 0.8 %collective-permute-done.13.rows_ref = bf16[40,512]{1,0:T(8,128)(2,1)S(1)} collective-permute-done((bf16[40,512]{1,0:T(8,128)(2,1)S(1)}, bf16[40,512]{1,0:T(8,128)(2,1)S(1)}, u32[]{:S(2)}, u32[]{:S(2)}) %collective-permute-start.13) | collective-permute-done | bytes 40992 | tf_op jit(solution)/shard_map/ppermute | solution.py:21
  40.2 0.9 %shard_map.129 = bf16[128,2048]{1,0:T(8,128)(2,1)} custom-call(bf16[2,128,40]{2,1,0:T(8,128)(2,1)S(1)} %shard_map.126.share_ref, bf16[40,512]{1,0:T(8,128)(2,1)S(1)} %collective-permute-done.13.rows_ref, bf16[128,2048]{1,0:T(8,128)(2,1)} %shard_map.128.refs_0_), custom_call_target="tpu_custom_call", output_to_operand_aliasing={{}: (2, {})} | custom-call | flops 20971520 | bytes 1110016 | tf_op jit(solution)/shard_map/pallas_call | solution.py:32
  (33 shorter events, 0.5 us)
Async XLA Ops:
  0.6 0.7 %copy-start.6 = (s32[1,128,8]{1,2,0:T(8,128)S(1)}, s32[1,128,8]{1,2,0:T(8,128)}, u32[]{:S(2)}) copy-start(s32[1,128,8]{1,2,0:T(8,128)} %param.15) | copy-start | bytes 12292
  0.6 1.0 %copy-start.9 = (bf16[1,128,2048]{2,1,0:T(8,128)(2,1)S(1)}, bf16[1,128,2048]{2,1,0:T(8,128)(2,1)}, u32[]{:S(2)}) copy-start(bf16[1,128,2048]{2,1,0:T(8,128)(2,1)} %param.14) | copy-start | bytes 1572868
  1.8 4.3 %copy-start.4 = (bf16[1,128,128]{2,1,0:T(8,128)(2,1)S(1)}, bf16[1,128,128]{2,1,0:T(8,128)(2,1)}, u32[]{:S(2)}) copy-start(bf16[1,128,128]{2,1,0:T(8,128)(2,1)} %param.11) | copy-start | bytes 98308
  1.9 4.3 %copy-start.5 = (bf16[1,128,128]{2,1,0:T(8,128)(2,1)S(1)}, bf16[1,128,128]{2,1,0:T(8,128)(2,1)}, u32[]{:S(2)}) copy-start(bf16[1,128,128]{2,1,0:T(8,128)(2,1)} %param.12) | copy-start | bytes 98308
  1.9 4.3 %copy-start.8 = (s32[1,128]{1,0:T(1,128)S(1)}, s32[1,128]{1,0:T(1,128)}, u32[]{:S(2)}) copy-start(s32[1,128]{1,0:T(1,128)} %segment_ref.2) | copy-start | bytes 1540
  1.9 6.5 %collective-permute-start = (bf16[40,512]{1,0:T(8,128)(2,1)S(1)}, bf16[40,512]{1,0:T(8,128)(2,1)S(1)}, u32[]{:S(2)}, u32[]{:S(2)}) collective-permute-start(bf16[40,512]{1,0:T(8,128)(2,1)S(1)} %shard_map.116.after_ref), channel_id=1, source_target_pairs={{0,8},{4,12},{8,0},{12,4},{1,9},{5,13},{9,1},{13,5},{2,10},{6,14},... | collective-permute-start | bytes 122888 | tf_op jit(solution)/shard_map/ppermute | solution.py:21
  6.3 9.3 %copy-start = (bf16[1,1024,768]{2,1,0:T(8,128)(2,1)S(1)}, bf16[1,1024,768]{2,1,0:T(8,128)(2,1)}, u32[]{:S(2)}) copy-start(bf16[1,1024,768]{2,1,0:T(8,128)(2,1)} %param.17) | copy-start | bytes 4718596
  6.3 9.3 %copy-start.1 = (bf16[1,1024,768]{2,1,0:T(8,128)(2,1)S(1)}, bf16[1,1024,768]{2,1,0:T(8,128)(2,1)}, u32[]{:S(2)}) copy-start(bf16[1,1024,768]{2,1,0:T(8,128)(2,1)} %param.18) | copy-start | bytes 4718596
  8.4 6.1 %collective-permute-start.3 = (bf16[40,512]{1,0:T(8,128)(2,1)S(1)}, bf16[40,512]{1,0:T(8,128)(2,1)S(1)}, u32[]{:S(2)}, u32[]{:S(2)}) collective-permute-start(bf16[40,512]{1,0:T(8,128)(2,1)S(1)} %get-tuple-element.24), channel_id=1, source_target_pairs={{0,6},{2,4},{4,2},{6,0},{8,14},{10,12},{12,10},{14,8},{1,7},{3,5},... | collective-permute-start | bytes 122888 | tf_op jit(solution)/shard_map/ppermute | solution.py:21
  10.9 4.0 %collective-permute-start.2 = (bf16[40,512]{1,0:T(8,128)(2,1)S(1)}, bf16[40,512]{1,0:T(8,128)(2,1)S(1)}, u32[]{:S(2)}, u32[]{:S(2)}) collective-permute-start(bf16[40,512]{1,0:T(8,128)(2,1)S(1)} %get-tuple-element.24), channel_id=1, source_target_pairs={{0,4},{2,6},{4,0},{6,2},{8,12},{10,14},{12,8},{14,10},{1,5},{3,7},... | collective-permute-start | bytes 122888 | tf_op jit(solution)/shard_map/ppermute | solution.py:21
  11.7 4.0 %collective-permute-start.1 = (bf16[40,512]{1,0:T(8,128)(2,1)S(1)}, bf16[40,512]{1,0:T(8,128)(2,1)S(1)}, u32[]{:S(2)}, u32[]{:S(2)}) collective-permute-start(bf16[40,512]{1,0:T(8,128)(2,1)S(1)} %get-tuple-element.23.refs_0_), channel_id=1, source_target_pairs={{0,2},{2,0},{4,6},{6,4},{8,10},{10,8},{12,14},{14,12},{1,3},{3,1},... | collective-permute-start | bytes 122888 | tf_op jit(solution)/shard_map/ppermute | solution.py:21
  12.0 8.2 %collective-permute-start.8 = (bf16[1,272,128]{2,1,0:T(8,128)(2,1)S(1)}, bf16[1,272,128]{2,1,0:T(8,128)(2,1)S(1)}, u32[]{:S(2)}, u32[]{:S(2)}) collective-permute-start(bf16[1,272,128]{2,1,0:T(8,128)(2,1)S(1)} %shard_map.117.held_ref), channel_id=1, source_target_pairs={{0,8},{4,12},{8,0},{12,4},{1,9},{5,13},{9,1},{13,5},{2,10},{6,14},... | collective-permute-start | bytes 208904 | tf_op jit(solution)/shard_map/ppermute | solution.py:21
  16.3 1.3 %collective-permute-start.4 = (bf16[40,768]{1,0:T(8,128)(2,1)S(1)}, bf16[40,768]{1,0:T(8,128)(2,1)S(1)}, u32[]{:S(2)}, u32[]{:S(2)}) collective-permute-start(bf16[40,768]{1,0:T(8,128)(2,1)S(1)} %get-tuple-element.26), channel_id=1, source_target_pairs={{0,1},{1,0},{2,3},{3,2},{4,5},{5,4},{6,7},{7,6},{8,9},{9,8},{10,11... | collective-permute-start | bytes 184328 | tf_op jit(solution)/shard_map/ppermute | solution.py:21
  16.4 1.4 %collective-permute-start.5 = (bf16[40,768]{1,0:T(8,128)(2,1)S(1)}, bf16[40,768]{1,0:T(8,128)(2,1)S(1)}, u32[]{:S(2)}, u32[]{:S(2)}) collective-permute-start(bf16[40,768]{1,0:T(8,128)(2,1)S(1)} %get-tuple-element.28), channel_id=1, source_target_pairs={{0,1},{1,0},{2,3},{3,2},{4,5},{5,4},{6,7},{7,6},{8,9},{9,8},{10,11... | collective-permute-start | bytes 184328 | tf_op jit(solution)/shard_map/ppermute | solution.py:21
  17.8 10.7 %copy-start.2 = (bf16[1,768,1024]{2,1,0:T(8,128)(2,1)S(1)}, bf16[1,768,1024]{2,1,0:T(8,128)(2,1)}, u32[]{:S(2)}) copy-start(bf16[1,768,1024]{2,1,0:T(8,128)(2,1)} %param.19) | copy-start | bytes 4718596
  17.9 9.3 %collective-permute-start.6 = (bf16[40,1536]{1,0:T(8,128)(2,1)S(1)}, bf16[40,1536]{1,0:T(8,128)(2,1)S(1)}, u32[]{:S(2)}, u32[]{:S(2)}) collective-permute-start(bf16[40,1536]{1,0:T(8,128)(2,1)S(1)} %get-tuple-element.30.after_ref), channel_id=1, source_target_pairs={{0,8},{4,12},{8,0},{12,4},{1,9},{5,13},{9,1},{13,5},{2,10},{6,14},... | collective-permute-start | bytes 368648 | tf_op jit(solution)/shard_map/ppermute | solution.py:21
  20.2 12.3 %copy-start.3 = (bf16[1,128,2048]{2,1,0:T(8,128)(2,1)S(1)}, bf16[1,128,2048]{2,1,0:T(8,128)(2,1)}, u32[]{:S(2)}) copy-start(bf16[1,128,2048]{2,1,0:T(8,128)(2,1)} %param.10) | copy-start | bytes 1572868
  20.3 12.2 %collective-permute-start.9 = (bf16[2,272,128]{2,1,0:T(8,128)(2,1)S(1)}, bf16[2,272,128]{2,1,0:T(8,128)(2,1)S(1)}, u32[]{:S(2)}, u32[]{:S(2)}) collective-permute-start(bf16[2,272,128]{2,1,0:T(8,128)(2,1)S(1)} %shard_map.123.held_ref), channel_id=1, source_target_pairs={{0,4},{4,0},{8,12},{12,8},{1,5},{5,1},{9,13},{13,9},{2,6},{6,2},{1... | collective-permute-start | bytes 417800 | tf_op jit(solution)/shard_map/ppermute | solution.py:21
  27.2 1.3 %collective-permute-start.7 = (bf16[40,768]{1,0:T(8,128)(2,1)S(1)}, bf16[40,768]{1,0:T(8,128)(2,1)S(1)}, u32[]{:S(2)}, u32[]{:S(2)}) collective-permute-start(bf16[40,768]{1,0:T(8,128)(2,1)S(1)} %shard_map.121.hidden_ref), channel_id=1, source_target_pairs={{0,1},{1,0},{2,3},{3,2},{4,5},{5,4},{6,7},{7,6},{8,9},{9,8},{10,11... | collective-permute-start | bytes 184328 | tf_op jit(solution)/shard_map/ppermute | solution.py:21
  28.5 9.7 %copy-start.7 = (f32[1,128,8]{1,2,0:T(8,128)S(1)}, f32[1,128,8]{1,2,0:T(8,128)}, u32[]{:S(2)}) copy-start(f32[1,128,8]{1,2,0:T(8,128)} %param.16) | copy-start | bytes 12292
  28.9 5.8 %collective-permute-start.10 = (bf16[40,512]{1,0:T(8,128)(2,1)S(1)}, bf16[40,512]{1,0:T(8,128)(2,1)S(1)}, u32[]{:S(2)}, u32[]{:S(2)}) collective-permute-start(bf16[40,512]{1,0:T(8,128)(2,1)S(1)} %get-tuple-element.38), channel_id=1, source_target_pairs={{0,2},{2,0},{4,6},{6,4},{8,10},{10,8},{12,14},{14,12},{1,3},{3,1},... | collective-permute-start | bytes 122888 | tf_op jit(solution)/shard_map/ppermute | solution.py:21
  29.4 5.3 %collective-permute-start.12 = (bf16[40,512]{1,0:T(8,128)(2,1)S(1)}, bf16[40,512]{1,0:T(8,128)(2,1)S(1)}, u32[]{:S(2)}, u32[]{:S(2)}) collective-permute-start(bf16[40,512]{1,0:T(8,128)(2,1)S(1)} %get-tuple-element.39), channel_id=1, source_target_pairs={{0,6},{2,4},{4,2},{6,0},{8,14},{10,12},{12,10},{14,8},{1,7},{3,5},... | collective-permute-start | bytes 122888 | tf_op jit(solution)/shard_map/ppermute | solution.py:21
  30.8 4.1 %collective-permute-start.11 = (bf16[40,512]{1,0:T(8,128)(2,1)S(1)}, bf16[40,512]{1,0:T(8,128)(2,1)S(1)}, u32[]{:S(2)}, u32[]{:S(2)}) collective-permute-start(bf16[40,512]{1,0:T(8,128)(2,1)S(1)} %get-tuple-element.34), channel_id=1, source_target_pairs={{0,4},{2,6},{4,0},{6,2},{8,12},{10,14},{12,8},{14,10},{1,5},{3,7},... | collective-permute-start | bytes 122888 | tf_op jit(solution)/shard_map/ppermute | solution.py:21
  35.0 5.3 %collective-permute-start.13 = (bf16[40,512]{1,0:T(8,128)(2,1)S(1)}, bf16[40,512]{1,0:T(8,128)(2,1)S(1)}, u32[]{:S(2)}, u32[]{:S(2)}) collective-permute-start(bf16[40,512]{1,0:T(8,128)(2,1)S(1)} %get-tuple-element.40), channel_id=1, source_target_pairs={{0,8},{4,12},{8,0},{12,4},{1,9},{5,13},{9,1},{13,5},{2,10},{6,14},... | collective-permute-start | bytes 122888 | tf_op jit(solution)/shard_map/ppermute | solution.py:21

commit v8 on v7

--- a/solution.py
+++ b/solution.py
@@ -162,19 +162,22 @@
 
     (earlier,) = call(before, [shaped(length, length)], flops=COST)
 
+    whole_groups = plan.first[:experts]
+    whole_rows = up_to(experts * CAP, 8)
+
     def rank(earlier_ref, ids_ref, out_ref):
-        chosen = ranked(ids_ref[...], None, earlier_ref[...], first_rows, own_expert(), plan.first)
-        for cut in range(cuts):
-            out_ref[cut] = cut_rows(chosen, plan.first, cut)
-
-    (chosen,) = call(rank, [jax.ShapeDtypeStruct((cuts, first_rows, length), BF)], earlier, ids)
+        chosen = ranked(ids_ref[...], None, earlier_ref[...], whole_rows, own_expert(), whole_groups)
+        out_ref[...] = chosen.astype(BF)
+
+    (chosen,) = call(rank, [shaped(whole_rows, length)], earlier, ids)
 
     def choose(run):
         def kernel(chosen_ref, x_ref, out_ref):
-            total = 0.0
-            for cut in range(cuts):
-                total = total + dot(chosen_ref[cut], x_ref[:, columns_of(run, cut, cuts)])
-            out_ref[...] = total.astype(BF)
+            rows = dot(chosen_ref[...], x_ref[:, columns_of(run, 0, 1)])[: experts * CAP]
+            pieces = [rows[:, cut * narrow : (cut + 1) * narrow] for cut in range(cuts)]
+            if first_rows > cuts * experts * CAP:
+                pieces.append(jnp.zeros((first_rows - cuts * experts * CAP, narrow), F32))
+            out_ref[...] = jnp.concatenate(pieces, axis=0).astype(BF)
 
         return call(kernel, [shaped(first_rows, narrow)], chosen, hidden_entry_rows[0], flops=COST)[0]
 

time: 41.3 us -> 41.3 us (level)
  no operation moved by 1% of the time
where the time goes in v8:
time: 41.3 us; the launch traced here: 41.1 us
  starting transfers between devices  22 us (53%)
  waiting for transfers between devices  11.3 us (27%)
  Pallas kernels  6.09 us (15%)
  local copies, waits for them, and re-layouts  0.95 us (2%)
  between operations  0.85 us (2%)
    ppermute x14, starting transfers between devices, swapped(): return lax.ppermute(value, axis, [(i, i ^ bit) for i in range(count)])  22 us
    ppermute x14, waiting for transfers between devices, swapped(): return lax.ppermute(value, axis, [(i, i ^ bit) for i in range(count)])  11.3 us
    pallas_call x17, Pallas kernels, call(): pl.pallas_call(kernel, out_shape=list(outs), in_specs=[HBM if i in far_in...  6.09 us
    unnamed x20, local copies, waits for them, and re-layouts  0.95 us
  transfers between devices with their start and end apart: 14, of which 9 were waited for; matrix products, arithmetic and copies ran while one was open for 0% of the time, Pallas kernels for 12%

profile of v8, /device:TPU:0, one launch (start us, length us, event | category | flops | bytes accessed | tf_op | source)
XLA Modules:
  0.0 41.1 jit_solution(155338728278745079)
XLA Ops:
  0.7 0.6 %copy-done.6 = s32[1,128,8]{1,2,0:T(8,128)S(1)} copy-done((s32[1,128,8]{1,2,0:T(8,128)S(1)}, s32[1,128,8]{1,2,0:T(8,128)}, u32[]{:S(2)}) %copy-start.6) | copy-done | bytes 4120
  1.3 0.1 shard_map.114.chosen_ref
  1.5 0.2 copy-done.9
  1.7 0.1 shard_map.116.after_ref
  1.9 4.1 %collective-permute-start = (bf16[40,512]{1,0:T(8,128)(2,1)S(1)}, bf16[40,512]{1,0:T(8,128)(2,1)S(1)}, u32[]{:S(2)}, u32[]{:S(2)}) collective-permute-start(bf16[40,512]{1,0:T(8,128)(2,1)S(1)} %shard_map.116.after_ref), channel_id=1, source_target_pairs={{0,8},{4,12},{8,0},{12,4},{1,9},{5,13},{9,1},{13,5},{2,10},{6,14},... | collective-permute-start | bytes 122888 | tf_op jit(solution)/shard_map/ppermute | solution.py:21
  6.0 0.1 shard_map.115.refs_0_
  6.2 0.1 shard_map.117.held_ref
  6.3 2.1 %collective-permute-done.refs_1_ = bf16[40,512]{1,0:T(8,128)(2,1)S(1)} collective-permute-done((bf16[40,512]{1,0:T(8,128)(2,1)S(1)}, bf16[40,512]{1,0:T(8,128)(2,1)S(1)}, u32[]{:S(2)}, u32[]{:S(2)}) %collective-permute-start) | collective-permute-done | bytes 40992 | tf_op jit(solution)/shard_map/ppermute | solution.py:21
  8.4 2.5 %collective-permute-start.3 = (bf16[40,512]{1,0:T(8,128)(2,1)S(1)}, bf16[40,512]{1,0:T(8,128)(2,1)S(1)}, u32[]{:S(2)}, u32[]{:S(2)}) collective-permute-start(bf16[40,512]{1,0:T(8,128)(2,1)S(1)} %get-tuple-element.24), channel_id=1, source_target_pairs={{0,6},{2,4},{4,2},{6,0},{8,14},{10,12},{12,10},{14,8},{1,7},{3,5},... | collective-permute-start | bytes 122888 | tf_op jit(solution)/shard_map/ppermute | solution.py:21
  10.9 0.8 %collective-permute-start.2 = (bf16[40,512]{1,0:T(8,128)(2,1)S(1)}, bf16[40,512]{1,0:T(8,128)(2,1)S(1)}, u32[]{:S(2)}, u32[]{:S(2)}) collective-permute-start(bf16[40,512]{1,0:T(8,128)(2,1)S(1)} %get-tuple-element.24), channel_id=1, source_target_pairs={{0,4},{2,6},{4,0},{6,2},{8,12},{10,14},{12,8},{14,10},{1,5},{3,7},... | collective-permute-start | bytes 122888 | tf_op jit(solution)/shard_map/ppermute | solution.py:21
  11.7 0.3 collective-permute-start.1
  12.0 2.5 %collective-permute-start.8 = (bf16[1,272,128]{2,1,0:T(8,128)(2,1)S(1)}, bf16[1,272,128]{2,1,0:T(8,128)(2,1)S(1)}, u32[]{:S(2)}, u32[]{:S(2)}) collective-permute-start(bf16[1,272,128]{2,1,0:T(8,128)(2,1)S(1)} %shard_map.117.held_ref), channel_id=1, source_target_pairs={{0,8},{4,12},{8,0},{12,4},{1,9},{5,13},{9,1},{13,5},{2,10},{6,14},... | collective-permute-start | bytes 208904 | tf_op jit(solution)/shard_map/ppermute | solution.py:21
  14.5 0.4 collective-permute-done.2.refs_2_
  14.9 0.8 %collective-permute-done.1.refs_1_ = bf16[40,512]{1,0:T(8,128)(2,1)S(1)} collective-permute-done((bf16[40,512]{1,0:T(8,128)(2,1)S(1)}, bf16[40,512]{1,0:T(8,128)(2,1)S(1)}, u32[]{:S(2)}, u32[]{:S(2)}) %collective-permute-start.1) | collective-permute-done | bytes 40992 | tf_op jit(solution)/shard_map/ppermute | solution.py:21
  15.7 0.7 %shard_map.119 = (bf16[40,768]{1,0:T(8,128)(2,1)S(1)}, f32[40,768]{1,0:T(8,128)S(1)}, bf16[40,768]{1,0:T(8,128)(2,1)S(1)}, f32[40,768]{1,0:T(8,128)S(1)}) custom-call(bf16[40,512]{1,0:T(8,128)(2,1)S(1)} %get-tuple-element.23.refs_0_, bf16[40,512]{1,0:T(8,128)(2,1)S(1)} %collective-permute-done.1.refs_1_, bf16[40,512]{1,0:T(8,128)(2,1)S(1)} %collective-permute-done.2.refs_2_, ...), custom_call_target="tpu_custom_call" | custom-call | tf_op jit(solution)/shard_map/pallas_call | solution.py:32
  16.4 0.5 %collective-permute-start.5 = (bf16[40,768]{1,0:T(8,128)(2,1)S(1)}, bf16[40,768]{1,0:T(8,128)(2,1)S(1)}, u32[]{:S(2)}, u32[]{:S(2)}) collective-permute-start(bf16[40,768]{1,0:T(8,128)(2,1)S(1)} %get-tuple-element.28), channel_id=1, source_target_pairs={{0,1},{1,0},{2,3},{3,2},{4,5},{5,4},{6,7},{7,6},{8,9},{9,8},{10,11... | collective-permute-start | bytes 184328 | tf_op jit(solution)/shard_map/ppermute | solution.py:21
  16.9 0.7 %collective-permute-done.4.gate_received_ref = bf16[40,768]{1,0:T(8,128)(2,1)S(1)} collective-permute-done((bf16[40,768]{1,0:T(8,128)(2,1)S(1)}, bf16[40,768]{1,0:T(8,128)(2,1)S(1)}, u32[]{:S(2)}, u32[]{:S(2)}) %collective-permute-start.4) | collective-permute-done | bytes 61472 | tf_op jit(solution)/shard_map/ppermute | solution.py:21
  17.6 0.2 collective-permute-done.5.up_received_ref
  17.9 2.4 %collective-permute-start.6 = (bf16[40,1536]{1,0:T(8,128)(2,1)S(1)}, bf16[40,1536]{1,0:T(8,128)(2,1)S(1)}, u32[]{:S(2)}, u32[]{:S(2)}) collective-permute-start(bf16[40,1536]{1,0:T(8,128)(2,1)S(1)} %get-tuple-element.30.after_ref), channel_id=1, source_target_pairs={{0,8},{4,12},{8,0},{12,4},{1,9},{5,13},{9,1},{13,5},{2,10},{6,14},... | collective-permute-start | bytes 368648 | tf_op jit(solution)/shard_map/ppermute | solution.py:21
  20.3 1.9 %collective-permute-start.9 = (bf16[2,272,128]{2,1,0:T(8,128)(2,1)S(1)}, bf16[2,272,128]{2,1,0:T(8,128)(2,1)S(1)}, u32[]{:S(2)}, u32[]{:S(2)}) collective-permute-start(bf16[2,272,128]{2,1,0:T(8,128)(2,1)S(1)} %shard_map.123.held_ref), channel_id=1, source_target_pairs={{0,4},{4,0},{8,12},{12,8},{1,5},{5,1},{9,13},{13,9},{2,6},{6,2},{1... | collective-permute-start | bytes 417800 | tf_op jit(solution)/shard_map/ppermute | solution.py:21
  22.2 4.9 %collective-permute-done.6.received_ref = bf16[40,1536]{1,0:T(8,128)(2,1)S(1)} collective-permute-done((bf16[40,1536]{1,0:T(8,128)(2,1)S(1)}, bf16[40,1536]{1,0:T(8,128)(2,1)S(1)}, u32[]{:S(2)}, u32[]{:S(2)}) %collective-permute-start.6) | collective-permute-done | bytes 122912 | tf_op jit(solution)/shard_map/ppermute | solution.py:21
  27.3 1.2 %collective-permute-done.7.received_ref = bf16[40,768]{1,0:T(8,128)(2,1)S(1)} collective-permute-done((bf16[40,768]{1,0:T(8,128)(2,1)S(1)}, bf16[40,768]{1,0:T(8,128)(2,1)S(1)}, u32[]{:S(2)}, u32[]{:S(2)}) %collective-permute-start.7) | collective-permute-done | bytes 61472 | tf_op jit(solution)/shard_map/ppermute | solution.py:21
  28.5 0.4 %shard_map.122 = (f32[40,512]{1,0:T(8,128)S(1)}, bf16[40,512]{1,0:T(8,128)(2,1)S(1)}, bf16[40,512]{1,0:T(8,128)(2,1)S(1)}, bf16[40,512]{1,0:T(8,128)(2,1)S(1)}) custom-call(bf16[40,768]{1,0:T(8,128)(2,1)S(1)} %shard_map.121.hidden_ref, bf16[40,768]{1,0:T(8,128)(2,1)S(1)} %collective-permute-done.7.received_ref, bf16[768,1024]{1,0:T(8,128)(2,1)S(1)} %bitcast.17), custom_call_target="tpu_custom_call" | custom-call | flops 125829120 | bytes 1900544 | tf_op jit(solution)/shard_map/pallas_call | solution.py:32
  28.9 0.5 %collective-permute-start.10 = (bf16[40,512]{1,0:T(8,128)(2,1)S(1)}, bf16[40,512]{1,0:T(8,128)(2,1)S(1)}, u32[]{:S(2)}, u32[]{:S(2)}) collective-permute-start(bf16[40,512]{1,0:T(8,128)(2,1)S(1)} %get-tuple-element.38), channel_id=1, source_target_pairs={{0,2},{2,0},{4,6},{6,4},{8,10},{10,8},{12,14},{14,12},{1,3},{3,1},... | collective-permute-start | bytes 122888 | tf_op jit(solution)/shard_map/ppermute | solution.py:21
  29.4 1.3 %collective-permute-start.12 = (bf16[40,512]{1,0:T(8,128)(2,1)S(1)}, bf16[40,512]{1,0:T(8,128)(2,1)S(1)}, u32[]{:S(2)}, u32[]{:S(2)}) collective-permute-start(bf16[40,512]{1,0:T(8,128)(2,1)S(1)} %get-tuple-element.39), channel_id=1, source_target_pairs={{0,6},{2,4},{4,2},{6,0},{8,14},{10,12},{12,10},{14,8},{1,7},{3,5},... | collective-permute-start | bytes 122888 | tf_op jit(solution)/shard_map/ppermute | solution.py:21
  30.8 1.7 %collective-permute-start.11 = (bf16[40,512]{1,0:T(8,128)(2,1)S(1)}, bf16[40,512]{1,0:T(8,128)(2,1)S(1)}, u32[]{:S(2)}, u32[]{:S(2)}) collective-permute-start(bf16[40,512]{1,0:T(8,128)(2,1)S(1)} %get-tuple-element.34), channel_id=1, source_target_pairs={{0,4},{2,6},{4,0},{6,2},{8,12},{10,14},{12,8},{14,10},{1,5},{3,7},... | collective-permute-start | bytes 122888 | tf_op jit(solution)/shard_map/ppermute | solution.py:21
  32.5 2.2 %shard_map.125 = bf16[128,2048]{1,0:T(8,128)(2,1)} custom-call(bf16[128,2048]{1,0:T(8,128)(2,1)S(1)} %bitcast.18, bf16[4,272,128]{2,1,0:T(8,128)(2,1)S(1)} %shard_map.124.held_ref, s32[1,128]{1,0:T(1,128)S(1)} %copy-done.8), custom_call_target="tpu_custom_call" | custom-call | tf_op jit(solution)/shard_map/pallas_call | solution.py:32
  34.9 3.3 %collective-permute-start.13 = (bf16[40,512]{1,0:T(8,128)(2,1)S(1)}, bf16[40,512]{1,0:T(8,128)(2,1)S(1)}, u32[]{:S(2)}, u32[]{:S(2)}) collective-permute-start(bf16[40,512]{1,0:T(8,128)(2,1)S(1)} %get-tuple-element.40), channel_id=1, source_target_pairs={{0,8},{4,12},{8,0},{12,4},{1,9},{5,13},{9,1},{13,5},{2,10},{6,14},... | collective-permute-start | bytes 122888 | tf_op jit(solution)/shard_map/ppermute | solution.py:21
  38.2 0.2 shard_map.126.share_ref
  38.5 0.9 %shard_map.128.refs_0_ = bf16[128,2048]{1,0:T(8,128)(2,1)} custom-call(bf16[2,128,40]{2,1,0:T(8,128)(2,1)S(1)} %shard_map.126.share_ref, bf16[40,512]{1,0:T(8,128)(2,1)S(1)} %get-tuple-element.41.rows_ref), custom_call_target="tpu_custom_call" | custom-call | flops 20971520 | bytes 585728 | tf_op jit(solution)/shard_map/pallas_call | solution.py:32
  39.4 0.8 %collective-permute-done.13.rows_ref = bf16[40,512]{1,0:T(8,128)(2,1)S(1)} collective-permute-done((bf16[40,512]{1,0:T(8,128)(2,1)S(1)}, bf16[40,512]{1,0:T(8,128)(2,1)S(1)}, u32[]{:S(2)}, u32[]{:S(2)}) %collective-permute-start.13) | collective-permute-done | bytes 40992 | tf_op jit(solution)/shard_map/ppermute | solution.py:21
  40.2 0.9 %shard_map.129 = bf16[128,2048]{1,0:T(8,128)(2,1)} custom-call(bf16[2,128,40]{2,1,0:T(8,128)(2,1)S(1)} %shard_map.126.share_ref, bf16[40,512]{1,0:T(8,128)(2,1)S(1)} %collective-permute-done.13.rows_ref, bf16[128,2048]{1,0:T(8,128)(2,1)} %shard_map.128.refs_0_), custom_call_target="tpu_custom_call", output_to_operand_aliasing={{}: (2, {})} | custom-call | flops 20971520 | bytes 1110016 | tf_op jit(solution)/shard_map/pallas_call | solution.py:32
  (33 shorter events, 0.5 us)
Async XLA Ops:
  0.6 0.7 %copy-start.6 = (s32[1,128,8]{1,2,0:T(8,128)S(1)}, s32[1,128,8]{1,2,0:T(8,128)}, u32[]{:S(2)}) copy-start(s32[1,128,8]{1,2,0:T(8,128)} %param.15) | copy-start | bytes 12292
  0.6 1.0 %copy-start.9 = (bf16[1,128,2048]{2,1,0:T(8,128)(2,1)S(1)}, bf16[1,128,2048]{2,1,0:T(8,128)(2,1)}, u32[]{:S(2)}) copy-start(bf16[1,128,2048]{2,1,0:T(8,128)(2,1)} %param.14) | copy-start | bytes 1572868
  1.8 4.3 %copy-start.4 = (bf16[1,128,128]{2,1,0:T(8,128)(2,1)S(1)}, bf16[1,128,128]{2,1,0:T(8,128)(2,1)}, u32[]{:S(2)}) copy-start(bf16[1,128,128]{2,1,0:T(8,128)(2,1)} %param.11) | copy-start | bytes 98308
  1.9 4.3 %copy-start.5 = (bf16[1,128,128]{2,1,0:T(8,128)(2,1)S(1)}, bf16[1,128,128]{2,1,0:T(8,128)(2,1)}, u32[]{:S(2)}) copy-start(bf16[1,128,128]{2,1,0:T(8,128)(2,1)} %param.12) | copy-start | bytes 98308
  1.9 4.3 %copy-start.8 = (s32[1,128]{1,0:T(1,128)S(1)}, s32[1,128]{1,0:T(1,128)}, u32[]{:S(2)}) copy-start(s32[1,128]{1,0:T(1,128)} %segment_ref.2) | copy-start | bytes 1540
  1.9 6.5 %collective-permute-start = (bf16[40,512]{1,0:T(8,128)(2,1)S(1)}, bf16[40,512]{1,0:T(8,128)(2,1)S(1)}, u32[]{:S(2)}, u32[]{:S(2)}) collective-permute-start(bf16[40,512]{1,0:T(8,128)(2,1)S(1)} %shard_map.116.after_ref), channel_id=1, source_target_pairs={{0,8},{4,12},{8,0},{12,4},{1,9},{5,13},{9,1},{13,5},{2,10},{6,14},... | collective-permute-start | bytes 122888 | tf_op jit(solution)/shard_map/ppermute | solution.py:21
  6.3 9.3 %copy-start = (bf16[1,1024,768]{2,1,0:T(8,128)(2,1)S(1)}, bf16[1,1024,768]{2,1,0:T(8,128)(2,1)}, u32[]{:S(2)}) copy-start(bf16[1,1024,768]{2,1,0:T(8,128)(2,1)} %param.17) | copy-start | bytes 4718596
  6.3 9.3 %copy-start.1 = (bf16[1,1024,768]{2,1,0:T(8,128)(2,1)S(1)}, bf16[1,1024,768]{2,1,0:T(8,128)(2,1)}, u32[]{:S(2)}) copy-start(bf16[1,1024,768]{2,1,0:T(8,128)(2,1)} %param.18) | copy-start | bytes 4718596
  8.4 6.1 %collective-permute-start.3 = (bf16[40,512]{1,0:T(8,128)(2,1)S(1)}, bf16[40,512]{1,0:T(8,128)(2,1)S(1)}, u32[]{:S(2)}, u32[]{:S(2)}) collective-permute-start(bf16[40,512]{1,0:T(8,128)(2,1)S(1)} %get-tuple-element.24), channel_id=1, source_target_pairs={{0,6},{2,4},{4,2},{6,0},{8,14},{10,12},{12,10},{14,8},{1,7},{3,5},... | collective-permute-start | bytes 122888 | tf_op jit(solution)/shard_map/ppermute | solution.py:21
  10.9 4.0 %collective-permute-start.2 = (bf16[40,512]{1,0:T(8,128)(2,1)S(1)}, bf16[40,512]{1,0:T(8,128)(2,1)S(1)}, u32[]{:S(2)}, u32[]{:S(2)}) collective-permute-start(bf16[40,512]{1,0:T(8,128)(2,1)S(1)} %get-tuple-element.24), channel_id=1, source_target_pairs={{0,4},{2,6},{4,0},{6,2},{8,12},{10,14},{12,8},{14,10},{1,5},{3,7},... | collective-permute-start | bytes 122888 | tf_op jit(solution)/shard_map/ppermute | solution.py:21
  11.7 4.0 %collective-permute-start.1 = (bf16[40,512]{1,0:T(8,128)(2,1)S(1)}, bf16[40,512]{1,0:T(8,128)(2,1)S(1)}, u32[]{:S(2)}, u32[]{:S(2)}) collective-permute-start(bf16[40,512]{1,0:T(8,128)(2,1)S(1)} %get-tuple-element.23.refs_0_), channel_id=1, source_target_pairs={{0,2},{2,0},{4,6},{6,4},{8,10},{10,8},{12,14},{14,12},{1,3},{3,1},... | collective-permute-start | bytes 122888 | tf_op jit(solution)/shard_map/ppermute | solution.py:21
  12.0 8.2 %collective-permute-start.8 = (bf16[1,272,128]{2,1,0:T(8,128)(2,1)S(1)}, bf16[1,272,128]{2,1,0:T(8,128)(2,1)S(1)}, u32[]{:S(2)}, u32[]{:S(2)}) collective-permute-start(bf16[1,272,128]{2,1,0:T(8,128)(2,1)S(1)} %shard_map.117.held_ref), channel_id=1, source_target_pairs={{0,8},{4,12},{8,0},{12,4},{1,9},{5,13},{9,1},{13,5},{2,10},{6,14},... | collective-permute-start | bytes 208904 | tf_op jit(solution)/shard_map/ppermute | solution.py:21
  16.3 1.3 %collective-permute-start.4 = (bf16[40,768]{1,0:T(8,128)(2,1)S(1)}, bf16[40,768]{1,0:T(8,128)(2,1)S(1)}, u32[]{:S(2)}, u32[]{:S(2)}) collective-permute-start(bf16[40,768]{1,0:T(8,128)(2,1)S(1)} %get-tuple-element.26), channel_id=1, source_target_pairs={{0,1},{1,0},{2,3},{3,2},{4,5},{5,4},{6,7},{7,6},{8,9},{9,8},{10,11... | collective-permute-start | bytes 184328 | tf_op jit(solution)/shard_map/ppermute | solution.py:21
  16.4 1.4 %collective-permute-start.5 = (bf16[40,768]{1,0:T(8,128)(2,1)S(1)}, bf16[40,768]{1,0:T(8,128)(2,1)S(1)}, u32[]{:S(2)}, u32[]{:S(2)}) collective-permute-start(bf16[40,768]{1,0:T(8,128)(2,1)S(1)} %get-tuple-element.28), channel_id=1, source_target_pairs={{0,1},{1,0},{2,3},{3,2},{4,5},{5,4},{6,7},{7,6},{8,9},{9,8},{10,11... | collective-permute-start | bytes 184328 | tf_op jit(solution)/shard_map/ppermute | solution.py:21
  17.8 10.7 %copy-start.2 = (bf16[1,768,1024]{2,1,0:T(8,128)(2,1)S(1)}, bf16[1,768,1024]{2,1,0:T(8,128)(2,1)}, u32[]{:S(2)}) copy-start(bf16[1,768,1024]{2,1,0:T(8,128)(2,1)} %param.19) | copy-start | bytes 4718596
  17.9 9.3 %collective-permute-start.6 = (bf16[40,1536]{1,0:T(8,128)(2,1)S(1)}, bf16[40,1536]{1,0:T(8,128)(2,1)S(1)}, u32[]{:S(2)}, u32[]{:S(2)}) collective-permute-start(bf16[40,1536]{1,0:T(8,128)(2,1)S(1)} %get-tuple-element.30.after_ref), channel_id=1, source_target_pairs={{0,8},{4,12},{8,0},{12,4},{1,9},{5,13},{9,1},{13,5},{2,10},{6,14},... | collective-permute-start | bytes 368648 | tf_op jit(solution)/shard_map/ppermute | solution.py:21
  20.2 12.3 %copy-start.3 = (bf16[1,128,2048]{2,1,0:T(8,128)(2,1)S(1)}, bf16[1,128,2048]{2,1,0:T(8,128)(2,1)}, u32[]{:S(2)}) copy-start(bf16[1,128,2048]{2,1,0:T(8,128)(2,1)} %param.10) | copy-start | bytes 1572868
  20.3 12.2 %collective-permute-start.9 = (bf16[2,272,128]{2,1,0:T(8,128)(2,1)S(1)}, bf16[2,272,128]{2,1,0:T(8,128)(2,1)S(1)}, u32[]{:S(2)}, u32[]{:S(2)}) collective-permute-start(bf16[2,272,128]{2,1,0:T(8,128)(2,1)S(1)} %shard_map.123.held_ref), channel_id=1, source_target_pairs={{0,4},{4,0},{8,12},{12,8},{1,5},{5,1},{9,13},{13,9},{2,6},{6,2},{1... | collective-permute-start | bytes 417800 | tf_op jit(solution)/shard_map/ppermute | solution.py:21
  27.2 1.3 %collective-permute-start.7 = (bf16[40,768]{1,0:T(8,128)(2,1)S(1)}, bf16[40,768]{1,0:T(8,128)(2,1)S(1)}, u32[]{:S(2)}, u32[]{:S(2)}) collective-permute-start(bf16[40,768]{1,0:T(8,128)(2,1)S(1)} %shard_map.121.hidden_ref), channel_id=1, source_target_pairs={{0,1},{1,0},{2,3},{3,2},{4,5},{5,4},{6,7},{7,6},{8,9},{9,8},{10,11... | collective-permute-start | bytes 184328 | tf_op jit(solution)/shard_map/ppermute | solution.py:21
  28.5 9.7 %copy-start.7 = (f32[1,128,8]{1,2,0:T(8,128)S(1)}, f32[1,128,8]{1,2,0:T(8,128)}, u32[]{:S(2)}) copy-start(f32[1,128,8]{1,2,0:T(8,128)} %param.16) | copy-start | bytes 12292
  28.9 5.8 %collective-permute-start.10 = (bf16[40,512]{1,0:T(8,128)(2,1)S(1)}, bf16[40,512]{1,0:T(8,128)(2,1)S(1)}, u32[]{:S(2)}, u32[]{:S(2)}) collective-permute-start(bf16[40,512]{1,0:T(8,128)(2,1)S(1)} %get-tuple-element.38), channel_id=1, source_target_pairs={{0,2},{2,0},{4,6},{6,4},{8,10},{10,8},{12,14},{14,12},{1,3},{3,1},... | collective-permute-start | bytes 122888 | tf_op jit(solution)/shard_map/ppermute | solution.py:21
  29.4 5.3 %collective-permute-start.12 = (bf16[40,512]{1,0:T(8,128)(2,1)S(1)}, bf16[40,512]{1,0:T(8,128)(2,1)S(1)}, u32[]{:S(2)}, u32[]{:S(2)}) collective-permute-start(bf16[40,512]{1,0:T(8,128)(2,1)S(1)} %get-tuple-element.39), channel_id=1, source_target_pairs={{0,6},{2,4},{4,2},{6,0},{8,14},{10,12},{12,10},{14,8},{1,7},{3,5},... | collective-permute-start | bytes 122888 | tf_op jit(solution)/shard_map/ppermute | solution.py:21
  30.8 4.1 %collective-permute-start.11 = (bf16[40,512]{1,0:T(8,128)(2,1)S(1)}, bf16[40,512]{1,0:T(8,128)(2,1)S(1)}, u32[]{:S(2)}, u32[]{:S(2)}) collective-permute-start(bf16[40,512]{1,0:T(8,128)(2,1)S(1)} %get-tuple-element.34), channel_id=1, source_target_pairs={{0,4},{2,6},{4,0},{6,2},{8,12},{10,14},{12,8},{14,10},{1,5},{3,7},... | collective-permute-start | bytes 122888 | tf_op jit(solution)/shard_map/ppermute | solution.py:21
  34.9 5.3 %collective-permute-start.13 = (bf16[40,512]{1,0:T(8,128)(2,1)S(1)}, bf16[40,512]{1,0:T(8,128)(2,1)S(1)}, u32[]{:S(2)}, u32[]{:S(2)}) collective-permute-start(bf16[40,512]{1,0:T(8,128)(2,1)S(1)} %get-tuple-element.40), channel_id=1, source_target_pairs={{0,8},{4,12},{8,0},{12,4},{1,9},{5,13},{9,1},{13,5},{2,10},{6,14},... | collective-permute-start | bytes 122888 | tf_op jit(solution)/shard_map/ppermute | solution.py:21

commit v9 on v8

--- a/solution.py
+++ b/solution.py
@@ -460,12 +460,13 @@
         def kernel(share_ref, rows_ref, *refs):
             out_ref, here, sems = refs[-3:]
             copies = []
+            block = length // 4
             for at in range(4):
-                cut, within = at * cuts // 4, at % (4 // cuts)
-                rows = rows_ref[:, within * (quarter // 4) : (within + 1) * (quarter // 4)]
-                here[at] = dot(share_ref[cut], rows).astype(BF)
-                target = out_ref.at[:, columns_of(run, at, 4)]
-                copies.append(pltpu.make_async_copy(here.at[at], target, sems.at[at]))
+                lines = pl.ds(at * block, block)
+                for cut in range(cuts):
+                    here[lines, cut * narrow : (cut + 1) * narrow] = dot(share_ref[cut, lines], rows_ref[...]).astype(BF)
+                target = out_ref.at[lines, columns_of(run, 0, 1)]
+                copies.append(pltpu.make_async_copy(here.at[lines], target, sems.at[at]))
                 copies[-1].start()
             for copy in copies:
                 copy.wait()
@@ -479,7 +480,7 @@
             mix(run),
             [shaped(length, wide)],
             *ins,
-            scratch=[pltpu.VMEM((4, length, quarter // 4), BF)],
+            scratch=[pltpu.VMEM((length, quarter), BF)],
             semaphores=4,
             far_in=(2,),
             far_out=(0,),

time: 41.3 us -> 41.3 us (level)
  no operation moved by 1% of the time
where the time goes in v9:
time: 41.3 us; the launch traced here: 41.1 us
  starting transfers between devices  22 us (53%)
  waiting for transfers between devices  11.3 us (27%)
  Pallas kernels  6.06 us (15%)
  local copies, waits for them, and re-layouts  0.95 us (2%)
  between operations  0.85 us (2%)
    ppermute x14, starting transfers between devices, swapped(): return lax.ppermute(value, axis, [(i, i ^ bit) for i in range(count)])  22 us
    ppermute x14, waiting for transfers between devices, swapped(): return lax.ppermute(value, axis, [(i, i ^ bit) for i in range(count)])  11.3 us
    pallas_call x17, Pallas kernels, call(): pl.pallas_call(kernel, out_shape=list(outs), in_specs=[HBM if i in far_in...  6.06 us
    unnamed x20, local copies, waits for them, and re-layouts  0.95 us
  transfers between devices with their start and end apart: 14, of which 9 were waited for; matrix products, arithmetic and copies ran while one was open for 0% of the time, Pallas kernels for 12%

profile of v9, /device:TPU:0, one launch (start us, length us, event | category | flops | bytes accessed | tf_op | source)
XLA Modules:
  0.0 41.1 jit_solution(6357331111218631471)
XLA Ops:
  0.7 0.6 %copy-done.6 = s32[1,128,8]{1,2,0:T(8,128)S(1)} copy-done((s32[1,128,8]{1,2,0:T(8,128)S(1)}, s32[1,128,8]{1,2,0:T(8,128)}, u32[]{:S(2)}) %copy-start.6) | copy-done | bytes 4120
  1.3 0.1 shard_map.114.chosen_ref
  1.5 0.2 copy-done.9
  1.7 0.1 shard_map.116.after_ref
  1.9 4.1 %collective-permute-start = (bf16[40,512]{1,0:T(8,128)(2,1)S(1)}, bf16[40,512]{1,0:T(8,128)(2,1)S(1)}, u32[]{:S(2)}, u32[]{:S(2)}) collective-permute-start(bf16[40,512]{1,0:T(8,128)(2,1)S(1)} %shard_map.116.after_ref), channel_id=1, source_target_pairs={{0,8},{4,12},{8,0},{12,4},{1,9},{5,13},{9,1},{13,5},{2,10},{6,14},... | collective-permute-start | bytes 122888 | tf_op jit(solution)/shard_map/ppermute | solution.py:21
  6.0 0.1 shard_map.115.refs_0_
  6.2 0.1 shard_map.117.held_ref
  6.3 2.1 %collective-permute-done.refs_1_ = bf16[40,512]{1,0:T(8,128)(2,1)S(1)} collective-permute-done((bf16[40,512]{1,0:T(8,128)(2,1)S(1)}, bf16[40,512]{1,0:T(8,128)(2,1)S(1)}, u32[]{:S(2)}, u32[]{:S(2)}) %collective-permute-start) | collective-permute-done | bytes 40992 | tf_op jit(solution)/shard_map/ppermute | solution.py:21
  8.4 2.5 %collective-permute-start.3 = (bf16[40,512]{1,0:T(8,128)(2,1)S(1)}, bf16[40,512]{1,0:T(8,128)(2,1)S(1)}, u32[]{:S(2)}, u32[]{:S(2)}) collective-permute-start(bf16[40,512]{1,0:T(8,128)(2,1)S(1)} %get-tuple-element.24), channel_id=1, source_target_pairs={{0,6},{2,4},{4,2},{6,0},{8,14},{10,12},{12,10},{14,8},{1,7},{3,5},... | collective-permute-start | bytes 122888 | tf_op jit(solution)/shard_map/ppermute | solution.py:21
  10.9 0.8 %collective-permute-start.2 = (bf16[40,512]{1,0:T(8,128)(2,1)S(1)}, bf16[40,512]{1,0:T(8,128)(2,1)S(1)}, u32[]{:S(2)}, u32[]{:S(2)}) collective-permute-start(bf16[40,512]{1,0:T(8,128)(2,1)S(1)} %get-tuple-element.24), channel_id=1, source_target_pairs={{0,4},{2,6},{4,0},{6,2},{8,12},{10,14},{12,8},{14,10},{1,5},{3,7},... | collective-permute-start | bytes 122888 | tf_op jit(solution)/shard_map/ppermute | solution.py:21
  11.7 0.3 collective-permute-start.1
  12.0 2.5 %collective-permute-start.8 = (bf16[1,272,128]{2,1,0:T(8,128)(2,1)S(1)}, bf16[1,272,128]{2,1,0:T(8,128)(2,1)S(1)}, u32[]{:S(2)}, u32[]{:S(2)}) collective-permute-start(bf16[1,272,128]{2,1,0:T(8,128)(2,1)S(1)} %shard_map.117.held_ref), channel_id=1, source_target_pairs={{0,8},{4,12},{8,0},{12,4},{1,9},{5,13},{9,1},{13,5},{2,10},{6,14},... | collective-permute-start | bytes 208904 | tf_op jit(solution)/shard_map/ppermute | solution.py:21
  14.5 0.4 collective-permute-done.2.refs_2_
  14.9 0.8 %collective-permute-done.1.refs_1_ = bf16[40,512]{1,0:T(8,128)(2,1)S(1)} collective-permute-done((bf16[40,512]{1,0:T(8,128)(2,1)S(1)}, bf16[40,512]{1,0:T(8,128)(2,1)S(1)}, u32[]{:S(2)}, u32[]{:S(2)}) %collective-permute-start.1) | collective-permute-done | bytes 40992 | tf_op jit(solution)/shard_map/ppermute | solution.py:21
  15.7 0.7 %shard_map.119 = (bf16[40,768]{1,0:T(8,128)(2,1)S(1)}, f32[40,768]{1,0:T(8,128)S(1)}, bf16[40,768]{1,0:T(8,128)(2,1)S(1)}, f32[40,768]{1,0:T(8,128)S(1)}) custom-call(bf16[40,512]{1,0:T(8,128)(2,1)S(1)} %get-tuple-element.23.refs_0_, bf16[40,512]{1,0:T(8,128)(2,1)S(1)} %collective-permute-done.1.refs_1_, bf16[40,512]{1,0:T(8,128)(2,1)S(1)} %collective-permute-done.2.refs_2_, ...), custom_call_target="tpu_custom_call" | custom-call | tf_op jit(solution)/shard_map/pallas_call | solution.py:32
  16.4 0.5 %collective-permute-start.5 = (bf16[40,768]{1,0:T(8,128)(2,1)S(1)}, bf16[40,768]{1,0:T(8,128)(2,1)S(1)}, u32[]{:S(2)}, u32[]{:S(2)}) collective-permute-start(bf16[40,768]{1,0:T(8,128)(2,1)S(1)} %get-tuple-element.28), channel_id=1, source_target_pairs={{0,1},{1,0},{2,3},{3,2},{4,5},{5,4},{6,7},{7,6},{8,9},{9,8},{10,11... | collective-permute-start | bytes 184328 | tf_op jit(solution)/shard_map/ppermute | solution.py:21
  16.9 0.7 %collective-permute-done.4.gate_received_ref = bf16[40,768]{1,0:T(8,128)(2,1)S(1)} collective-permute-done((bf16[40,768]{1,0:T(8,128)(2,1)S(1)}, bf16[40,768]{1,0:T(8,128)(2,1)S(1)}, u32[]{:S(2)}, u32[]{:S(2)}) %collective-permute-start.4) | collective-permute-done | bytes 61472 | tf_op jit(solution)/shard_map/ppermute | solution.py:21
  17.6 0.2 collective-permute-done.5.up_received_ref
  17.9 2.4 %collective-permute-start.6 = (bf16[40,1536]{1,0:T(8,128)(2,1)S(1)}, bf16[40,1536]{1,0:T(8,128)(2,1)S(1)}, u32[]{:S(2)}, u32[]{:S(2)}) collective-permute-start(bf16[40,1536]{1,0:T(8,128)(2,1)S(1)} %get-tuple-element.30.after_ref), channel_id=1, source_target_pairs={{0,8},{4,12},{8,0},{12,4},{1,9},{5,13},{9,1},{13,5},{2,10},{6,14},... | collective-permute-start | bytes 368648 | tf_op jit(solution)/shard_map/ppermute | solution.py:21
  20.3 1.9 %collective-permute-start.9 = (bf16[2,272,128]{2,1,0:T(8,128)(2,1)S(1)}, bf16[2,272,128]{2,1,0:T(8,128)(2,1)S(1)}, u32[]{:S(2)}, u32[]{:S(2)}) collective-permute-start(bf16[2,272,128]{2,1,0:T(8,128)(2,1)S(1)} %shard_map.123.held_ref), channel_id=1, source_target_pairs={{0,4},{4,0},{8,12},{12,8},{1,5},{5,1},{9,13},{13,9},{2,6},{6,2},{1... | collective-permute-start | bytes 417800 | tf_op jit(solution)/shard_map/ppermute | solution.py:21
  22.2 4.9 %collective-permute-done.6.received_ref = bf16[40,1536]{1,0:T(8,128)(2,1)S(1)} collective-permute-done((bf16[40,1536]{1,0:T(8,128)(2,1)S(1)}, bf16[40,1536]{1,0:T(8,128)(2,1)S(1)}, u32[]{:S(2)}, u32[]{:S(2)}) %collective-permute-start.6) | collective-permute-done | bytes 122912 | tf_op jit(solution)/shard_map/ppermute | solution.py:21
  27.3 1.2 %collective-permute-done.7.received_ref = bf16[40,768]{1,0:T(8,128)(2,1)S(1)} collective-permute-done((bf16[40,768]{1,0:T(8,128)(2,1)S(1)}, bf16[40,768]{1,0:T(8,128)(2,1)S(1)}, u32[]{:S(2)}, u32[]{:S(2)}) %collective-permute-start.7) | collective-permute-done | bytes 61472 | tf_op jit(solution)/shard_map/ppermute | solution.py:21
  28.5 0.4 %shard_map.122 = (f32[40,512]{1,0:T(8,128)S(1)}, bf16[40,512]{1,0:T(8,128)(2,1)S(1)}, bf16[40,512]{1,0:T(8,128)(2,1)S(1)}, bf16[40,512]{1,0:T(8,128)(2,1)S(1)}) custom-call(bf16[40,768]{1,0:T(8,128)(2,1)S(1)} %shard_map.121.hidden_ref, bf16[40,768]{1,0:T(8,128)(2,1)S(1)} %collective-permute-done.7.received_ref, bf16[768,1024]{1,0:T(8,128)(2,1)S(1)} %bitcast.17), custom_call_target="tpu_custom_call" | custom-call | flops 125829120 | bytes 1900544 | tf_op jit(solution)/shard_map/pallas_call | solution.py:32
  28.9 0.5 %collective-permute-start.10 = (bf16[40,512]{1,0:T(8,128)(2,1)S(1)}, bf16[40,512]{1,0:T(8,128)(2,1)S(1)}, u32[]{:S(2)}, u32[]{:S(2)}) collective-permute-start(bf16[40,512]{1,0:T(8,128)(2,1)S(1)} %get-tuple-element.38), channel_id=1, source_target_pairs={{0,2},{2,0},{4,6},{6,4},{8,10},{10,8},{12,14},{14,12},{1,3},{3,1},... | collective-permute-start | bytes 122888 | tf_op jit(solution)/shard_map/ppermute | solution.py:21
  29.4 1.3 %collective-permute-start.12 = (bf16[40,512]{1,0:T(8,128)(2,1)S(1)}, bf16[40,512]{1,0:T(8,128)(2,1)S(1)}, u32[]{:S(2)}, u32[]{:S(2)}) collective-permute-start(bf16[40,512]{1,0:T(8,128)(2,1)S(1)} %get-tuple-element.39), channel_id=1, source_target_pairs={{0,6},{2,4},{4,2},{6,0},{8,14},{10,12},{12,10},{14,8},{1,7},{3,5},... | collective-permute-start | bytes 122888 | tf_op jit(solution)/shard_map/ppermute | solution.py:21
  30.8 1.7 %collective-permute-start.11 = (bf16[40,512]{1,0:T(8,128)(2,1)S(1)}, bf16[40,512]{1,0:T(8,128)(2,1)S(1)}, u32[]{:S(2)}, u32[]{:S(2)}) collective-permute-start(bf16[40,512]{1,0:T(8,128)(2,1)S(1)} %get-tuple-element.34), channel_id=1, source_target_pairs={{0,4},{2,6},{4,0},{6,2},{8,12},{10,14},{12,8},{14,10},{1,5},{3,7},... | collective-permute-start | bytes 122888 | tf_op jit(solution)/shard_map/ppermute | solution.py:21
  32.5 2.2 %shard_map.125 = bf16[128,2048]{1,0:T(8,128)(2,1)} custom-call(bf16[128,2048]{1,0:T(8,128)(2,1)S(1)} %bitcast.18, bf16[4,272,128]{2,1,0:T(8,128)(2,1)S(1)} %shard_map.124.held_ref, s32[1,128]{1,0:T(1,128)S(1)} %copy-done.8), custom_call_target="tpu_custom_call" | custom-call | tf_op jit(solution)/shard_map/pallas_call | solution.py:32
  34.9 3.3 %collective-permute-start.13 = (bf16[40,512]{1,0:T(8,128)(2,1)S(1)}, bf16[40,512]{1,0:T(8,128)(2,1)S(1)}, u32[]{:S(2)}, u32[]{:S(2)}) collective-permute-start(bf16[40,512]{1,0:T(8,128)(2,1)S(1)} %get-tuple-element.40), channel_id=1, source_target_pairs={{0,8},{4,12},{8,0},{12,4},{1,9},{5,13},{9,1},{13,5},{2,10},{6,14},... | collective-permute-start | bytes 122888 | tf_op jit(solution)/shard_map/ppermute | solution.py:21
  38.2 0.2 shard_map.126.share_ref
  38.5 0.9 %shard_map.128.refs_0_ = bf16[128,2048]{1,0:T(8,128)(2,1)} custom-call(bf16[2,128,40]{2,1,0:T(8,128)(2,1)S(1)} %shard_map.126.share_ref, bf16[40,512]{1,0:T(8,128)(2,1)S(1)} %get-tuple-element.41.rows_ref), custom_call_target="tpu_custom_call" | custom-call | flops 20971520 | bytes 585728 | tf_op jit(solution)/shard_map/pallas_call | solution.py:32
  39.4 0.8 %collective-permute-done.13.rows_ref = bf16[40,512]{1,0:T(8,128)(2,1)S(1)} collective-permute-done((bf16[40,512]{1,0:T(8,128)(2,1)S(1)}, bf16[40,512]{1,0:T(8,128)(2,1)S(1)}, u32[]{:S(2)}, u32[]{:S(2)}) %collective-permute-start.13) | collective-permute-done | bytes 40992 | tf_op jit(solution)/shard_map/ppermute | solution.py:21
  40.2 0.9 %shard_map.129 = bf16[128,2048]{1,0:T(8,128)(2,1)} custom-call(bf16[2,128,40]{2,1,0:T(8,128)(2,1)S(1)} %shard_map.126.share_ref, bf16[40,512]{1,0:T(8,128)(2,1)S(1)} %collective-permute-done.13.rows_ref, bf16[128,2048]{1,0:T(8,128)(2,1)} %shard_map.128.refs_0_), custom_call_target="tpu_custom_call", output_to_operand_aliasing={{}: (2, {})} | custom-call | flops 20971520 | bytes 1110016 | tf_op jit(solution)/shard_map/pallas_call | solution.py:32
  (33 shorter events, 0.5 us)
Async XLA Ops:
  0.6 0.7 %copy-start.6 = (s32[1,128,8]{1,2,0:T(8,128)S(1)}, s32[1,128,8]{1,2,0:T(8,128)}, u32[]{:S(2)}) copy-start(s32[1,128,8]{1,2,0:T(8,128)} %param.15) | copy-start | bytes 12292
  0.6 1.0 %copy-start.9 = (bf16[1,128,2048]{2,1,0:T(8,128)(2,1)S(1)}, bf16[1,128,2048]{2,1,0:T(8,128)(2,1)}, u32[]{:S(2)}) copy-start(bf16[1,128,2048]{2,1,0:T(8,128)(2,1)} %param.14) | copy-start | bytes 1572868
  1.8 4.3 %copy-start.4 = (bf16[1,128,128]{2,1,0:T(8,128)(2,1)S(1)}, bf16[1,128,128]{2,1,0:T(8,128)(2,1)}, u32[]{:S(2)}) copy-start(bf16[1,128,128]{2,1,0:T(8,128)(2,1)} %param.11) | copy-start | bytes 98308
  1.9 4.3 %copy-start.5 = (bf16[1,128,128]{2,1,0:T(8,128)(2,1)S(1)}, bf16[1,128,128]{2,1,0:T(8,128)(2,1)}, u32[]{:S(2)}) copy-start(bf16[1,128,128]{2,1,0:T(8,128)(2,1)} %param.12) | copy-start | bytes 98308
  1.9 4.3 %copy-start.8 = (s32[1,128]{1,0:T(1,128)S(1)}, s32[1,128]{1,0:T(1,128)}, u32[]{:S(2)}) copy-start(s32[1,128]{1,0:T(1,128)} %segment_ref.2) | copy-start | bytes 1540
  1.9 6.5 %collective-permute-start = (bf16[40,512]{1,0:T(8,128)(2,1)S(1)}, bf16[40,512]{1,0:T(8,128)(2,1)S(1)}, u32[]{:S(2)}, u32[]{:S(2)}) collective-permute-start(bf16[40,512]{1,0:T(8,128)(2,1)S(1)} %shard_map.116.after_ref), channel_id=1, source_target_pairs={{0,8},{4,12},{8,0},{12,4},{1,9},{5,13},{9,1},{13,5},{2,10},{6,14},... | collective-permute-start | bytes 122888 | tf_op jit(solution)/shard_map/ppermute | solution.py:21
  6.3 9.3 %copy-start = (bf16[1,1024,768]{2,1,0:T(8,128)(2,1)S(1)}, bf16[1,1024,768]{2,1,0:T(8,128)(2,1)}, u32[]{:S(2)}) copy-start(bf16[1,1024,768]{2,1,0:T(8,128)(2,1)} %param.17) | copy-start | bytes 4718596
  6.3 9.3 %copy-start.1 = (bf16[1,1024,768]{2,1,0:T(8,128)(2,1)S(1)}, bf16[1,1024,768]{2,1,0:T(8,128)(2,1)}, u32[]{:S(2)}) copy-start(bf16[1,1024,768]{2,1,0:T(8,128)(2,1)} %param.18) | copy-start | bytes 4718596
  8.4 6.1 %collective-permute-start.3 = (bf16[40,512]{1,0:T(8,128)(2,1)S(1)}, bf16[40,512]{1,0:T(8,128)(2,1)S(1)}, u32[]{:S(2)}, u32[]{:S(2)}) collective-permute-start(bf16[40,512]{1,0:T(8,128)(2,1)S(1)} %get-tuple-element.24), channel_id=1, source_target_pairs={{0,6},{2,4},{4,2},{6,0},{8,14},{10,12},{12,10},{14,8},{1,7},{3,5},... | collective-permute-start | bytes 122888 | tf_op jit(solution)/shard_map/ppermute | solution.py:21
  10.9 4.0 %collective-permute-start.2 = (bf16[40,512]{1,0:T(8,128)(2,1)S(1)}, bf16[40,512]{1,0:T(8,128)(2,1)S(1)}, u32[]{:S(2)}, u32[]{:S(2)}) collective-permute-start(bf16[40,512]{1,0:T(8,128)(2,1)S(1)} %get-tuple-element.24), channel_id=1, source_target_pairs={{0,4},{2,6},{4,0},{6,2},{8,12},{10,14},{12,8},{14,10},{1,5},{3,7},... | collective-permute-start | bytes 122888 | tf_op jit(solution)/shard_map/ppermute | solution.py:21
  11.7 4.0 %collective-permute-start.1 = (bf16[40,512]{1,0:T(8,128)(2,1)S(1)}, bf16[40,512]{1,0:T(8,128)(2,1)S(1)}, u32[]{:S(2)}, u32[]{:S(2)}) collective-permute-start(bf16[40,512]{1,0:T(8,128)(2,1)S(1)} %get-tuple-element.23.refs_0_), channel_id=1, source_target_pairs={{0,2},{2,0},{4,6},{6,4},{8,10},{10,8},{12,14},{14,12},{1,3},{3,1},... | collective-permute-start | bytes 122888 | tf_op jit(solution)/shard_map/ppermute | solution.py:21
  12.0 8.2 %collective-permute-start.8 = (bf16[1,272,128]{2,1,0:T(8,128)(2,1)S(1)}, bf16[1,272,128]{2,1,0:T(8,128)(2,1)S(1)}, u32[]{:S(2)}, u32[]{:S(2)}) collective-permute-start(bf16[1,272,128]{2,1,0:T(8,128)(2,1)S(1)} %shard_map.117.held_ref), channel_id=1, source_target_pairs={{0,8},{4,12},{8,0},{12,4},{1,9},{5,13},{9,1},{13,5},{2,10},{6,14},... | collective-permute-start | bytes 208904 | tf_op jit(solution)/shard_map/ppermute | solution.py:21
  16.3 1.3 %collective-permute-start.4 = (bf16[40,768]{1,0:T(8,128)(2,1)S(1)}, bf16[40,768]{1,0:T(8,128)(2,1)S(1)}, u32[]{:S(2)}, u32[]{:S(2)}) collective-permute-start(bf16[40,768]{1,0:T(8,128)(2,1)S(1)} %get-tuple-element.26), channel_id=1, source_target_pairs={{0,1},{1,0},{2,3},{3,2},{4,5},{5,4},{6,7},{7,6},{8,9},{9,8},{10,11... | collective-permute-start | bytes 184328 | tf_op jit(solution)/shard_map/ppermute | solution.py:21
  16.4 1.4 %collective-permute-start.5 = (bf16[40,768]{1,0:T(8,128)(2,1)S(1)}, bf16[40,768]{1,0:T(8,128)(2,1)S(1)}, u32[]{:S(2)}, u32[]{:S(2)}) collective-permute-start(bf16[40,768]{1,0:T(8,128)(2,1)S(1)} %get-tuple-element.28), channel_id=1, source_target_pairs={{0,1},{1,0},{2,3},{3,2},{4,5},{5,4},{6,7},{7,6},{8,9},{9,8},{10,11... | collective-permute-start | bytes 184328 | tf_op jit(solution)/shard_map/ppermute | solution.py:21
  17.8 10.7 %copy-start.2 = (bf16[1,768,1024]{2,1,0:T(8,128)(2,1)S(1)}, bf16[1,768,1024]{2,1,0:T(8,128)(2,1)}, u32[]{:S(2)}) copy-start(bf16[1,768,1024]{2,1,0:T(8,128)(2,1)} %param.19) | copy-start | bytes 4718596
  17.9 9.3 %collective-permute-start.6 = (bf16[40,1536]{1,0:T(8,128)(2,1)S(1)}, bf16[40,1536]{1,0:T(8,128)(2,1)S(1)}, u32[]{:S(2)}, u32[]{:S(2)}) collective-permute-start(bf16[40,1536]{1,0:T(8,128)(2,1)S(1)} %get-tuple-element.30.after_ref), channel_id=1, source_target_pairs={{0,8},{4,12},{8,0},{12,4},{1,9},{5,13},{9,1},{13,5},{2,10},{6,14},... | collective-permute-start | bytes 368648 | tf_op jit(solution)/shard_map/ppermute | solution.py:21
  20.2 12.3 %copy-start.3 = (bf16[1,128,2048]{2,1,0:T(8,128)(2,1)S(1)}, bf16[1,128,2048]{2,1,0:T(8,128)(2,1)}, u32[]{:S(2)}) copy-start(bf16[1,128,2048]{2,1,0:T(8,128)(2,1)} %param.10) | copy-start | bytes 1572868
  20.3 12.2 %collective-permute-start.9 = (bf16[2,272,128]{2,1,0:T(8,128)(2,1)S(1)}, bf16[2,272,128]{2,1,0:T(8,128)(2,1)S(1)}, u32[]{:S(2)}, u32[]{:S(2)}) collective-permute-start(bf16[2,272,128]{2,1,0:T(8,128)(2,1)S(1)} %shard_map.123.held_ref), channel_id=1, source_target_pairs={{0,4},{4,0},{8,12},{12,8},{1,5},{5,1},{9,13},{13,9},{2,6},{6,2},{1... | collective-permute-start | bytes 417800 | tf_op jit(solution)/shard_map/ppermute | solution.py:21
  27.2 1.3 %collective-permute-start.7 = (bf16[40,768]{1,0:T(8,128)(2,1)S(1)}, bf16[40,768]{1,0:T(8,128)(2,1)S(1)}, u32[]{:S(2)}, u32[]{:S(2)}) collective-permute-start(bf16[40,768]{1,0:T(8,128)(2,1)S(1)} %shard_map.121.hidden_ref), channel_id=1, source_target_pairs={{0,1},{1,0},{2,3},{3,2},{4,5},{5,4},{6,7},{7,6},{8,9},{9,8},{10,11... | collective-permute-start | bytes 184328 | tf_op jit(solution)/shard_map/ppermute | solution.py:21
  28.5 9.7 %copy-start.7 = (f32[1,128,8]{1,2,0:T(8,128)S(1)}, f32[1,128,8]{1,2,0:T(8,128)}, u32[]{:S(2)}) copy-start(f32[1,128,8]{1,2,0:T(8,128)} %param.16) | copy-start | bytes 12292
  28.9 5.8 %collective-permute-start.10 = (bf16[40,512]{1,0:T(8,128)(2,1)S(1)}, bf16[40,512]{1,0:T(8,128)(2,1)S(1)}, u32[]{:S(2)}, u32[]{:S(2)}) collective-permute-start(bf16[40,512]{1,0:T(8,128)(2,1)S(1)} %get-tuple-element.38), channel_id=1, source_target_pairs={{0,2},{2,0},{4,6},{6,4},{8,10},{10,8},{12,14},{14,12},{1,3},{3,1},... | collective-permute-start | bytes 122888 | tf_op jit(solution)/shard_map/ppermute | solution.py:21
  29.4 5.3 %collective-permute-start.12 = (bf16[40,512]{1,0:T(8,128)(2,1)S(1)}, bf16[40,512]{1,0:T(8,128)(2,1)S(1)}, u32[]{:S(2)}, u32[]{:S(2)}) collective-permute-start(bf16[40,512]{1,0:T(8,128)(2,1)S(1)} %get-tuple-element.39), channel_id=1, source_target_pairs={{0,6},{2,4},{4,2},{6,0},{8,14},{10,12},{12,10},{14,8},{1,7},{3,5},... | collective-permute-start | bytes 122888 | tf_op jit(solution)/shard_map/ppermute | solution.py:21
  30.8 4.1 %collective-permute-start.11 = (bf16[40,512]{1,0:T(8,128)(2,1)S(1)}, bf16[40,512]{1,0:T(8,128)(2,1)S(1)}, u32[]{:S(2)}, u32[]{:S(2)}) collective-permute-start(bf16[40,512]{1,0:T(8,128)(2,1)S(1)} %get-tuple-element.34), channel_id=1, source_target_pairs={{0,4},{2,6},{4,0},{6,2},{8,12},{10,14},{12,8},{14,10},{1,5},{3,7},... | collective-permute-start | bytes 122888 | tf_op jit(solution)/shard_map/ppermute | solution.py:21
  34.9 5.3 %collective-permute-start.13 = (bf16[40,512]{1,0:T(8,128)(2,1)S(1)}, bf16[40,512]{1,0:T(8,128)(2,1)S(1)}, u32[]{:S(2)}, u32[]{:S(2)}) collective-permute-start(bf16[40,512]{1,0:T(8,128)(2,1)S(1)} %get-tuple-element.40), channel_id=1, source_target_pairs={{0,8},{4,12},{8,0},{12,4},{1,9},{5,13},{9,1},{13,5},{2,10},{6,14},... | collective-permute-start | bytes 122888 | tf_op jit(solution)/shard_map/ppermute | solution.py:21

commit v10 on v8

--- a/solution.py
+++ b/solution.py
@@ -433,7 +433,7 @@
         semaphores=heads // batch,
         far_out=(0,),
     )
-    own[0], attended = lax.optimization_barrier((own[0], attended))
+    own, other, attended = lax.optimization_barrier((own, other, attended))
 
     def add_parts(*refs):
         sums = []

time: 41.3 us -> 41.3 us (level)
  no operation moved by 1% of the time
where the time goes in v10:
time: 41.3 us; the launch traced here: 41.1 us
  starting transfers between devices  22 us (53%)
  waiting for transfers between devices  11.3 us (27%)
  Pallas kernels  6.09 us (15%)
  local copies, waits for them, and re-layouts  0.95 us (2%)
  between operations  0.85 us (2%)
    ppermute x14, starting transfers between devices, swapped(): return lax.ppermute(value, axis, [(i, i ^ bit) for i in range(count)])  22 us
    ppermute x14, waiting for transfers between devices, swapped(): return lax.ppermute(value, axis, [(i, i ^ bit) for i in range(count)])  11.3 us
    pallas_call x17, Pallas kernels, call(): pl.pallas_call(kernel, out_shape=list(outs), in_specs=[HBM if i in far_in...  6.09 us
    unnamed x20, local copies, waits for them, and re-layouts  0.95 us
  transfers between devices with their start and end apart: 14, of which 9 were waited for; matrix products, arithmetic and copies ran while one was open for 0% of the time, Pallas kernels for 12%

profile of v10, /device:TPU:0, one launch (start us, length us, event | category | flops | bytes accessed | tf_op | source)
XLA Modules:
  0.0 41.1 jit_solution(13402199446334297995)
XLA Ops:
  0.7 0.6 %copy-done.6 = s32[1,128,8]{1,2,0:T(8,128)S(1)} copy-done((s32[1,128,8]{1,2,0:T(8,128)S(1)}, s32[1,128,8]{1,2,0:T(8,128)}, u32[]{:S(2)}) %copy-start.6) | copy-done | bytes 4120
  1.3 0.1 shard_map.114.chosen_ref
  1.5 0.2 copy-done.9
  1.7 0.1 shard_map.116.after_ref
  1.9 4.1 %collective-permute-start = (bf16[40,512]{1,0:T(8,128)(2,1)S(1)}, bf16[40,512]{1,0:T(8,128)(2,1)S(1)}, u32[]{:S(2)}, u32[]{:S(2)}) collective-permute-start(bf16[40,512]{1,0:T(8,128)(2,1)S(1)} %shard_map.116.after_ref), channel_id=1, source_target_pairs={{0,8},{4,12},{8,0},{12,4},{1,9},{5,13},{9,1},{13,5},{2,10},{6,14},... | collective-permute-start | bytes 122888 | tf_op jit(solution)/shard_map/ppermute | solution.py:21
  6.0 0.1 shard_map.115.refs_0_
  6.2 0.1 shard_map.117.held_ref
  6.3 2.1 %collective-permute-done.refs_1_ = bf16[40,512]{1,0:T(8,128)(2,1)S(1)} collective-permute-done((bf16[40,512]{1,0:T(8,128)(2,1)S(1)}, bf16[40,512]{1,0:T(8,128)(2,1)S(1)}, u32[]{:S(2)}, u32[]{:S(2)}) %collective-permute-start) | collective-permute-done | bytes 40992 | tf_op jit(solution)/shard_map/ppermute | solution.py:21
  8.4 2.5 %collective-permute-start.3 = (bf16[40,512]{1,0:T(8,128)(2,1)S(1)}, bf16[40,512]{1,0:T(8,128)(2,1)S(1)}, u32[]{:S(2)}, u32[]{:S(2)}) collective-permute-start(bf16[40,512]{1,0:T(8,128)(2,1)S(1)} %get-tuple-element.27), channel_id=1, source_target_pairs={{0,6},{2,4},{4,2},{6,0},{8,14},{10,12},{12,10},{14,8},{1,7},{3,5},... | collective-permute-start | bytes 122888 | tf_op jit(solution)/shard_map/ppermute | solution.py:21
  10.9 0.8 %collective-permute-start.2 = (bf16[40,512]{1,0:T(8,128)(2,1)S(1)}, bf16[40,512]{1,0:T(8,128)(2,1)S(1)}, u32[]{:S(2)}, u32[]{:S(2)}) collective-permute-start(bf16[40,512]{1,0:T(8,128)(2,1)S(1)} %get-tuple-element.27), channel_id=1, source_target_pairs={{0,4},{2,6},{4,0},{6,2},{8,12},{10,14},{12,8},{14,10},{1,5},{3,7},... | collective-permute-start | bytes 122888 | tf_op jit(solution)/shard_map/ppermute | solution.py:21
  11.7 0.3 collective-permute-start.1
  12.0 2.5 %collective-permute-start.11 = (bf16[1,272,128]{2,1,0:T(8,128)(2,1)S(1)}, bf16[1,272,128]{2,1,0:T(8,128)(2,1)S(1)}, u32[]{:S(2)}, u32[]{:S(2)}) collective-permute-start(bf16[1,272,128]{2,1,0:T(8,128)(2,1)S(1)} %shard_map.117.held_ref), channel_id=1, source_target_pairs={{0,8},{4,12},{8,0},{12,4},{1,9},{5,13},{9,1},{13,5},{2,10},{6,14},... | collective-permute-start | bytes 208904 | tf_op jit(solution)/shard_map/ppermute | solution.py:21
  14.5 0.4 collective-permute-done.2.refs_2_
  14.9 0.8 %collective-permute-done.1.refs_1_ = bf16[40,512]{1,0:T(8,128)(2,1)S(1)} collective-permute-done((bf16[40,512]{1,0:T(8,128)(2,1)S(1)}, bf16[40,512]{1,0:T(8,128)(2,1)S(1)}, u32[]{:S(2)}, u32[]{:S(2)}) %collective-permute-start.1) | collective-permute-done | bytes 40992 | tf_op jit(solution)/shard_map/ppermute | solution.py:21
  15.7 0.7 %shard_map.119 = (bf16[40,768]{1,0:T(8,128)(2,1)S(1)}, f32[40,768]{1,0:T(8,128)S(1)}, bf16[40,768]{1,0:T(8,128)(2,1)S(1)}, f32[40,768]{1,0:T(8,128)S(1)}) custom-call(bf16[40,512]{1,0:T(8,128)(2,1)S(1)} %get-tuple-element.26.refs_0_, bf16[40,512]{1,0:T(8,128)(2,1)S(1)} %collective-permute-done.1.refs_1_, bf16[40,512]{1,0:T(8,128)(2,1)S(1)} %collective-permute-done.2.refs_2_, ...), custom_call_target="tpu_custom_call" | custom-call | tf_op jit(solution)/shard_map/pallas_call | solution.py:32
  16.4 0.5 %collective-permute-start.5 = (bf16[40,768]{1,0:T(8,128)(2,1)S(1)}, bf16[40,768]{1,0:T(8,128)(2,1)S(1)}, u32[]{:S(2)}, u32[]{:S(2)}) collective-permute-start(bf16[40,768]{1,0:T(8,128)(2,1)S(1)} %get-tuple-element.31), channel_id=1, source_target_pairs={{0,1},{1,0},{2,3},{3,2},{4,5},{5,4},{6,7},{7,6},{8,9},{9,8},{10,11... | collective-permute-start | bytes 184328 | tf_op jit(solution)/shard_map/ppermute | solution.py:21
  16.9 0.7 %collective-permute-done.4.gate_received_ref = bf16[40,768]{1,0:T(8,128)(2,1)S(1)} collective-permute-done((bf16[40,768]{1,0:T(8,128)(2,1)S(1)}, bf16[40,768]{1,0:T(8,128)(2,1)S(1)}, u32[]{:S(2)}, u32[]{:S(2)}) %collective-permute-start.4) | collective-permute-done | bytes 61472 | tf_op jit(solution)/shard_map/ppermute | solution.py:21
  17.6 0.2 collective-permute-done.5.up_received_ref
  17.9 2.4 %collective-permute-start.6 = (bf16[40,1536]{1,0:T(8,128)(2,1)S(1)}, bf16[40,1536]{1,0:T(8,128)(2,1)S(1)}, u32[]{:S(2)}, u32[]{:S(2)}) collective-permute-start(bf16[40,1536]{1,0:T(8,128)(2,1)S(1)} %get-tuple-element.33.after_ref), channel_id=1, source_target_pairs={{0,8},{4,12},{8,0},{12,4},{1,9},{5,13},{9,1},{13,5},{2,10},{6,14},... | collective-permute-start | bytes 368648 | tf_op jit(solution)/shard_map/ppermute | solution.py:21
  20.3 1.9 %collective-permute-start.12 = (bf16[2,272,128]{2,1,0:T(8,128)(2,1)S(1)}, bf16[2,272,128]{2,1,0:T(8,128)(2,1)S(1)}, u32[]{:S(2)}, u32[]{:S(2)}) collective-permute-start(bf16[2,272,128]{2,1,0:T(8,128)(2,1)S(1)} %shard_map.123.held_ref), channel_id=1, source_target_pairs={{0,4},{4,0},{8,12},{12,8},{1,5},{5,1},{9,13},{13,9},{2,6},{6,2},{1... | collective-permute-start | bytes 417800 | tf_op jit(solution)/shard_map/ppermute | solution.py:21
  22.2 4.9 %collective-permute-done.6.received_ref = bf16[40,1536]{1,0:T(8,128)(2,1)S(1)} collective-permute-done((bf16[40,1536]{1,0:T(8,128)(2,1)S(1)}, bf16[40,1536]{1,0:T(8,128)(2,1)S(1)}, u32[]{:S(2)}, u32[]{:S(2)}) %collective-permute-start.6) | collective-permute-done | bytes 122912 | tf_op jit(solution)/shard_map/ppermute | solution.py:21
  27.3 1.2 %collective-permute-done.7.received_ref = bf16[40,768]{1,0:T(8,128)(2,1)S(1)} collective-permute-done((bf16[40,768]{1,0:T(8,128)(2,1)S(1)}, bf16[40,768]{1,0:T(8,128)(2,1)S(1)}, u32[]{:S(2)}, u32[]{:S(2)}) %collective-permute-start.7) | collective-permute-done | bytes 61472 | tf_op jit(solution)/shard_map/ppermute | solution.py:21
  28.5 0.4 %shard_map.122 = (f32[40,512]{1,0:T(8,128)S(1)}, bf16[40,512]{1,0:T(8,128)(2,1)S(1)}, bf16[40,512]{1,0:T(8,128)(2,1)S(1)}, bf16[40,512]{1,0:T(8,128)(2,1)S(1)}) custom-call(bf16[40,768]{1,0:T(8,128)(2,1)S(1)} %shard_map.121.hidden_ref, bf16[40,768]{1,0:T(8,128)(2,1)S(1)} %collective-permute-done.7.received_ref, bf16[768,1024]{1,0:T(8,128)(2,1)S(1)} %bitcast.17), custom_call_target="tpu_custom_call" | custom-call | flops 125829120 | bytes 1900544 | tf_op jit(solution)/shard_map/pallas_call | solution.py:32
  28.9 0.5 %collective-permute-start.8 = (bf16[40,512]{1,0:T(8,128)(2,1)S(1)}, bf16[40,512]{1,0:T(8,128)(2,1)S(1)}, u32[]{:S(2)}, u32[]{:S(2)}) collective-permute-start(bf16[40,512]{1,0:T(8,128)(2,1)S(1)} %get-tuple-element.35), channel_id=1, source_target_pairs={{0,2},{2,0},{4,6},{6,4},{8,10},{10,8},{12,14},{14,12},{1,3},{3,1},... | collective-permute-start | bytes 122888 | tf_op jit(solution)/shard_map/ppermute | solution.py:21
  29.4 1.3 %collective-permute-start.10 = (bf16[40,512]{1,0:T(8,128)(2,1)S(1)}, bf16[40,512]{1,0:T(8,128)(2,1)S(1)}, u32[]{:S(2)}, u32[]{:S(2)}) collective-permute-start(bf16[40,512]{1,0:T(8,128)(2,1)S(1)} %get-tuple-element.37), channel_id=1, source_target_pairs={{0,6},{2,4},{4,2},{6,0},{8,14},{10,12},{12,10},{14,8},{1,7},{3,5},... | collective-permute-start | bytes 122888 | tf_op jit(solution)/shard_map/ppermute | solution.py:21
  30.8 1.7 %collective-permute-start.9 = (bf16[40,512]{1,0:T(8,128)(2,1)S(1)}, bf16[40,512]{1,0:T(8,128)(2,1)S(1)}, u32[]{:S(2)}, u32[]{:S(2)}) collective-permute-start(bf16[40,512]{1,0:T(8,128)(2,1)S(1)} %get-tuple-element.36), channel_id=1, source_target_pairs={{0,4},{2,6},{4,0},{6,2},{8,12},{10,14},{12,8},{14,10},{1,5},{3,7},... | collective-permute-start | bytes 122888 | tf_op jit(solution)/shard_map/ppermute | solution.py:21
  32.5 2.2 %shard_map.125 = bf16[128,2048]{1,0:T(8,128)(2,1)} custom-call(bf16[128,2048]{1,0:T(8,128)(2,1)S(1)} %bitcast.18, bf16[4,272,128]{2,1,0:T(8,128)(2,1)S(1)} %shard_map.124.held_ref, s32[1,128]{1,0:T(1,128)S(1)} %copy-done.8), custom_call_target="tpu_custom_call" | custom-call | tf_op jit(solution)/shard_map/pallas_call | solution.py:32
  34.9 3.3 %collective-permute-start.13 = (bf16[40,512]{1,0:T(8,128)(2,1)S(1)}, bf16[40,512]{1,0:T(8,128)(2,1)S(1)}, u32[]{:S(2)}, u32[]{:S(2)}) collective-permute-start(bf16[40,512]{1,0:T(8,128)(2,1)S(1)} %get-tuple-element.46), channel_id=1, source_target_pairs={{0,8},{4,12},{8,0},{12,4},{1,9},{5,13},{9,1},{13,5},{2,10},{6,14},... | collective-permute-start | bytes 122888 | tf_op jit(solution)/shard_map/ppermute | solution.py:21
  38.2 0.2 shard_map.126.share_ref
  38.5 0.9 %shard_map.128.refs_0_ = bf16[128,2048]{1,0:T(8,128)(2,1)} custom-call(bf16[2,128,40]{2,1,0:T(8,128)(2,1)S(1)} %shard_map.126.share_ref, bf16[40,512]{1,0:T(8,128)(2,1)S(1)} %get-tuple-element.47.rows_ref), custom_call_target="tpu_custom_call" | custom-call | flops 20971520 | bytes 585728 | tf_op jit(solution)/shard_map/pallas_call | solution.py:32
  39.4 0.8 %collective-permute-done.13.rows_ref = bf16[40,512]{1,0:T(8,128)(2,1)S(1)} collective-permute-done((bf16[40,512]{1,0:T(8,128)(2,1)S(1)}, bf16[40,512]{1,0:T(8,128)(2,1)S(1)}, u32[]{:S(2)}, u32[]{:S(2)}) %collective-permute-start.13) | collective-permute-done | bytes 40992 | tf_op jit(solution)/shard_map/ppermute | solution.py:21
  40.2 0.9 %shard_map.129 = bf16[128,2048]{1,0:T(8,128)(2,1)} custom-call(bf16[2,128,40]{2,1,0:T(8,128)(2,1)S(1)} %shard_map.126.share_ref, bf16[40,512]{1,0:T(8,128)(2,1)S(1)} %collective-permute-done.13.rows_ref, bf16[128,2048]{1,0:T(8,128)(2,1)} %shard_map.128.refs_0_), custom_call_target="tpu_custom_call", output_to_operand_aliasing={{}: (2, {})} | custom-call | flops 20971520 | bytes 1110016 | tf_op jit(solution)/shard_map/pallas_call | solution.py:32
  (33 shorter events, 0.5 us)
Async XLA Ops:
  0.6 0.7 %copy-start.6 = (s32[1,128,8]{1,2,0:T(8,128)S(1)}, s32[1,128,8]{1,2,0:T(8,128)}, u32[]{:S(2)}) copy-start(s32[1,128,8]{1,2,0:T(8,128)} %param.15) | copy-start | bytes 12292
  0.6 1.0 %copy-start.9 = (bf16[1,128,2048]{2,1,0:T(8,128)(2,1)S(1)}, bf16[1,128,2048]{2,1,0:T(8,128)(2,1)}, u32[]{:S(2)}) copy-start(bf16[1,128,2048]{2,1,0:T(8,128)(2,1)} %param.14) | copy-start | bytes 1572868
  1.8 4.3 %copy-start.4 = (bf16[1,128,128]{2,1,0:T(8,128)(2,1)S(1)}, bf16[1,128,128]{2,1,0:T(8,128)(2,1)}, u32[]{:S(2)}) copy-start(bf16[1,128,128]{2,1,0:T(8,128)(2,1)} %param.11) | copy-start | bytes 98308
  1.9 4.3 %copy-start.5 = (bf16[1,128,128]{2,1,0:T(8,128)(2,1)S(1)}, bf16[1,128,128]{2,1,0:T(8,128)(2,1)}, u32[]{:S(2)}) copy-start(bf16[1,128,128]{2,1,0:T(8,128)(2,1)} %param.12) | copy-start | bytes 98308
  1.9 4.3 %copy-start.8 = (s32[1,128]{1,0:T(1,128)S(1)}, s32[1,128]{1,0:T(1,128)}, u32[]{:S(2)}) copy-start(s32[1,128]{1,0:T(1,128)} %segment_ref.2) | copy-start | bytes 1540
  1.9 6.5 %collective-permute-start = (bf16[40,512]{1,0:T(8,128)(2,1)S(1)}, bf16[40,512]{1,0:T(8,128)(2,1)S(1)}, u32[]{:S(2)}, u32[]{:S(2)}) collective-permute-start(bf16[40,512]{1,0:T(8,128)(2,1)S(1)} %shard_map.116.after_ref), channel_id=1, source_target_pairs={{0,8},{4,12},{8,0},{12,4},{1,9},{5,13},{9,1},{13,5},{2,10},{6,14},... | collective-permute-start | bytes 122888 | tf_op jit(solution)/shard_map/ppermute | solution.py:21
  6.3 9.3 %copy-start = (bf16[1,1024,768]{2,1,0:T(8,128)(2,1)S(1)}, bf16[1,1024,768]{2,1,0:T(8,128)(2,1)}, u32[]{:S(2)}) copy-start(bf16[1,1024,768]{2,1,0:T(8,128)(2,1)} %param.17) | copy-start | bytes 4718596
  6.3 9.3 %copy-start.1 = (bf16[1,1024,768]{2,1,0:T(8,128)(2,1)S(1)}, bf16[1,1024,768]{2,1,0:T(8,128)(2,1)}, u32[]{:S(2)}) copy-start(bf16[1,1024,768]{2,1,0:T(8,128)(2,1)} %param.18) | copy-start | bytes 4718596
  8.4 6.1 %collective-permute-start.3 = (bf16[40,512]{1,0:T(8,128)(2,1)S(1)}, bf16[40,512]{1,0:T(8,128)(2,1)S(1)}, u32[]{:S(2)}, u32[]{:S(2)}) collective-permute-start(bf16[40,512]{1,0:T(8,128)(2,1)S(1)} %get-tuple-element.27), channel_id=1, source_target_pairs={{0,6},{2,4},{4,2},{6,0},{8,14},{10,12},{12,10},{14,8},{1,7},{3,5},... | collective-permute-start | bytes 122888 | tf_op jit(solution)/shard_map/ppermute | solution.py:21
  10.9 4.0 %collective-permute-start.2 = (bf16[40,512]{1,0:T(8,128)(2,1)S(1)}, bf16[40,512]{1,0:T(8,128)(2,1)S(1)}, u32[]{:S(2)}, u32[]{:S(2)}) collective-permute-start(bf16[40,512]{1,0:T(8,128)(2,1)S(1)} %get-tuple-element.27), channel_id=1, source_target_pairs={{0,4},{2,6},{4,0},{6,2},{8,12},{10,14},{12,8},{14,10},{1,5},{3,7},... | collective-permute-start | bytes 122888 | tf_op jit(solution)/shard_map/ppermute | solution.py:21
  11.7 4.0 %collective-permute-start.1 = (bf16[40,512]{1,0:T(8,128)(2,1)S(1)}, bf16[40,512]{1,0:T(8,128)(2,1)S(1)}, u32[]{:S(2)}, u32[]{:S(2)}) collective-permute-start(bf16[40,512]{1,0:T(8,128)(2,1)S(1)} %get-tuple-element.26.refs_0_), channel_id=1, source_target_pairs={{0,2},{2,0},{4,6},{6,4},{8,10},{10,8},{12,14},{14,12},{1,3},{3,1},... | collective-permute-start | bytes 122888 | tf_op jit(solution)/shard_map/ppermute | solution.py:21
  12.0 8.2 %collective-permute-start.11 = (bf16[1,272,128]{2,1,0:T(8,128)(2,1)S(1)}, bf16[1,272,128]{2,1,0:T(8,128)(2,1)S(1)}, u32[]{:S(2)}, u32[]{:S(2)}) collective-permute-start(bf16[1,272,128]{2,1,0:T(8,128)(2,1)S(1)} %shard_map.117.held_ref), channel_id=1, source_target_pairs={{0,8},{4,12},{8,0},{12,4},{1,9},{5,13},{9,1},{13,5},{2,10},{6,14},... | collective-permute-start | bytes 208904 | tf_op jit(solution)/shard_map/ppermute | solution.py:21
  16.3 1.3 %collective-permute-start.4 = (bf16[40,768]{1,0:T(8,128)(2,1)S(1)}, bf16[40,768]{1,0:T(8,128)(2,1)S(1)}, u32[]{:S(2)}, u32[]{:S(2)}) collective-permute-start(bf16[40,768]{1,0:T(8,128)(2,1)S(1)} %get-tuple-element.29), channel_id=1, source_target_pairs={{0,1},{1,0},{2,3},{3,2},{4,5},{5,4},{6,7},{7,6},{8,9},{9,8},{10,11... | collective-permute-start | bytes 184328 | tf_op jit(solution)/shard_map/ppermute | solution.py:21
  16.4 1.4 %collective-permute-start.5 = (bf16[40,768]{1,0:T(8,128)(2,1)S(1)}, bf16[40,768]{1,0:T(8,128)(2,1)S(1)}, u32[]{:S(2)}, u32[]{:S(2)}) collective-permute-start(bf16[40,768]{1,0:T(8,128)(2,1)S(1)} %get-tuple-element.31), channel_id=1, source_target_pairs={{0,1},{1,0},{2,3},{3,2},{4,5},{5,4},{6,7},{7,6},{8,9},{9,8},{10,11... | collective-permute-start | bytes 184328 | tf_op jit(solution)/shard_map/ppermute | solution.py:21
  17.8 10.7 %copy-start.2 = (bf16[1,768,1024]{2,1,0:T(8,128)(2,1)S(1)}, bf16[1,768,1024]{2,1,0:T(8,128)(2,1)}, u32[]{:S(2)}) copy-start(bf16[1,768,1024]{2,1,0:T(8,128)(2,1)} %param.19) | copy-start | bytes 4718596
  17.9 9.3 %collective-permute-start.6 = (bf16[40,1536]{1,0:T(8,128)(2,1)S(1)}, bf16[40,1536]{1,0:T(8,128)(2,1)S(1)}, u32[]{:S(2)}, u32[]{:S(2)}) collective-permute-start(bf16[40,1536]{1,0:T(8,128)(2,1)S(1)} %get-tuple-element.33.after_ref), channel_id=1, source_target_pairs={{0,8},{4,12},{8,0},{12,4},{1,9},{5,13},{9,1},{13,5},{2,10},{6,14},... | collective-permute-start | bytes 368648 | tf_op jit(solution)/shard_map/ppermute | solution.py:21
  20.2 12.3 %copy-start.3 = (bf16[1,128,2048]{2,1,0:T(8,128)(2,1)S(1)}, bf16[1,128,2048]{2,1,0:T(8,128)(2,1)}, u32[]{:S(2)}) copy-start(bf16[1,128,2048]{2,1,0:T(8,128)(2,1)} %param.10) | copy-start | bytes 1572868
  20.3 12.2 %collective-permute-start.12 = (bf16[2,272,128]{2,1,0:T(8,128)(2,1)S(1)}, bf16[2,272,128]{2,1,0:T(8,128)(2,1)S(1)}, u32[]{:S(2)}, u32[]{:S(2)}) collective-permute-start(bf16[2,272,128]{2,1,0:T(8,128)(2,1)S(1)} %shard_map.123.held_ref), channel_id=1, source_target_pairs={{0,4},{4,0},{8,12},{12,8},{1,5},{5,1},{9,13},{13,9},{2,6},{6,2},{1... | collective-permute-start | bytes 417800 | tf_op jit(solution)/shard_map/ppermute | solution.py:21
  27.2 1.3 %collective-permute-start.7 = (bf16[40,768]{1,0:T(8,128)(2,1)S(1)}, bf16[40,768]{1,0:T(8,128)(2,1)S(1)}, u32[]{:S(2)}, u32[]{:S(2)}) collective-permute-start(bf16[40,768]{1,0:T(8,128)(2,1)S(1)} %shard_map.121.hidden_ref), channel_id=1, source_target_pairs={{0,1},{1,0},{2,3},{3,2},{4,5},{5,4},{6,7},{7,6},{8,9},{9,8},{10,11... | collective-permute-start | bytes 184328 | tf_op jit(solution)/shard_map/ppermute | solution.py:21
  28.5 9.7 %copy-start.7 = (f32[1,128,8]{1,2,0:T(8,128)S(1)}, f32[1,128,8]{1,2,0:T(8,128)}, u32[]{:S(2)}) copy-start(f32[1,128,8]{1,2,0:T(8,128)} %param.16) | copy-start | bytes 12292
  28.9 5.8 %collective-permute-start.8 = (bf16[40,512]{1,0:T(8,128)(2,1)S(1)}, bf16[40,512]{1,0:T(8,128)(2,1)S(1)}, u32[]{:S(2)}, u32[]{:S(2)}) collective-permute-start(bf16[40,512]{1,0:T(8,128)(2,1)S(1)} %get-tuple-element.35), channel_id=1, source_target_pairs={{0,2},{2,0},{4,6},{6,4},{8,10},{10,8},{12,14},{14,12},{1,3},{3,1},... | collective-permute-start | bytes 122888 | tf_op jit(solution)/shard_map/ppermute | solution.py:21
  29.4 5.3 %collective-permute-start.10 = (bf16[40,512]{1,0:T(8,128)(2,1)S(1)}, bf16[40,512]{1,0:T(8,128)(2,1)S(1)}, u32[]{:S(2)}, u32[]{:S(2)}) collective-permute-start(bf16[40,512]{1,0:T(8,128)(2,1)S(1)} %get-tuple-element.37), channel_id=1, source_target_pairs={{0,6},{2,4},{4,2},{6,0},{8,14},{10,12},{12,10},{14,8},{1,7},{3,5},... | collective-permute-start | bytes 122888 | tf_op jit(solution)/shard_map/ppermute | solution.py:21
  30.8 4.1 %collective-permute-start.9 = (bf16[40,512]{1,0:T(8,128)(2,1)S(1)}, bf16[40,512]{1,0:T(8,128)(2,1)S(1)}, u32[]{:S(2)}, u32[]{:S(2)}) collective-permute-start(bf16[40,512]{1,0:T(8,128)(2,1)S(1)} %get-tuple-element.36), channel_id=1, source_target_pairs={{0,4},{2,6},{4,0},{6,2},{8,12},{10,14},{12,8},{14,10},{1,5},{3,7},... | collective-permute-start | bytes 122888 | tf_op jit(solution)/shard_map/ppermute | solution.py:21
  34.9 5.3 %collective-permute-start.13 = (bf16[40,512]{1,0:T(8,128)(2,1)S(1)}, bf16[40,512]{1,0:T(8,128)(2,1)S(1)}, u32[]{:S(2)}, u32[]{:S(2)}) collective-permute-start(bf16[40,512]{1,0:T(8,128)(2,1)S(1)} %get-tuple-element.46), channel_id=1, source_target_pairs={{0,8},{4,12},{8,0},{12,4},{1,9},{5,13},{9,1},{13,5},{2,10},{6,14},... | collective-permute-start | bytes 122888 | tf_op jit(solution)/shard_map/ppermute | solution.py:21
